TPU v7x, 32 devices: a whole 2x2x4 slice. The times are simulated.
32 devices in a mesh: dp: 8 (over z, y), ctx: 4 (over x, core).
Axes of the slice: x: 2, y: 2, z: 4, core: 2. Of those that a mesh axis runs over, the one named last changes fastest.
Arguments:
- tokens: bfloat16 [8, 2048, 768], P('dp', 'ctx'), may hold values from -6 to 6
- attn_gain: bfloat16 [768], P('dp'), may hold values from 0.5 to 1.5
- attn_shift: bfloat16 [768], P('dp'), may hold values from -2 to 2
- w_qkv: bfloat16 [768, 2304], P('dp'), may hold values from -0.21875 to 0.21875
- w_out: bfloat16 [768, 768], P('dp'), may hold values from -6 to 6
- ffn_gain: bfloat16 [768], P('dp'), may hold values from 0.5 to 1.5
- ffn_shift: bfloat16 [768], P('dp'), may hold values from -2 to 2
- w_in: bfloat16 [768, 3072], P('dp'), may hold values from -0.21875 to 0.21875
- b_in: bfloat16 [3072], P('dp'), may hold values from -2 to 2
- w_down: bfloat16 [3072, 768], P('dp'), may hold values from -0.109375 to 0.109375
- b_down: bfloat16 [768], P('dp'), may hold values from -2 to 2
- cotangent: bfloat16 [8, 2048, 768], P('dp', 'ctx'), may hold values from -6 to 6
- lengths: int32 [8], P('dp'), may hold values from 512 to 2048, as said below
- block_order: int32 [8, 4], P('dp'), may hold values from 0 to 3, each once within a row
Outputs:
- layer_out: bfloat16 [8, 2048, 768], P('dp', 'ctx')
- input_grad: bfloat16 [8, 2048, 768], P('dp', 'ctx')
- grad_attn_gain: float32 [768], P('dp')
- grad_attn_shift: float32 [768], P('dp')
- grad_w_qkv: float32 [768, 2304], P('dp')
- grad_w_out: float32 [768, 768], P('dp')
- grad_ffn_gain: float32 [768], P('dp')
- grad_ffn_shift: float32 [768], P('dp')
- grad_w_in: float32 [768, 3072], P('dp')
- grad_b_in: float32 [3072], P('dp')
- grad_w_down: float32 [3072, 768], P('dp')
- grad_b_down: float32 [768], P('dp')
Inputs may be any that keep to these rules, and one draw needn't show every extreme that they name: `lengths`: valid positions form the head of each sequence; one sequence has 2048 of them and one has 512. Each row is a permutation; index c of ctx holds positions block_order[s, c] * 512 to block_order[s, c] * 512 + 511 of sequence s.
All inputs are finite; a program needn't handle non-finite values.
Results may differ from a plain program's by a relative error of at most 0.013.
Values may be sent and summed in bfloat16 or wider, within the bound.
No kernel may reach another device: no remote copies, remote signals or barrier semaphores. Data moves between devices by JAX's collectives and lax.ppermute only.
A program may use at most 128 MiB of HBM per device.

v0:
```python
import jax
import jax.numpy as jnp
from jax import lax
from jax.sharding import PartitionSpec as P

H = 12


epsilon = 1e-05
masked_score = -1000000000.0
highest = lax.Precision.HIGHEST
gelu_coeff = 0.7978845608
cubic_term = 0.044715


def shifted(value, axis, by):
    peers = lax.axis_size(axis)
    return lax.ppermute(value, axis, [(i, (i + by) % peers) for i in range(peers)])


def gate_parts(values):
    bent = jnp.tanh(gelu_coeff * (values + cubic_term * values * values * values))
    result = 0.5 * values * (1.0 + bent)
    slope = 0.5 * (1.0 + bent) + 0.5 * values * (1.0 - bent * bent) * gelu_coeff * (
        1.0 + 3.0 * cubic_term * values * values
    )
    return (result, slope)


def norm_parts(values):
    center = values - jnp.mean(values, axis=-1, keepdims=True)
    spread = jnp.mean(center * center, axis=-1, keepdims=True)
    inverse = lax.rsqrt(spread + epsilon)
    return (center * inverse, inverse)


def norm_back(grad, unit_part, inverse, gain):
    gain_grad = jnp.sum(grad * unit_part, axis=0)
    shift_grad = jnp.sum(grad, axis=0)
    scaled = grad * gain
    value_grad = inverse * (
        scaled
        - jnp.mean(scaled, axis=-1, keepdims=True)
        - unit_part * jnp.mean(scaled * unit_part, axis=-1, keepdims=True)
    )
    return (gain_grad, shift_grad, value_grad)


def on_device(
    tokens,
    attn_gain,
    attn_shift,
    w_qkv,
    w_out,
    ffn_gain,
    ffn_shift,
    w_in,
    b_in,
    w_down,
    b_down,
    cotangent,
    lengths,
    block_order,
):
    inputs = tokens[0].astype(jnp.float32)
    row_count, width = inputs.shape
    head_count = H
    head_size = width // head_count
    scale = head_size ** (-0.5)
    ctx_size = lax.axis_size("ctx")
    my_index = lax.axis_index("ctx")
    seq_length = lengths[0]
    order_row = block_order[0]
    places = jnp.arange(ctx_size, dtype=jnp.int32)

    def key_valid_rows(start_row, piece_len):
        stored = start_row + jnp.arange(piece_len, dtype=jnp.int32)
        owner = stored // row_count
        block_id = jnp.sum(
            jnp.where(owner[:, None] == places[None, :], order_row[None, :], 0), axis=1
        )
        return block_id * row_count + stored % row_count < seq_length

    local_valid = key_valid_rows(my_index * row_count, row_count).astype(jnp.float32)
    gain_one, shift_one, qkv_weight, out_weight = (
        lax.all_gather(attn_gain, "dp", axis=0, tiled=True),
        lax.all_gather(attn_shift, "dp", axis=0, tiled=True),
        lax.all_gather(w_qkv, "dp", axis=0, tiled=True),
        lax.all_gather(w_out, "dp", axis=0, tiled=True),
    )
    unit_one, inverse_one = norm_parts(inputs)
    first = (unit_one * gain_one.astype(jnp.float32) + shift_one.astype(jnp.float32)).astype(
        jnp.bfloat16
    )
    qkv = jnp.dot(first, qkv_weight, preferred_element_type=jnp.float32).astype(jnp.bfloat16)
    query = qkv[:, :width].reshape(row_count, head_count, head_size)
    key_value = qkv[:, width:]

    def attend(carry, piece_rows, start_row):
        top_score, denom_sum, weighted = carry
        piece_len = piece_rows.shape[0]
        key_heads = piece_rows[:, :width].reshape(piece_len, head_count, head_size)
        value_heads = (
            piece_rows[:, width:].reshape(piece_len, head_count, head_size).astype(jnp.float32)
        )
        key_valid = key_valid_rows(start_row, piece_len)[None, None, :]
        scores = (
            jnp.einsum("qhd,khd->hqk", query, key_heads, preferred_element_type=jnp.float32) * scale
        )
        scores = jnp.where(key_valid, scores, masked_score)
        new_top = jnp.maximum(top_score, jnp.max(scores, axis=-1))
        weights = jnp.where(key_valid, jnp.exp(scores - new_top[..., None]), 0.0)
        factor = jnp.exp(top_score - new_top)
        denom_sum = denom_sum * factor + jnp.sum(weights, axis=-1)
        weighted = weighted * factor[..., None] + jnp.einsum(
            "hqk,khd->hqd", weights, value_heads, precision=highest
        )
        return (new_top, denom_sum, weighted)

    initial = (
        jnp.full((head_count, row_count), masked_score, jnp.float32),
        jnp.zeros((head_count, row_count), jnp.float32),
        jnp.zeros((head_count, row_count, head_size), jnp.float32),
    )
    carry = initial
    piece_rows = lax.all_gather(key_value, "ctx", axis=0, tiled=True)
    piece_len = piece_rows.shape[0]
    span = row_count * max(1, 512 // row_count)

    def visit_span(state, offset):
        part_rows = lax.dynamic_slice_in_dim(piece_rows, offset, span, 0)
        return (attend(state, part_rows, offset), None)

    carry, _ = lax.scan(visit_span, carry, jnp.arange(0, piece_len, span, dtype=jnp.int32))
    top_score, denom_sum, weighted = carry
    attended = weighted / denom_sum[..., None]
    log_total = top_score + jnp.log(denom_sum)
    attn_low = attended.transpose(1, 0, 2).reshape(row_count, width).astype(jnp.bfloat16)
    mixed = inputs + jnp.dot(attn_low, out_weight, preferred_element_type=jnp.float32)
    gain_two, shift_two, in_weight, in_bias, down_weight, down_bias = (
        lax.all_gather(ffn_gain, "dp", axis=0, tiled=True),
        lax.all_gather(ffn_shift, "dp", axis=0, tiled=True),
        lax.all_gather(w_in, "dp", axis=0, tiled=True),
        lax.all_gather(b_in, "dp", axis=0, tiled=True),
        lax.all_gather(w_down, "dp", axis=0, tiled=True),
        lax.all_gather(b_down, "dp", axis=0, tiled=True),
    )
    unit_two, inverse_two = norm_parts(mixed)
    second = (unit_two * gain_two.astype(jnp.float32) + shift_two.astype(jnp.float32)).astype(
        jnp.bfloat16
    )
    hidden = jnp.dot(second, in_weight, preferred_element_type=jnp.float32) + in_bias.astype(
        jnp.float32
    )
    gated, gate_slope = gate_parts(hidden)
    active = gated.astype(jnp.bfloat16)
    output = (
        mixed
        + jnp.dot(active, down_weight, preferred_element_type=jnp.float32)
        + down_bias.astype(jnp.float32)
    ) * local_valid[:, None]
    gain_two, shift_two, in_weight, in_bias, down_weight, down_bias = (
        lax.all_gather(ffn_gain, "dp", axis=0, tiled=True),
        lax.all_gather(ffn_shift, "dp", axis=0, tiled=True),
        lax.all_gather(w_in, "dp", axis=0, tiled=True),
        lax.all_gather(b_in, "dp", axis=0, tiled=True),
        lax.all_gather(w_down, "dp", axis=0, tiled=True),
        lax.all_gather(b_down, "dp", axis=0, tiled=True),
    )
    grad_out = cotangent[0].astype(jnp.float32) * local_valid[:, None]
    grad_low = grad_out.astype(jnp.bfloat16)
    grad_down_w = jnp.einsum("ti,tj->ij", active, grad_low, preferred_element_type=jnp.float32)
    grad_down_b = jnp.sum(grad_low.astype(jnp.float32), axis=0)
    grad_active = jnp.einsum("tj,ij->ti", grad_low, down_weight, preferred_element_type=jnp.float32)
    grad_hidden = (grad_active * gate_slope).astype(jnp.bfloat16)
    grad_in_w = jnp.einsum("ti,tj->ij", second, grad_hidden, preferred_element_type=jnp.float32)
    grad_in_b = jnp.sum(grad_hidden.astype(jnp.float32), axis=0)
    grad_second = jnp.einsum(
        "tj,ij->ti", grad_hidden, in_weight, preferred_element_type=jnp.float32
    )
    grad_gain_two, grad_shift_two, grad_norm_two = norm_back(
        grad_second, unit_two, inverse_two, gain_two.astype(jnp.float32)
    )
    grad_mixed = grad_out + grad_norm_two
    ffn_shares = (
        lax.psum_scatter(
            grad_gain_two.astype(jnp.bfloat16), "dp", scatter_dimension=0, tiled=True
        ).astype(jnp.float32),
        lax.psum_scatter(
            grad_shift_two.astype(jnp.bfloat16), "dp", scatter_dimension=0, tiled=True
        ).astype(jnp.float32),
        lax.psum_scatter(
            grad_in_w.astype(jnp.bfloat16), "dp", scatter_dimension=0, tiled=True
        ).astype(jnp.float32),
        lax.psum_scatter(
            grad_in_b.astype(jnp.bfloat16), "dp", scatter_dimension=0, tiled=True
        ).astype(jnp.float32),
        lax.psum_scatter(
            grad_down_w.astype(jnp.bfloat16), "dp", scatter_dimension=0, tiled=True
        ).astype(jnp.float32),
        lax.psum_scatter(
            grad_down_b.astype(jnp.bfloat16), "dp", scatter_dimension=0, tiled=True
        ).astype(jnp.float32),
    )
    gain_one, shift_one, qkv_weight, out_weight = (
        lax.all_gather(attn_gain, "dp", axis=0, tiled=True),
        lax.all_gather(attn_shift, "dp", axis=0, tiled=True),
        lax.all_gather(w_qkv, "dp", axis=0, tiled=True),
        lax.all_gather(w_out, "dp", axis=0, tiled=True),
    )
    grad_branch = grad_mixed.astype(jnp.bfloat16)
    grad_out_w = jnp.einsum("ti,tj->ij", attn_low, grad_branch, preferred_element_type=jnp.float32)
    grad_attn = jnp.einsum(
        "tj,ij->ti", grad_branch, out_weight, preferred_element_type=jnp.float32
    ).astype(jnp.bfloat16)
    grad_heads = grad_attn.reshape(row_count, head_count, head_size)
    delta_sum = jnp.sum(grad_heads.astype(jnp.float32).transpose(1, 0, 2) * attended, axis=-1)

    def pair_grads(query_in, grad_in, lse_in, delta_in, piece_rows, anchor):
        key_heads = piece_rows[:, :width].reshape(row_count, head_count, head_size)
        value_heads = piece_rows[:, width:].reshape(row_count, head_count, head_size)
        key_valid = key_valid_rows(anchor * row_count, row_count)[None, None, :]
        scores = (
            jnp.einsum("qhd,khd->hqk", query_in, key_heads, preferred_element_type=jnp.float32)
            * scale
        )
        scores = jnp.where(key_valid, scores, masked_score)
        probs = jnp.where(key_valid, jnp.exp(scores - lse_in[..., None]), 0.0)
        grad_probs = jnp.einsum(
            "qhd,khd->hqk", grad_in, value_heads, preferred_element_type=jnp.float32
        )
        grad_scores = (probs * (grad_probs - delta_in[..., None])).astype(jnp.bfloat16)
        query_add = jnp.einsum(
            "hqk,khd->qhd", grad_scores, key_heads, preferred_element_type=jnp.float32
        )
        grad_keys = (
            jnp.einsum("hqk,qhd->khd", grad_scores, query_in, preferred_element_type=jnp.float32)
            * scale
        )
        grad_values = jnp.einsum(
            "hqk,qhd->khd", probs, grad_in.astype(jnp.float32), precision=highest
        )
        return (
            query_add,
            jnp.concatenate(
                [grad_keys.reshape(row_count, width), grad_values.reshape(row_count, width)], axis=1
            ),
        )

    def visit_block(position, state):
        piece_rows, piece_grad, grad_query = state
        anchor = (my_index - position) % ctx_size
        query_add, kv_add = pair_grads(query, grad_heads, log_total, delta_sum, piece_rows, anchor)
        piece_grad = piece_grad + kv_add
        grad_query = grad_query + query_add
        piece_rows = shifted(piece_rows, "ctx", 1)
        piece_grad = shifted(piece_grad, "ctx", 1)
        return (piece_rows, piece_grad, grad_query)

    start_state = (
        key_value,
        jnp.zeros((row_count, 2 * width), jnp.float32),
        jnp.zeros((row_count, head_count, head_size), jnp.float32),
    )
    piece_rows, piece_grad, grad_query = lax.fori_loop(0, ctx_size - 1, visit_block, start_state)
    last_anchor = (my_index - (ctx_size - 1)) % ctx_size
    query_add, kv_add = pair_grads(query, grad_heads, log_total, delta_sum, piece_rows, last_anchor)
    grad_query = grad_query + query_add
    own_grad = shifted((piece_grad + kv_add).astype(jnp.bfloat16), "ctx", 1).astype(jnp.float32)
    grad_qkv = jnp.concatenate(
        [(grad_query * scale).reshape(row_count, width), own_grad], axis=1
    ).astype(jnp.bfloat16)
    grad_qkv_w = jnp.einsum("ti,tj->ij", first, grad_qkv, preferred_element_type=jnp.float32)
    grad_first = jnp.einsum("tj,ij->ti", grad_qkv, qkv_weight, preferred_element_type=jnp.float32)
    grad_gain_one, grad_shift_one, grad_norm_one = norm_back(
        grad_first, unit_one, inverse_one, gain_one.astype(jnp.float32)
    )
    grad_inputs = grad_mixed + grad_norm_one
    attn_shares = (
        lax.psum_scatter(
            grad_gain_one.astype(jnp.bfloat16), "dp", scatter_dimension=0, tiled=True
        ).astype(jnp.float32),
        lax.psum_scatter(
            grad_shift_one.astype(jnp.bfloat16), "dp", scatter_dimension=0, tiled=True
        ).astype(jnp.float32),
        lax.psum_scatter(
            grad_qkv_w.astype(jnp.bfloat16), "dp", scatter_dimension=0, tiled=True
        ).astype(jnp.float32),
        lax.psum_scatter(
            grad_out_w.astype(jnp.bfloat16), "dp", scatter_dimension=0, tiled=True
        ).astype(jnp.float32),
    )
    summed = lax.psum(
        (
            attn_shares[0],
            attn_shares[1],
            attn_shares[2],
            attn_shares[3],
            ffn_shares[0],
            ffn_shares[1],
            ffn_shares[2],
            ffn_shares[3],
            ffn_shares[4],
            ffn_shares[5],
        ),
        "ctx",
    )
    return (
        output.astype(jnp.bfloat16)[None],
        grad_inputs.astype(jnp.bfloat16)[None],
        summed[0],
        summed[1],
        summed[2],
        summed[3],
        summed[4],
        summed[5],
        summed[6],
        summed[7],
        summed[8],
        summed[9],
    )


def solution(mesh):
    placed = (
        P("dp", "ctx", None),
        P("dp"),
        P("dp"),
        P("dp", None),
        P("dp", None),
        P("dp"),
        P("dp"),
        P("dp", None),
        P("dp"),
        P("dp", None),
        P("dp"),
        P("dp", "ctx", None),
        P("dp"),
        P("dp", None),
    )
    return jax.shard_map(
        on_device,
        mesh=mesh,
        in_specs=placed,
        out_specs=(
            P("dp", "ctx", None),
            P("dp", "ctx", None),
            P("dp"),
            P("dp"),
            P("dp", None),
            P("dp", None),
            P("dp"),
            P("dp"),
            P("dp", None),
            P("dp"),
            P("dp", None),
            P("dp"),
        ),
        check_vma=False,
    )
```

profile of v0, /device:TPU:0, one launch (start us, length us, event | category | flops | bytes accessed | tf_op | source)
XLA Modules:
  0.0 992.9 jit_solution(11425371288573215815)
XLA Ops:
  13.3 23.8 %all-reduce.13 = (bf16[768]{0:T(1024)(128)(2,1)S(1)}, bf16[768]{0:T(1024)(128)(2,1)S(1)}, bf16[768]{0:T(1024)(128)(2,1)S(1)}, bf16[768]{0:T(1024)(128)(2,1)S(1)}) all-reduce(bf16[768]{0:T(1024)(128)(2,1)S(1)} %dynamic-update-slice.1, bf16[768]{0:T(1024)(128)(2,1)S(1)} %dynamic-update-slice, ...), channel_id=1, replica_groups=mesh['dp'=8,'ctx'=4] {'dp'}, use_global_device_ids=true, to_apply=%add.1 | all-reduce | flops 3072 | bytes 12288
  40.0 38.6 %all-gather.7.cloned.1.call-done = bf16[768,2304]{1,0:T(8,128)(2,1)} async-done(((bf16[96,2304]{1,0:T(8,128)(2,1)}), bf16[768,2304]{1,0:T(8,128)(2,1)}) %all-gather.7.cloned.1.call-update) | async-done | bytes 3538960 | tf_op jit(solution)/shard_map/all_gather | solution.py:88
  88.5 25.9 %all-gather = bf16[8,1,384]{2,1,0:T(2,128)(2,1)S(1)} all-gather(bf16[1,1,384]{2,1,0:T(2,128)(2,1)S(1)} %reshape.334), channel_id=1, replica_groups=mesh['dp'=8,'ctx'=4] {'dp'}, dimensions={0}, use_global_device_ids=true | all-gather | bytes 6912 | tf_op jit(solution)/shard_map/all_gather | solution.py:144
  117.0 13.7 %all-gather.9.cloned.1.call-done = bf16[2048,1536]{1,0:T(8,128)(2,1)} async-done(((bf16[512,1536]{1,0:T(8,128)(2,1)}), bf16[2048,1536]{1,0:T(8,128)(2,1)}) %all-gather.9.cloned.1.call-update) | async-done | bytes 6291472 | tf_op jit(solution)/shard_map/all_gather | solution.py:126
  130.8 92.6 %while.38 = (s32[]{:T(128)}, f32[12,512]{1,0:T(8,128)S(1)}, f32[12,512]{1,0:T(8,128)S(1)}, f32[12,512,64]{1,2,0:T(8,128)}, s32[4]{0:T(128)S(1)}, /*index=5*/s32[...) while((s32[]{:T(128)}, f32[12,512]{1,0:T(8,128)S(1)}, ...), condition=%wide.region_6.7_spmd.clone, body=%wide.region_2.6_spmd.clone.sunk | while | flops 2857552896 | bytes 62531876 | solution.py:134
  144.8 7.9 fusion.176
  167.8 7.9 fusion.176
  190.9 7.9 fusion.176
  213.8 7.9 fusion.176
  227.7 27.1 %all-gather.13.cloned.1.call-done = bf16[768,3072]{1,0:T(8,128)(2,1)} async-done(((bf16[96,3072]{1,0:T(8,128)(2,1)}), bf16[768,3072]{1,0:T(8,128)(2,1)}) %all-gather.13.cloned.1.call-update) | async-done | bytes 4718608 | tf_op jit(solution)/shard_map/all_gather | solution.py:143
  254.8 7.1 fusion.104
  261.8 73.0 %all-gather.15.cloned.1.call-done = bf16[3072,768]{1,0:T(8,128)(2,1)} async-done(((bf16[384,768]{1,0:T(8,128)(2,1)}), bf16[3072,768]{1,0:T(8,128)(2,1)}) %all-gather.15.cloned.1.call-update) | async-done | bytes 4718608 | tf_op jit(solution)/shard_map/all_gather | solution.py:145
  334.9 9.5 fusion.110
  359.2 237.7 %while.39 = (s32[]{:T(128)}, bf16[512,1536]{0,1:T(8,128)(2,1)}, f32[512,1536]{0,1:T(8,128)}, f32[512,12,64]{0,2,1:T(8,128)}, s32[]{:T(128)}, /*index=5*/s32[1,4]...) while((s32[]{:T(128)}, bf16[512,1536]{0,1:T(8,128)(2,1)}, ...), condition=%wide.region_15.16_spmd.clone, body=%wide.region_13.15_spmd.clone.sunk | while | flops 4063908864 | bytes 128272296 | solution.py:265
  363.5 8.7 fusion.189
  392.1 46.4 %collective-permute-done = bf16[512,1536]{0,1:T(8,128)(2,1)} collective-permute-done((bf16[512,1536]{0,1:T(8,128)(2,1)S(1)}, bf16[512,1536]{0,1:T(8,128)(2,1)}, u32[]{:S(2)}, u32[]{:S(2)}) %collective-permute-start) | collective-permute-done | bytes 1572896 | tf_op jit(solution)/shard_map/while/body/eval_jaxpr/ppermute | solution.py:18
  442.6 8.7 fusion.189
  465.4 6.4 bitcast_add_fusion.3
  471.7 45.9 %collective-permute-done = bf16[512,1536]{0,1:T(8,128)(2,1)} collective-permute-done((bf16[512,1536]{0,1:T(8,128)(2,1)S(1)}, bf16[512,1536]{0,1:T(8,128)(2,1)}, u32[]{:S(2)}, u32[]{:S(2)}) %collective-permute-start) | collective-permute-done | bytes 1572896 | tf_op jit(solution)/shard_map/while/body/eval_jaxpr/ppermute | solution.py:18
  521.8 8.7 fusion.189
  544.5 6.4 bitcast_add_fusion.3
  550.9 45.9 %collective-permute-done = bf16[512,1536]{0,1:T(8,128)(2,1)} collective-permute-done((bf16[512,1536]{0,1:T(8,128)(2,1)S(1)}, bf16[512,1536]{0,1:T(8,128)(2,1)}, u32[]{:S(2)}, u32[]{:S(2)}) %collective-permute-start) | collective-permute-done | bytes 1572896 | tf_op jit(solution)/shard_map/while/body/eval_jaxpr/ppermute | solution.py:18
  600.2 8.7 fusion.41
  620.5 17.8 %collective-permute-done.2 = bf16[512,1536]{0,1:T(8,128)(2,1)S(1)} collective-permute-done((bf16[512,1536]{0,1:T(8,128)(2,1)S(1)}, bf16[512,1536]{0,1:T(8,128)(2,1)S(1)}, u32[]{:S(2)}, u32[]{:S(2)}) %collective-permute-start.2) | collective-permute-done | bytes 1572896 | tf_op jit(solution)/shard_map/ppermute | solution.py:18
  644.9 6.5 convolution_convert_fusion.1
  652.6 8.6 convolution_convert_fusion
  663.3 6.4 fusion.70
  669.7 35.1 %all-reduce.12 = (bf16[768]{0:T(1024)(128)(2,1)S(1)}, bf16[768]{0:T(1024)(128)(2,1)S(1)}, bf16[768]{0:T(1024)(128)(2,1)S(1)}, bf16[768]{0:T(1024)(128)(2,1)S(1)}...) all-reduce(bf16[768]{0:T(1024)(128)(2,1)S(1)} %dynamic-update-slice, ...), channel_id=1, replica_groups=mesh['dp'=8,'ctx'=4] {'dp'}, use_global_device_ids=true, to_apply=%add.4 | all-reduce | flops 7680 | bytes 30720
  708.1 9.1 fusion.78
  721.6 98.5 %reduce-scatter.9.cloned.1.call-done = bf16[96,3072]{1,0:T(8,128)(2,1)} async-done(((bf16[768,3072]{1,0:T(8,128)(2,1)}), bf16[96,3072]{1,0:T(8,128)(2,1)}) %reduce-scatter.9.cloned.1.call-update) | async-done | bytes 589840 | tf_op jit(solution)/shard_map/reduce_scatter | solution.py:192
  820.1 98.7 %reduce-scatter.11.cloned.1.call-done = bf16[384,768]{1,0:T(8,128)(2,1)} async-done(((bf16[3072,768]{1,0:T(8,128)(2,1)}), bf16[384,768]{1,0:T(8,128)(2,1)}) %reduce-scatter.11.cloned.1.call-update) | async-done | bytes 589840 | tf_op jit(solution)/shard_map/reduce_scatter | solution.py:198
  918.8 67.1 %all-reduce.15 = (f32[96]{0:T(128)}, f32[96]{0:T(128)}, f32[96,2304]{1,0:T(8,128)}, f32[96,768]{1,0:T(8,128)}, f32[96]{0:T(128)}, /*index=5*/f32[96]{0:T(128)}, ...) all-reduce(f32[96]{0:T(128)S(1)} %dynamic-slice_convert_fusion.5, ...), channel_id=1, replica_groups=mesh['dp'=8,'ctx'=4] {'ctx'}, use_global_device_ids=true, to_apply=%region_21.22 | all-reduce | flops 885600 | bytes 5315328 | tf_op jit(solution)/shard_map/psum | solution.py:293
  (280 shorter events, 182.5 us)
Async XLA Ops:
  7.2 71.4 %all-gather.7.cloned.1.call-start = ((), (), s32[]{:S(2)}) async-start(), calls=%async_computation.4 | async-start | bytes 3981312 | tf_op jit(solution)/shard_map/all_gather | solution.py:88
  7.9 122.8 %all-gather.9.cloned.1.call-start = ((), (), s32[]{:S(2)}) async-start(), calls=%async_computation.5 | async-start | bytes 7864320 | tf_op jit(solution)/shard_map/all_gather | solution.py:126
  37.1 45.8 %copy-start.32 = (f32[768]{0:T(1024)}, f32[768]{0:T(1024)S(1)}, u32[]{:S(2)}) copy-start(f32[768]{0:T(1024)S(1)} %convert_element_type.164) | copy-start | bytes 9220
  37.1 45.8 %copy-start.21 = (f32[768]{0:T(1024)}, f32[768]{0:T(1024)S(1)}, u32[]{:S(2)}) copy-start(f32[768]{0:T(1024)S(1)} %convert_element_type.163) | copy-start | bytes 9220
  38.5 44.5 %copy-start.15 = (f32[512]{0:T(512)}, f32[512]{0:T(512)S(1)}, u32[]{:S(2)}) copy-start(f32[512]{0:T(512)S(1)} %broadcast_multiply_fusion.5) | copy-start | bytes 6148
  40.0 43.0 %copy-start.27 = (f32[512]{0:T(512)}, f32[512]{0:T(512)S(1)}, u32[]{:S(2)}) copy-start(f32[512]{0:T(512)S(1)} %add_rsqrt_fusion.1) | copy-start | bytes 6148
  84.4 30.0 %copy-start.14 = (s32[1,4]{1,0:T(1,128)S(1)}, s32[1,4]{1,0:T(1,128)}, u32[]{:S(2)}) copy-start(s32[1,4]{1,0:T(1,128)} %param.31) | copy-start | bytes 52
  85.7 29.5 %copy-start.4 = (bf16[512,1536]{1,0:T(8,128)(2,1)S(1)}, bf16[512,1536]{1,0:T(8,128)(2,1)}, u32[]{:S(2)}) copy-start(bf16[512,1536]{1,0:T(8,128)(2,1)} %slice.54) | copy-start | bytes 4718596
  85.7 31.0 %slice-start = ((bf16[512,2304]{1,0:T(8,128)(2,1)}), bf16[512,768]{1,0:T(8,128)(2,1)S(1)}, s32[]{:S(2)}) async-start(bf16[512,2304]{1,0:T(8,128)(2,1)} %copy-done.11), calls=%async_computation.13 | async-start | bytes 1572864 | tf_op jit(solution)/shard_map/slice | solution.py:96
  85.7 139.2 %all-gather.11.cloned.1.call-start = ((), (), s32[]{:S(2)}) async-start(), calls=%async_computation.6 | async-start | bytes 1327104 | tf_op jit(solution)/shard_map/all_gather | solution.py:89
  86.5 168.3 %all-gather.13.cloned.1.call-start = ((), (), s32[]{:S(2)}) async-start(), calls=%async_computation.7 | async-start | bytes 5308416 | tf_op jit(solution)/shard_map/all_gather | solution.py:143
  87.1 247.8 %all-gather.15.cloned.1.call-start = ((), (), s32[]{:S(2)}) async-start(), calls=%async_computation.8 | async-start | bytes 5308416 | tf_op jit(solution)/shard_map/all_gather | solution.py:145
  87.6 629.6 %reduce-scatter.7.cloned.1.call-start = ((), (), s32[]{:S(2)}) async-start(), calls=%async_computation.10 | async-start | bytes 1327104 | tf_op jit(solution)/shard_map/reduce_scatter | solution.py:289
  88.4 259.5 %copy-start.23 = (f32[768]{0:T(1024)}, f32[768]{0:T(1024)S(1)}, u32[]{:S(2)}) copy-start(f32[768]{0:T(1024)S(1)} %convert_element_type.170) | copy-start | bytes 9220
  88.5 166.3 %copy-start.34 = (f32[768]{0:T(1024)}, f32[768]{0:T(1024)S(1)}, u32[]{:S(2)}) copy-start(f32[768]{0:T(1024)S(1)} %convert_element_type.171) | copy-start | bytes 9220
  114.4 220.5 %copy-start.25 = (f32[8,1,384]{2,1,0:T(1,128)}, f32[8,1,384]{2,1,0:T(1,128)S(1)}, u32[]{:S(2)}) copy-start(f32[8,1,384]{2,1,0:T(1,128)S(1)} %convert_element_type.206) | copy-start | bytes 36868
  115.1 232.8 %copy-start.17 = (f32[512]{0:T(512)}, f32[512]{0:T(512)S(1)}, u32[]{:S(2)}) copy-start(f32[512]{0:T(512)S(1)} %fusion.91) | copy-start | bytes 6148
  227.3 117.0 %copy-start.8 = (f32[512,768]{1,0:T(8,128)}, f32[512,768]{1,0:T(8,128)S(1)}, u32[]{:S(2)}) copy-start(f32[512,768]{1,0:T(8,128)S(1)} %get-tuple-element.712) | copy-start | bytes 4718596
  227.4 120.6 %copy-start.19 = (f32[512]{0:T(512)}, f32[512]{0:T(512)S(1)}, u32[]{:S(2)}) copy-start(f32[512]{0:T(512)S(1)} %broadcast_multiply_fusion.4) | copy-start | bytes 6148
  227.7 120.3 %copy-start.29 = (f32[512]{0:T(512)}, f32[512]{0:T(512)S(1)}, u32[]{:S(2)}) copy-start(f32[512]{0:T(512)S(1)} %add_rsqrt_fusion) | copy-start | bytes 6148
  357.0 364.6 %reduce-scatter.5.cloned.1.call-start = ((), (), s32[]{:S(2)}) async-start(), calls=%async_computation.9 | async-start | bytes 3981312 | tf_op jit(solution)/shard_map/reduce_scatter | solution.py:286
  384.6 53.9 %collective-permute-start.1 = (f32[512,1536]{0,1:T(8,128)}, f32[512,1536]{0,1:T(8,128)}, u32[]{:S(2)}, u32[]{:S(2)}) collective-permute-start(f32[512,1536]{0,1:T(8,128)} %maximum_add_fusion.3), channel_id=1, source_target_pairs={{0,1},{1,2},{2,3},{3,0},{4,5},{5,6},{6,7},{7,4},{8,9},{9,10},{10,1... | collective-permute-start | bytes 9437192 | tf_op jit(solution)/shard_map/while/body/eval_jaxpr/ppermute | solution.py:18
  384.7 53.9 %collective-permute-start = (bf16[512,1536]{0,1:T(8,128)(2,1)S(1)}, bf16[512,1536]{0,1:T(8,128)(2,1)}, u32[]{:S(2)}, u32[]{:S(2)}) collective-permute-start(bf16[512,1536]{0,1:T(8,128)(2,1)S(1)} %copy.82), channel_id=1, source_target_pairs={{0,1},{1,2},{2,3},{3,0},{4,5},{5,6},{6,7},{7,4},{8,9},{9,10},{10,1... | collective-permute-start | bytes 4718600 | tf_op jit(solution)/shard_map/while/body/eval_jaxpr/ppermute | solution.py:18
  463.8 53.9 %collective-permute-start.1 = (f32[512,1536]{0,1:T(8,128)}, f32[512,1536]{0,1:T(8,128)}, u32[]{:S(2)}, u32[]{:S(2)}) collective-permute-start(f32[512,1536]{0,1:T(8,128)} %maximum_add_fusion.3), channel_id=1, source_target_pairs={{0,1},{1,2},{2,3},{3,0},{4,5},{5,6},{6,7},{7,4},{8,9},{9,10},{10,1... | collective-permute-start | bytes 9437192 | tf_op jit(solution)/shard_map/while/body/eval_jaxpr/ppermute | solution.py:18
  463.8 53.9 %collective-permute-start = (bf16[512,1536]{0,1:T(8,128)(2,1)S(1)}, bf16[512,1536]{0,1:T(8,128)(2,1)}, u32[]{:S(2)}, u32[]{:S(2)}) collective-permute-start(bf16[512,1536]{0,1:T(8,128)(2,1)S(1)} %copy.82), channel_id=1, source_target_pairs={{0,1},{1,2},{2,3},{3,0},{4,5},{5,6},{6,7},{7,4},{8,9},{9,10},{10,1... | collective-permute-start | bytes 4718600 | tf_op jit(solution)/shard_map/while/body/eval_jaxpr/ppermute | solution.py:18
  543.0 53.9 %collective-permute-start.1 = (f32[512,1536]{0,1:T(8,128)}, f32[512,1536]{0,1:T(8,128)}, u32[]{:S(2)}, u32[]{:S(2)}) collective-permute-start(f32[512,1536]{0,1:T(8,128)} %maximum_add_fusion.3), channel_id=1, source_target_pairs={{0,1},{1,2},{2,3},{3,0},{4,5},{5,6},{6,7},{7,4},{8,9},{9,10},{10,1... | collective-permute-start | bytes 9437192 | tf_op jit(solution)/shard_map/while/body/eval_jaxpr/ppermute | solution.py:18
  543.0 53.9 %collective-permute-start = (bf16[512,1536]{0,1:T(8,128)(2,1)S(1)}, bf16[512,1536]{0,1:T(8,128)(2,1)}, u32[]{:S(2)}, u32[]{:S(2)}) collective-permute-start(bf16[512,1536]{0,1:T(8,128)(2,1)S(1)} %copy.82), channel_id=1, source_target_pairs={{0,1},{1,2},{2,3},{3,0},{4,5},{5,6},{6,7},{7,4},{8,9},{9,10},{10,1... | collective-permute-start | bytes 4718600 | tf_op jit(solution)/shard_map/while/body/eval_jaxpr/ppermute | solution.py:18
  618.3 19.9 %collective-permute-start.2 = (bf16[512,1536]{0,1:T(8,128)(2,1)S(1)}, bf16[512,1536]{0,1:T(8,128)(2,1)S(1)}, u32[]{:S(2)}, u32[]{:S(2)}) collective-permute-start(bf16[512,1536]{0,1:T(8,128)(2,1)S(1)} %fusion.54), channel_id=1, source_target_pairs={{0,1},{1,2},{2,3},{3,0},{4,5},{5,6},{6,7},{7,4},{8,9},{9,10},{10,1... | collective-permute-start | bytes 4718600 | tf_op jit(solution)/shard_map/ppermute | solution.py:18
  618.4 21.0 %copy-start.5 = (bf16[1,512,768]{2,1,0:T(8,128)(2,1)S(1)}, bf16[1,512,768]{2,1,0:T(8,128)(2,1)}, u32[]{:S(2)}) copy-start(bf16[1,512,768]{2,1,0:T(8,128)(2,1)} %param.18) | copy-start | bytes 2359300
  643.5 176.6 %reduce-scatter.9.cloned.1.call-start = ((), (), s32[]{:S(2)}) async-start(), calls=%async_computation.11 | async-start | bytes 5308416 | tf_op jit(solution)/shard_map/reduce_scatter | solution.py:192
  651.5 267.3 %reduce-scatter.11.cloned.1.call-start = ((), (), s32[]{:S(2)}) async-start(), calls=%async_computation.12 | async-start | bytes 5308416 | tf_op jit(solution)/shard_map/reduce_scatter | solution.py:198
  663.3 41.9 %copy-start.3 = (f32[512,768]{1,0:T(8,128)S(1)}, f32[512,768]{1,0:T(8,128)}, u32[]{:S(2)}) copy-start(f32[512,768]{1,0:T(8,128)} %copy-done.2) | copy-start | bytes 4718596
  (37 other events, 177.1 us)
Sparse Core Ops, SparseCore 0:
  10.2 68.3 all-gather.6
  85.8 44.8 all-gather.8
  132.9 41.0 all-gather.10
  176.1 78.6 all-gather.12
  256.8 78.0 all-gather.14
  357.2 62.2 reduce-scatter.6
  643.7 77.9 reduce-scatter.4
  725.3 94.7 reduce-scatter.8
  823.8 94.9 reduce-scatter.10
where the time goes:
time: 998 us; the launch traced here: 993 us
  waiting for transfers between devices  512 us (51%)
  matrix products  199 us (20%)
  blocking collectives  152 us (15%)
  other arithmetic  53.5 us (5%)
  local copies, waits for them, and re-layouts  44.5 us (4%)
  between operations  17.6 us (2%)
    ppermute x7, waiting for transfers between devices, shifted(): lax.ppermute(value, axis, [(i, (i + by) % peers) for i in range(peers)])  156 us
    reduce_scatter x1, waiting for transfers between devices, on_device(): lax.psum_scatter(grad_down_w.astype(jnp.bfloat16), 'dp', scatter_dimensio...  98.7 us
    reduce_scatter x1, waiting for transfers between devices, on_device(): lax.psum_scatter(grad_in_w.astype(jnp.bfloat16), 'dp', scatter_dimension=...  98.5 us
    all_gather x1, waiting for transfers between devices, on_device(): lax.all_gather(w_down, 'dp', axis=0, tiled=True)  73 us
    psum x1, blocking collectives, on_device(): lax.psum((attn_shares[0], attn_shares[1], attn_shares[2], attn_shares[3],...  67.1 us
    unnamed x2, blocking collectives  58.9 us
    all_gather x1, waiting for transfers between devices, on_device(): lax.all_gather(w_qkv, 'dp', axis=0, tiled=True)  38.6 us
    dot_general x4, matrix products, pair_grads(): jnp.einsum('hqk,qhd->khd', probs, grad_in.astype(jnp.float32), precision=...  34.8 us
  transfers between devices with their start and end apart: 16, of which 11 were waited for; matrix products, arithmetic and copies ran while one was open for 26% of the time, Pallas kernels for 0%

commit v1 on v0

v1 whole, which is shorter than its diff:
```python
import functools
import math

import jax
import jax.numpy as jnp
from jax import lax
from jax.experimental import pallas as pl
from jax.experimental.pallas import tpu as pltpu
from jax.sharding import PartitionSpec as P

H = 12

epsilon = 1e-05
gelu_coeff = 0.7978845608
cubic_term = 0.044715
excluded = -1073741824.0
bf16 = jnp.bfloat16
f32 = jnp.float32
LANES = 128
GROUP = 4
VMEM_BYTES = 52 * 1024 * 1024

nt_dims = (((1,), (1,)), ((), ()))
tn_dims = (((0,), (0,)), ((), ()))


def mm(left, right):
    return jnp.dot(left, right, preferred_element_type=f32)


def mm_nt(left, right):
    return lax.dot_general(left, right, nt_dims, preferred_element_type=f32)


def mm_tn(left, right):
    return lax.dot_general(left, right, tn_dims, preferred_element_type=f32)


def whole(memory_space=pltpu.VMEM):
    return pl.BlockSpec(memory_space=memory_space)


def lanes_of(shape):
    return lax.broadcasted_iota(jnp.int32, shape, 1)


def norm_parts(values):
    center = values - jnp.mean(values, axis=-1, keepdims=True)
    spread = jnp.mean(center * center, axis=-1, keepdims=True)
    inverse = lax.rsqrt(spread + epsilon)
    return center * inverse, inverse


def norm_back(scaled, unit, inverse):
    return inverse * (
        scaled
        - jnp.mean(scaled, axis=-1, keepdims=True)
        - unit * jnp.mean(scaled * unit, axis=-1, keepdims=True)
    )


def three_parts(value):
    first = value.astype(bf16).astype(f32)
    rest = value - first
    second = rest.astype(bf16).astype(f32)
    return first, second, rest - second


def with_parts(base, value):
    lane = lanes_of(base.shape)
    one, two, three = three_parts(value)
    return jnp.where(
        lane == 64, one, jnp.where(lane == 65, two, jnp.where(lane == 66, three, base))
    )


def unpack_rows(packed, rows):
    tail = jnp.concatenate([packed[rows:, :64], packed[rows:, 64:]], axis=0)
    return packed[:rows], tail


def swap(value, axis, bit):
    size = lax.axis_size(axis)
    return lax.ppermute(value, axis, [(i, i ^ bit) for i in range(size)])


def gather_dp(piece):
    far = [piece]
    for k in range(1, lax.axis_size("dp") // 2):
        far.append(swap(piece, "dp", 2 * k))
    near = jnp.stack(far)
    return near, swap(near, "dp", 1)


def scatter_dp(even, odd):
    received = swap(odd, "dp", 1)
    parts = []
    for k in range(even.shape[0]):
        parts.append((even[k].astype(f32) + received[k].astype(f32)).astype(bf16))
    total = parts[0].astype(f32)
    for k in range(1, even.shape[0]):
        total = total + swap(parts[k], "dp", 2 * k).astype(f32)
    return total


def sum_far_ctx(value, start):
    bit = start
    while bit < lax.axis_size("ctx"):
        low = value.astype(bf16)
        value = low.astype(f32) + swap(low, "ctx", bit).astype(f32)
        bit *= 2
    return value


def position_of(order_ref, slot, rows):
    index = lax.axis_index("ctx")
    return order_ref[0, lax.bitwise_xor(index, slot)] * rows


def qkv_kernel(length_ref, order_ref, *refs):
    tokens = refs[:GROUP]
    near, cross = refs[GROUP : GROUP + 2]
    q_ref, k_ref, v_ref, first_ref, small_ref, w_ref, sems = refs[GROUP + 2 :]
    halves, rows, _ = near.shape
    row_count, width = tokens[0].shape
    me = lax.axis_index("dp")
    copies = []
    for parity, source in ((0, near), (1, cross)):
        for k in range(halves):
            owner = lax.bitwise_xor(me, 2 * k + parity)
            copies.append(
                pltpu.make_async_copy(
                    source.at[k],
                    w_ref.at[pl.ds(pl.multiple_of(owner * rows, 16), rows)],
                    sems.at[2 * k + parity],
                )
            )
    for copy in copies:
        copy.start()
    for copy in copies:
        copy.wait()
    small = w_ref[:, 512:640].astype(f32).T
    small_ref[...] = small[64:80]
    gain, shift = small[64:65], small[65:66]
    length = length_ref[0]
    lane = lanes_of((row_count, LANES))
    ones = jnp.where((lane >= 64) & (lane < 67), 1.0, 0.0)
    bias_lane = jnp.where(lane == 67, 1.0, 0.0)
    for d in range(GROUP):
        unit, _ = norm_parts(tokens[d][...].astype(f32))
        first = (unit * gain + shift).astype(bf16)
        part = pl.ds(d * row_count, row_count)
        first_ref[part] = first
        qkv = mm(first, w_ref[...]).astype(bf16).astype(f32)

        def head(place):
            block = qkv[:, place // 2 * LANES : (place // 2 + 1) * LANES]
            if place % 2:
                block = pltpu.roll(block, 64, 1)
            return jnp.where(lane < 64, block, 0.0)

        stored = lax.broadcasted_iota(jnp.int32, (row_count, LANES), 0)
        position = position_of(order_ref, d, row_count) + stored
        bias = jnp.where(position < length, 0.0, excluded) * bias_lane
        for h in range(3):
            q_ref[h, part] = (head(2 * h) * 0.125 + bias_lane).astype(bf16)
            k_ref[h, part] = (head(2 * h + 1) + ones + bias).astype(bf16)
            v_ref[h, part] = (head(6 + h) + ones).astype(bf16)


def project(length, order, tokens, near, cross):
    row_count, width = tokens[0].shape
    total = GROUP * row_count
    wide = near.shape[2]
    head_out = jax.ShapeDtypeStruct((3, total, LANES), bf16)
    return pl.pallas_call(
        qkv_kernel,
        out_shape=(
            head_out,
            head_out,
            head_out,
            jax.ShapeDtypeStruct((total, width), bf16),
            jax.ShapeDtypeStruct((16, width), f32),
            jax.ShapeDtypeStruct((width, wide), bf16),
        ),
        in_specs=[whole(pltpu.SMEM)] * 2 + [whole()] * GROUP + [whole(pl.ANY)] * 2,
        out_specs=[whole()] * 6,
        scratch_shapes=[pltpu.SemaphoreType.DMA((2 * near.shape[0],))],
        compiler_params=pltpu.CompilerParams(vmem_limit_bytes=VMEM_BYTES),
        cost_estimate=pl.CostEstimate(
            flops=2 * total * width * wide, bytes_accessed=20 * total * width, transcendentals=0
        ),
    )(length, order, *tokens, near, cross)


def attend_kernel(block_rows, q_ref, k_ref, v_ref, packed_ref, q_out_ref):
    row_count = q_ref.shape[1]
    half = row_count // 2
    lane = lanes_of((block_rows, LANES))
    for i in range(row_count // block_rows):
        part = pl.ds(i * block_rows, block_rows)
        heads = []
        for h in range(3):
            query = q_ref[h, part]
            scores = mm_nt(query, k_ref[h])
            top = jnp.max(scores, axis=1, keepdims=True)
            weights = jnp.exp(scores - top).astype(bf16)
            result = mm(weights, v_ref[h])
            denom = result[:, 64:65]
            heads.append(jnp.where(lane < 64, result / denom, 0.0))
            log_total = top + jnp.log(denom)
            q_out_ref[h, part] = with_parts(query.astype(f32), -log_total).astype(bf16)
        packed_ref[0, part] = (heads[0] + pltpu.roll(heads[1], 64, 1)).astype(bf16)
        for r in range(0, block_rows, half):
            size = min(half, block_rows)
            row = i * block_rows + r
            side, place = row // half, row % half
            packed_ref[
                0, pl.ds(row_count + place, size), 64 * side : 64 * side + 64
            ] = heads[2][r : r + size, :64].astype(bf16)


def attend(query, keys, values, first_slot, slots, row_count):
    total = keys.shape[1]
    block_rows = min(row_count // 2, 256)
    return pl.pallas_call(
        functools.partial(attend_kernel, block_rows),
        grid=(slots,),
        out_shape=(
            jax.ShapeDtypeStruct((slots, row_count * 3 // 2, LANES), bf16),
            jax.ShapeDtypeStruct((3, slots * row_count, LANES), bf16),
        ),
        in_specs=[
            pl.BlockSpec((3, row_count, LANES), lambda s: (0, s + first_slot, 0)),
            whole(),
            whole(),
        ],
        out_specs=(
            pl.BlockSpec((1, row_count * 3 // 2, LANES), lambda s: (s, 0, 0)),
            pl.BlockSpec((3, row_count, LANES), lambda s: (0, s, 0)),
        ),
        compiler_params=pltpu.CompilerParams(vmem_limit_bytes=VMEM_BYTES),
        cost_estimate=pl.CostEstimate(
            flops=3 * slots * row_count * total * 64 * 4 * 4,
            bytes_accessed=3 * total * LANES * 8,
            transcendentals=3 * slots * row_count * total,
        ),
    )(query, keys, values)


def ffn_kernel(length_ref, order_ref, *refs):
    token_ref, cot_ref = refs[:2]
    attn_refs = refs[2 : 2 + GROUP]
    small_ref, bias_ref = refs[6:8]
    pieces = refs[8:16]
    out_ref, dmixed_ref, dattn_ref = refs[16:19]
    even_in, odd_in, sib_in, even_down, odd_down, sib_down = refs[19:25]
    small_grad_ref, bias_grad_ref = refs[25:27]
    w_o, w_i, w_d, g_o, g_i, g_d, second_t, second_ref, dlow_ref, out_acc, ds_acc, sems = refs[27:]
    row_count, width = token_ref.shape
    ff = w_i.shape[1]
    halves, rows, _ = pieces[0].shape
    frows = pieces[4].shape[1]
    me = lax.axis_index("dp")
    index = lax.axis_index("ctx")
    core = lax.rem(index, 2)
    low = lax.rem(index, GROUP)
    half_o, half_i, half_d = width // 2, ff // 2, width // 2

    loads = ([], [], [])
    for side in range(2):
        here = core if side == 0 else 1 - core
        for parity in range(2):
            in_piece = pieces[2 * side + parity]
            down_piece = pieces[4 + 2 * side + parity]
            for k in range(halves):
                owner = lax.bitwise_xor(me, 2 * k + parity)
                at_rows = pl.ds(pl.multiple_of(owner * rows, 16), rows)
                loads[0].append(
                    (
                        in_piece.at[k, :, pl.ds(0, half_o)],
                        w_o.at[at_rows, pl.ds(pl.multiple_of(here * half_o, LANES), half_o)],
                    )
                )
                loads[1].append(
                    (
                        in_piece.at[k, :, pl.ds(half_o, half_i)],
                        w_i.at[at_rows, pl.ds(pl.multiple_of(here * half_i, LANES), half_i)],
                    )
                )
                loads[2].append(
                    (
                        down_piece.at[k],
                        w_d.at[
                            pl.ds(pl.multiple_of(owner * frows, 16), frows),
                            pl.ds(pl.multiple_of(here * half_d, LANES), half_d),
                        ],
                    )
                )
    number = len(loads[0])
    copies = [
        [pltpu.make_async_copy(a, b, sems.at[g * number + i]) for i, (a, b) in enumerate(group)]
        for g, group in enumerate(loads)
    ]
    for group in copies:
        for copy in group:
            copy.start()
    for copy in copies[0]:
        copy.wait()

    def out_rows(d):
        return pl.ds(pl.multiple_of(lax.bitwise_xor(low, d) * 192, 16), 192)

    attn = []
    for d in range(GROUP):
        packed = attn_refs[d][...]
        attn.append(jnp.concatenate(unpack_rows(packed, row_count), axis=1))
    mixed = token_ref[...].astype(f32)
    for d in range(GROUP):
        mixed = mixed + mm(attn[d], w_o[out_rows(d), :])
    unit, inverse = norm_parts(mixed)
    gain = small_ref[2:3]
    second = unit * gain + small_ref[3:4]
    second_ref[...] = second.astype(bf16)
    second_t[...] = second.T.astype(bf16)
    stored = lax.broadcasted_iota(jnp.int32, (row_count, LANES), 0)[:, :1]
    position = position_of(order_ref, 0, row_count) + stored
    valid = jnp.where(position < length_ref[0], 1.0, 0.0)
    dout = cot_ref[...].astype(f32) * valid
    dlow_ref[...] = dout.astype(bf16)
    out_acc[...] = mixed + small_ref[4:5]
    ds_acc[...] = jnp.zeros_like(ds_acc)
    for group in copies[1:]:
        for copy in group:
            copy.wait()
    chunk = 512

    def step(f, carry):
        cols = pl.ds(pl.multiple_of(f * chunk, chunk), chunk)
        hidden = mm(second_ref[...], w_i[:, cols]) + bias_ref[:, cols]
        squared = hidden * hidden
        bent = jnp.tanh(hidden * (gelu_coeff + gelu_coeff * cubic_term * squared))
        plus = 0.5 + 0.5 * bent
        active = (hidden * plus).astype(bf16)
        slope = plus + hidden * (plus * (1.0 - bent)) * (
            gelu_coeff + gelu_coeff * 3.0 * cubic_term * squared
        )
        out_acc[...] += mm(active, w_d[cols, :])
        dhid = (mm_nt(dlow_ref[...], w_d[cols, :]) * slope).astype(bf16)
        g_d[cols, :] = mm_tn(active, dlow_ref[...]).astype(bf16)
        g_i[:, cols] = mm(second_t[...], dhid).astype(bf16)
        bias_grad_ref[:, cols] = jnp.sum(dhid.astype(f32), axis=0, keepdims=True)
        ds_acc[...] += mm_nt(dhid, w_i[:, cols])
        return carry

    lax.fori_loop(0, ff // chunk, step, 0)

    def store(g, index_of, source, target):
        copy = pltpu.make_async_copy(source, target, sems.at[g * number + index_of])
        copy.start()
        return copy

    stores = []
    for side in range(2):
        here = core if side == 0 else 1 - core
        for parity in range(2):
            for k in range(halves):
                owner = lax.bitwise_xor(me, 2 * k + parity)
                at = (side * 2 + parity) * halves + k
                if side == 0:
                    to_in = (even_in, odd_in)[parity].at[k]
                    to_down = (even_down, odd_down)[parity].at[k]
                else:
                    to_in, to_down = sib_in.at[parity, k], sib_down.at[parity, k]
                at_rows = pl.ds(pl.multiple_of(owner * rows, 16), rows)
                stores.append(
                    store(
                        1,
                        at,
                        g_i.at[at_rows, pl.ds(pl.multiple_of(here * half_i, LANES), half_i)],
                        to_in.at[:, pl.ds(half_o, half_i)],
                    )
                )
                stores.append(
                    store(
                        2,
                        at,
                        g_d.at[
                            pl.ds(pl.multiple_of(owner * frows, 16), frows),
                            pl.ds(pl.multiple_of(here * half_d, LANES), half_d),
                        ],
                        to_down,
                    )
                )

    out_ref[...] = (out_acc[...] * valid).astype(bf16)
    ds = ds_acc[...]
    dmixed = dout + norm_back(ds * gain, unit, inverse)
    dmixed_ref[...] = dmixed
    dbranch = dmixed.astype(bf16)
    for d in range(GROUP):
        dattn = mm_nt(dbranch, w_o[out_rows(d), :])
        dattn_ref[d, pl.ds(0, row_count)] = dattn[:, :LANES].astype(bf16)
        half = row_count // 2
        dattn_ref[d, pl.ds(row_count, half), :64] = dattn[:half, LANES:].astype(bf16)
        dattn_ref[d, pl.ds(row_count, half), 64:] = dattn[half:, LANES:].astype(bf16)
    for d in range(GROUP):
        g_o[out_rows(d), :] = mm_tn(attn[d], dbranch).astype(bf16)
    for side in range(2):
        here = core if side == 0 else 1 - core
        for parity in range(2):
            for k in range(halves):
                owner = lax.bitwise_xor(me, 2 * k + parity)
                at = (side * 2 + parity) * halves + k
                if side == 0:
                    to_in = (even_in, odd_in)[parity].at[k]
                else:
                    to_in = sib_in.at[parity, k]
                stores.append(
                    store(
                        0,
                        at,
                        g_o.at[
                            pl.ds(pl.multiple_of(owner * rows, 16), rows),
                            pl.ds(pl.multiple_of(here * half_o, LANES), half_o),
                        ],
                        to_in.at[:, pl.ds(0, half_o)],
                    )
                )
    small_grad_ref[...] = jnp.zeros_like(small_grad_ref)
    small_grad_ref[2:3] = jnp.sum(ds * unit, axis=0, keepdims=True)
    small_grad_ref[3:4] = jnp.sum(ds, axis=0, keepdims=True)
    small_grad_ref[4:5] = jnp.sum(dout, axis=0, keepdims=True)
    for copy in stores:
        copy.wait()


def feed_forward(length, order, tokens, cotangent, attn, small, bias, in_pieces, down_pieces, ff):
    row_count, width = tokens.shape
    halves, rows, wide = in_pieces[0].shape
    frows, narrow = down_pieces[0].shape[1:]
    in_half = jax.ShapeDtypeStruct((halves, rows, wide), bf16)
    down_half = jax.ShapeDtypeStruct((halves, frows, narrow), bf16)
    return pl.pallas_call(
        ffn_kernel,
        out_shape=(
            jax.ShapeDtypeStruct((row_count, width), bf16),
            jax.ShapeDtypeStruct((row_count, width), f32),
            jax.ShapeDtypeStruct((GROUP, row_count * 3 // 2, LANES), bf16),
            in_half,
            in_half,
            jax.ShapeDtypeStruct((2, halves, rows, wide), bf16),
            down_half,
            down_half,
            jax.ShapeDtypeStruct((2, halves, frows, narrow), bf16),
            jax.ShapeDtypeStruct((16, width), f32),
            jax.ShapeDtypeStruct((1, ff), f32),
        ),
        in_specs=[whole(pltpu.SMEM)] * 2 + [whole()] * 8 + [whole(pl.ANY)] * 8,
        out_specs=[whole()] * 3 + [whole(pl.ANY)] * 6 + [whole()] * 2,
        scratch_shapes=[
            pltpu.VMEM((width, width), bf16),
            pltpu.VMEM((width, ff), bf16),
            pltpu.VMEM((ff, width), bf16),
            pltpu.VMEM((width, width), bf16),
            pltpu.VMEM((width, ff), bf16),
            pltpu.VMEM((ff, width), bf16),
            pltpu.VMEM((width, row_count), bf16),
            pltpu.VMEM((row_count, width), bf16),
            pltpu.VMEM((row_count, width), bf16),
            pltpu.VMEM((row_count, width), f32),
            pltpu.VMEM((row_count, width), f32),
            pltpu.SemaphoreType.DMA((12 * halves,)),
        ],
        compiler_params=pltpu.CompilerParams(vmem_limit_bytes=VMEM_BYTES),
        cost_estimate=pl.CostEstimate(
            flops=2 * row_count * width * (6 * ff + 4 * width),
            bytes_accessed=8 * width * ff + 8 * width * width,
            transcendentals=row_count * ff,
        ),
    )(length, order, tokens, cotangent, *attn, small, bias, *in_pieces, *down_pieces)


def attend_back_kernel(final, row_count, *refs):
    q_ref, k_ref, v_ref, near_attn, far_attn = refs[:5]
    dattn_refs = refs[5 : 5 + GROUP]
    outs = refs[5 + GROUP : -5]
    grad_ref, k_turned, dq_ref, dk_ref, dv_ref = refs[-5:]
    head, slot = pl.program_id(0), pl.program_id(1)
    total = k_ref.shape[1]
    chunk = row_count

    @pl.when((head == 0) & (slot == 0))
    def _():
        lane = lanes_of((row_count, LANES))
        for d in range(GROUP):
            packed = dattn_refs[d][...]
            attn = (near_attn if d < 2 else far_attn)[d % 2]
            top, tail = unpack_rows(packed.astype(f32), row_count)
            top_a, tail_a = unpack_rows(attn.astype(f32), row_count)
            product = top * top_a
            heads = (
                (top, jnp.sum(jnp.where(lane < 64, product, 0.0), axis=1, keepdims=True)),
                (
                    pltpu.roll(top, 64, 1),
                    jnp.sum(jnp.where(lane >= 64, product, 0.0), axis=1, keepdims=True),
                ),
                (
                    jnp.concatenate([tail, tail], axis=1),
                    jnp.sum(tail * tail_a, axis=1, keepdims=True),
                ),
            )
            for h, (block, delta) in enumerate(heads):
                base = jnp.where(lane < 64, block, 0.0)
                grad_ref[h, pl.ds(d * row_count, row_count)] = with_parts(base, -delta).astype(bf16)

    @pl.when(slot == 0)
    def _():
        k_turned[...] = k_ref[0].astype(f32).T.astype(bf16)
        dk_ref[...] = jnp.zeros_like(dk_ref)
        dv_ref[...] = jnp.zeros_like(dv_ref)

    query = q_ref[0]
    part = pl.ds(pl.multiple_of(slot * row_count, row_count), row_count)
    grad = grad_ref[head, part]
    turned = jnp.zeros((LANES, row_count), f32)
    for c in range(total // chunk):
        at = pl.ds(c * chunk, chunk)
        probs = jnp.exp(mm_nt(k_ref[0, at], query))
        dscores = (probs * mm_nt(v_ref[0, at], grad)).astype(bf16)
        dv_ref[at] += mm(probs.astype(bf16), grad)
        dk_ref[at] += mm(dscores, query)
        turned = turned + mm(k_turned[:, at], dscores)
    dq_ref[part] = turned.T * 0.125

    @pl.when(slot == GROUP - 1)
    def _():
        if final:
            one_ref, two_ref = outs
            lane = lanes_of(dq_ref.shape)
            one_ref[0] = jnp.where(
                lane < 64, dq_ref[...], pltpu.roll(dk_ref[...], 64, 1)
            ).astype(bf16)
            two_ref[0] = jnp.where(lane < 64, dv_ref[...], 0.0).astype(bf16)
        else:
            outs[0][0] = dq_ref[...]
            outs[1][0] = dk_ref[...]
            outs[2][0] = dv_ref[...]


def attend_back(query, keys, values, near_attn, far_attn, dattn, final):
    rows = query.shape[1]
    row_count = rows // GROUP
    total = keys.shape[1]

    def per_head(size, kind):
        return (
            jax.ShapeDtypeStruct((3, size, LANES), kind),
            pl.BlockSpec((1, size, LANES), lambda h, s: (h, 0, 0)),
        )

    if final:
        outs = [per_head(rows, bf16), per_head(rows, bf16)]
    else:
        outs = [per_head(rows, f32), per_head(total, f32), per_head(total, f32)]
    return pl.pallas_call(
        functools.partial(attend_back_kernel, final, row_count),
        grid=(3, GROUP),
        out_shape=[shape for shape, _ in outs],
        out_specs=[spec for _, spec in outs],
        in_specs=[
            pl.BlockSpec((1, row_count, LANES), lambda h, s: (h, s, 0)),
            pl.BlockSpec((1, total, LANES), lambda h, s: (h, 0, 0)),
            pl.BlockSpec((1, total, LANES), lambda h, s: (h, 0, 0)),
        ]
        + [whole()] * (2 + GROUP),
        scratch_shapes=[
            pltpu.VMEM((3, rows, LANES), bf16),
            pltpu.VMEM((LANES, total), bf16),
            pltpu.VMEM((rows, LANES), f32),
            pltpu.VMEM((total, LANES), f32),
            pltpu.VMEM((total, LANES), f32),
        ],
        compiler_params=pltpu.CompilerParams(vmem_limit_bytes=VMEM_BYTES),
        cost_estimate=pl.CostEstimate(
            flops=3 * rows * total * 64 * 2 * 5 * 4,
            bytes_accessed=3 * total * LANES * 12,
            transcendentals=3 * rows * total,
        ),
    )(query, keys, values, near_attn, far_attn, *dattn)


def tail_kernel(one_ref, two_ref, first_ref, w_ref, grads_ref, *refs):
    even_ref, odd_ref, keep_ref, send_ref, d_ref, g_ref, sems = refs
    total, width = first_ref.shape
    row_count = total // GROUP
    halves, rows, _ = even_ref.shape
    me = lax.axis_index("dp")
    for h in range(3):
        d_ref[:, h * LANES : (h + 1) * LANES] = one_ref[h]
    moved = pltpu.roll(two_ref[1].astype(f32), 64, 1).astype(bf16)
    d_ref[:, 384:512] = two_ref[0] + moved
    d_ref[:, 512:640] = two_ref[2]
    for d in range(GROUP):
        part = mm_nt(d_ref[d * row_count : (d + 1) * row_count], w_ref[...]).astype(bf16)
        (send_ref if d % 2 else keep_ref)[d // 2] = part
    weights = w_ref[...].astype(f32)
    grad = mm_tn(first_ref[...], d_ref[...])
    columns = jnp.sum(d_ref[...].astype(f32), axis=0, keepdims=True)
    gain, shift = weights[:, 576:577], weights[:, 577:578]
    gain_grad = jnp.sum(weights * (grad - shift * columns), axis=1, keepdims=True) / gain
    shift_grad = jnp.sum(weights * columns, axis=1, keepdims=True)
    g_ref[:, :512] = grad[:, :512].astype(bf16)
    lane = lanes_of((width, LANES))
    turned = jnp.concatenate(
        [jnp.zeros((64, width), f32), grads_ref[...], jnp.zeros((48, width), f32)], axis=0
    ).T
    last = jnp.where(lane < 64, grad[:, 512:640], turned)
    last = jnp.where(lane == 64, gain_grad, jnp.where(lane == 65, shift_grad, last))
    g_ref[:, 512:640] = last.astype(bf16)
    copies = []
    for parity in range(2):
        for k in range(halves):
            owner = lax.bitwise_xor(me, 2 * k + parity)
            copies.append(
                pltpu.make_async_copy(
                    g_ref.at[pl.ds(pl.multiple_of(owner * rows, 16), rows)],
                    (even_ref, odd_ref)[parity].at[k],
                    sems.at[2 * k + parity],
                )
            )
    for copy in copies:
        copy.start()
    for copy in copies:
        copy.wait()


def tail(one, two, first, weights, grads, halves):
    total, width = first.shape
    wide = weights.shape[1]
    rows = width // (2 * halves)
    piece = jax.ShapeDtypeStruct((halves, rows, wide), bf16)
    pair = jax.ShapeDtypeStruct((2, total // GROUP, width), bf16)
    return pl.pallas_call(
        tail_kernel,
        out_shape=(piece, piece, pair, pair),
        in_specs=[whole()] * 5,
        out_specs=[whole(pl.ANY)] * 2 + [whole()] * 2,
        scratch_shapes=[
            pltpu.VMEM((total, wide), bf16),
            pltpu.VMEM((width, wide), bf16),
            pltpu.SemaphoreType.DMA((2 * halves,)),
        ],
        compiler_params=pltpu.CompilerParams(vmem_limit_bytes=VMEM_BYTES),
        cost_estimate=pl.CostEstimate(
            flops=4 * total * width * wide, bytes_accessed=8 * total * width, transcendentals=0
        ),
    )(one, two, first, weights, grads)


def last_kernel(token_ref, one_ref, two_ref, three_ref, dmixed_ref, small_ref, out_ref):
    unit, inverse = norm_parts(token_ref[...].astype(f32))
    df = one_ref[...].astype(f32) + two_ref[...].astype(f32) + three_ref[...].astype(f32)
    back = norm_back(df * small_ref[0:1], unit, inverse)
    out_ref[...] = (dmixed_ref[...] + back).astype(bf16)


def last(tokens, one, two, three, dmixed, small):
    return pl.pallas_call(
        last_kernel,
        out_shape=jax.ShapeDtypeStruct(tokens.shape, bf16),
        in_specs=[whole()] * 6,
        out_specs=whole(),
        compiler_params=pltpu.CompilerParams(vmem_limit_bytes=VMEM_BYTES),
    )(tokens, one, two, three, dmixed, small)


def on_device(
    tokens,
    attn_gain,
    attn_shift,
    w_qkv,
    w_out,
    ffn_gain,
    ffn_shift,
    w_in,
    b_in,
    w_down,
    b_down,
    cotangent,
    lengths,
    block_order,
):
    mine = tokens[0]
    row_count, width = mine.shape
    ctx_size = lax.axis_size("ctx")
    dp_size = lax.axis_size("dp")
    index = lax.axis_index("ctx")
    low = lax.rem(index, GROUP)
    core = lax.rem(index, 2)
    far = ctx_size // GROUP
    rows = w_qkv.shape[0]
    ff = w_in.shape[1]
    per_row = b_in.shape[0] // rows
    assert math.gcd(H, ctx_size) == GROUP

    mine_qkv = lax.dynamic_index_in_dim(w_qkv.reshape(rows, 3, GROUP, 3, 64), low, 2, False)
    columns = [mine_qkv[:, 0, 0], mine_qkv[:, 1, 0], mine_qkv[:, 0, 1], mine_qkv[:, 1, 1]]
    columns += [mine_qkv[:, 0, 2], mine_qkv[:, 1, 2]]
    columns += [mine_qkv[:, 2, 0], mine_qkv[:, 2, 1], mine_qkv[:, 2, 2]]
    smalls = [attn_gain, attn_shift, ffn_gain, ffn_shift, b_down]
    columns += [v[:, None] for v in smalls] + [b_in.reshape(per_row, rows).T]
    columns.append(jnp.zeros((rows, 640 - 576 - 5 - per_row), bf16))
    qkv_piece = jnp.concatenate(columns, axis=1)
    near_qkv, cross_qkv = gather_dp(qkv_piece)

    side = swap(mine, "ctx", 1)
    over = swap(mine, "ctx", 2)
    blocks = [mine, side, over, swap(over, "ctx", 1)]

    half_out = lax.dynamic_slice_in_dim(w_out, core * (width // 2), width // 2, 1)
    half_in = lax.dynamic_slice_in_dim(w_in, core * (ff // 2), ff // 2, 1)
    half_down = lax.dynamic_slice_in_dim(w_down, core * (width // 2), width // 2, 1)
    in_pieces = gather_dp(jnp.concatenate([half_out, half_in], axis=1))
    down_pieces = gather_dp(half_down)
    in_pieces += tuple(swap(p, "ctx", 1) for p in in_pieces)
    down_pieces += tuple(swap(p, "ctx", 1) for p in down_pieces)

    query, keys, values, first, small, qkv_weight = project(
        lengths, block_order, blocks, near_qkv, cross_qkv
    )
    bias = small[5 : 5 + per_row].reshape(per_row, dp_size, rows).transpose(1, 0, 2).reshape(1, ff)
    if far > 1:
        groups = [[g * GROUP + i for g in range(far)] for i in range(GROUP)]
        keys = lax.all_gather(keys, "ctx", axis=1, tiled=True, axis_index_groups=groups)
        values = lax.all_gather(values, "ctx", axis=1, tiled=True, axis_index_groups=groups)
    far_attn, far_query = attend(query, keys, values, 2, 2, row_count)
    near_attn, near_query = attend(query, keys, values, 0, 2, row_count)
    attn = [
        near_attn[0],
        swap(near_attn[1], "ctx", 1),
        swap(far_attn[0], "ctx", 2),
        swap(far_attn[1], "ctx", 3),
    ]
    (
        layer_out,
        dmixed,
        dattn,
        even_in,
        odd_in,
        sib_in,
        even_down,
        odd_down,
        sib_down,
        small_grad,
        bias_grad,
    ) = feed_forward(
        lengths, block_order, mine, cotangent[0], attn, small, bias, in_pieces, down_pieces, ff
    )
    dattn = [dattn[0]] + [swap(dattn[d], "ctx", d) for d in range(1, GROUP)]

    def reduce_pair(even, odd, sib):
        received = swap(sib, "ctx", 1)
        even = (even.astype(f32) + received[0].astype(f32)).astype(bf16)
        odd = (odd.astype(f32) + received[1].astype(f32)).astype(bf16)
        return sum_far_ctx(scatter_dp(even, odd), 2).astype(bf16)

    def both_halves(half):
        other = swap(half, "ctx", 1)
        left = jnp.where(core == 0, half, other).astype(f32)
        right = jnp.where(core == 0, other, half).astype(f32)
        return left, right

    down_left, down_right = both_halves(reduce_pair(even_down, odd_down, sib_down))
    in_left, in_right = both_halves(reduce_pair(even_in, odd_in, sib_in))
    grad_w_down = jnp.concatenate([down_left, down_right], axis=1)
    cut = width // 2
    grad_w_out = jnp.concatenate([in_left[:, :cut], in_right[:, :cut]], axis=1)
    grad_w_in = jnp.concatenate([in_left[:, cut:], in_right[:, cut:]], axis=1)

    all_query = jnp.concatenate([near_query, far_query], axis=1)
    grads = attend_back(all_query, keys, values, near_attn, far_attn, dattn, far == 1)
    if far > 1:
        dq, dk, dv = grads
        dk, dv = (
            lax.psum_scatter(
                v, "ctx", scatter_dimension=1, tiled=True, axis_index_groups=groups
            )
            for v in (dk, dv)
        )
        one = jnp.concatenate([dq[..., :64], dk[..., :64]], axis=-1).astype(bf16)
        two = jnp.concatenate([dv[..., :64], jnp.zeros_like(dv[..., :64])], axis=-1).astype(bf16)
    else:
        one, two = grads
    bias_rows = bias_grad.reshape(dp_size, per_row, rows).transpose(1, 0, 2).reshape(per_row, width)
    small_grads = jnp.concatenate([small_grad[:5], bias_rows, small_grad[5 + per_row :]], axis=0)
    even, odd, keep, send = tail(one, two, first, qkv_weight, small_grads, dp_size // 2)
    back = swap(send[1], "ctx", 1)
    crossing = (keep[1].astype(f32) + back.astype(f32)).astype(bf16)
    near_back = swap(send[0], "ctx", 1)
    input_grad = last(mine, keep[0], near_back, swap(crossing, "ctx", 2), dmixed, small)

    share = sum_far_ctx(scatter_dp(even, odd), GROUP).astype(bf16)
    share_over = swap(share, "ctx", 2)
    shares = jnp.stack([share, swap(share, "ctx", 1), share_over, swap(share_over, "ctx", 1)])
    places = lax.bitwise_xor(low, jnp.arange(GROUP, dtype=jnp.int32))
    shares = jnp.take(shares, places, axis=0).astype(f32)
    heads = shares[:, :, :576].reshape(GROUP, rows, 9, 64)
    pick = [heads[:, :, [0, 2, 4]], heads[:, :, [1, 3, 5]], heads[:, :, [6, 7, 8]]]
    grad_w_qkv = jnp.stack(pick, axis=1).transpose(2, 1, 0, 3, 4).reshape(rows, 3 * width)
    small_sum = jnp.sum(shares[:, :, 576 : 581 + per_row], axis=0)
    small_list = [small_sum[:, i] for i in range(5)]
    grad_b_in = small_sum[:, 5:].T.reshape(-1)
    return (
        layer_out[None],
        input_grad[None],
        small_list[0],
        small_list[1],
        grad_w_qkv,
        grad_w_out,
        small_list[2],
        small_list[3],
        grad_w_in,
        grad_b_in,
        grad_w_down,
        small_list[4],
    )


def solution(mesh):
    placed = (
        P("dp", "ctx", None),
        P("dp"),
        P("dp"),
        P("dp", None),
        P("dp", None),
        P("dp"),
        P("dp"),
        P("dp", None),
        P("dp"),
        P("dp", None),
        P("dp"),
        P("dp", "ctx", None),
        P("dp"),
        P("dp", None),
    )
    return jax.shard_map(
        on_device,
        mesh=mesh,
        in_specs=placed,
        out_specs=(
            P("dp", "ctx", None),
            P("dp", "ctx", None),
            P("dp"),
            P("dp"),
            P("dp", None),
            P("dp", None),
            P("dp"),
            P("dp"),
            P("dp", None),
            P("dp"),
            P("dp", None),
            P("dp"),
        ),
        check_vma=False,
    )
```

time: 998 us -> 399 us (0.40)
  waiting for transfers between devices: 512 us -> 149 us
  matrix products: 199 us -> 0 us
  blocking collectives: 152 us -> 0 us
  Pallas kernels: 0 us -> 121 us
  starting transfers between devices: 5.1 us -> 73.7 us
  local copies, waits for them, and re-layouts: 44.5 us -> 18.7 us
  other arithmetic: 53.5 us -> 30.9 us
  between operations: 17.6 us -> 2.21 us
    reduce_scatter x4 -> x0, waiting for transfers between devices: 202 us -> none  [the longest x1 98.7 us: on_device(): lax.psum_scatter(grad_down_w.astype(jnp.bfloat16), 'dp', scatter_dimensio...]
    dot_general x40 -> x0, matrix products: 199 us -> none  [the longest x4 34.8 us: pair_grads(): jnp.einsum('hqk,qhd->khd', probs, grad_in.astype(jnp.float32), precision=...]
    all_gather x5 -> x0, waiting for transfers between devices: 152 us -> none  [the longest x1 73 us: on_device(): lax.all_gather(w_down, 'dp', axis=0, tiled=True)]
    pallas_call x0 -> x7, Pallas kernels: none -> 121 us  [the longest x1 39.2 us: attend_back(): pl.pallas_call(functools.partial(attend_back_kernel, final, row_count), g...]
    ppermute x7 -> x49, starting transfers between devices: 4.74 us -> 73.7 us  [swap(): return lax.ppermute(value, axis, [(i, i ^ bit) for i in range(size)])]
    psum x1 -> x0, blocking collectives: 67.1 us -> none  [on_device(): lax.psum((attn_shares[0], attn_shares[1], attn_shares[2], attn_shares[3],...]
    unnamed x2 -> x0, blocking collectives: 58.9 us -> none
    all_gather x1 -> x0, blocking collectives: 25.9 us -> none  [on_device(): lax.all_gather(b_in, 'dp', axis=0, tiled=True)]
  transfers between devices with their start and end apart: 16 -> 49, of which waited for: 11 -> 19; matrix products, arithmetic and copies ran while one was open for 26% -> 11% of each run, Pallas kernels for 0% -> 23%
where the time goes in v1:
time: 399 us; the launch traced here: 395 us
  waiting for transfers between devices  149 us (37%)
  Pallas kernels  121 us (30%)
  starting transfers between devices  73.7 us (18%)
  other arithmetic  30.9 us (8%)
  local copies, waits for them, and re-layouts  18.7 us (5%)
    ppermute x49, waiting for transfers between devices, swap(): return lax.ppermute(value, axis, [(i, i ^ bit) for i in range(size)])  149 us
    ppermute x49, starting transfers between devices, swap(): return lax.ppermute(value, axis, [(i, i ^ bit) for i in range(size)])  73.7 us
    pallas_call x1, Pallas kernels, attend_back(): pl.pallas_call(functools.partial(attend_back_kernel, final, row_count), g...  39.2 us
    pallas_call x1, Pallas kernels, feed_forward(): pl.pallas_call(ffn_kernel, out_shape=(jax.ShapeDtypeStruct((row_count, wi...  31 us
    pallas_call x2, Pallas kernels, attend(): pl.pallas_call(functools.partial(attend_kernel, block_rows), grid=(slots,...  23.8 us
    pallas_call x1, Pallas kernels, tail(): pl.pallas_call(tail_kernel, out_shape=(piece, piece, pair, pair), in_spec...  12.1 us
    pallas_call x1, Pallas kernels, project(): pl.pallas_call(qkv_kernel, out_shape=(head_out, head_out, head_out, jax.S...  10.6 us
  transfers between devices with their start and end apart: 49, of which 19 were waited for; matrix products, arithmetic and copies ran while one was open for 11% of the time, Pallas kernels for 23%

profile of v1, /device:TPU:0, one launch (start us, length us, event | category | flops | bytes accessed | tf_op | source)
XLA Modules:
  0.0 394.8 jit_solution(677700220457356918)
XLA Ops:
  2.8 3.1 collective-permute-start.10
  5.8 2.6 collective-permute-start.11
  10.1 3.5 collective-permute-start.17
  13.6 8.8 %collective-permute-done.10 = bf16[96,1920]{1,0:T(8,128)(2,1)S(1)} collective-permute-done((bf16[96,1920]{1,0:T(8,128)(2,1)S(1)}, bf16[96,1920]{1,0:T(8,128)(2,1)S(1)}, u32[]{:S(2)}, u32[]{:S(2)}) %collective-permute-start.10) | collective-permute-done | bytes 368672 | tf_op jit(solution)/shard_map/ppermute | solution.py:84
  23.1 4.6 %collective-permute-start.18 = (bf16[384,384]{1,0:T(8,128)(2,1)}, bf16[384,384]{1,0:T(8,128)(2,1)}, u32[]{:S(2)}, u32[]{:S(2)}) collective-permute-start(bf16[384,384]{1,0:T(8,128)(2,1)} %constant_dynamic-slice_fusion), channel_id=1, source_target_pairs={{0,24},{4,28},{8,16},{12,20},{16,8},{20,12},{24,0},{28,4},{1,25},{... | collective-permute-start | bytes 884744 | tf_op jit(solution)/shard_map/ppermute | solution.py:84
  28.1 6.1 %collective-permute-done.11 = bf16[96,1920]{1,0:T(8,128)(2,1)} collective-permute-done((bf16[96,1920]{1,0:T(8,128)(2,1)S(1)}, bf16[96,1920]{1,0:T(8,128)(2,1)}, u32[]{:S(2)}, u32[]{:S(2)}) %collective-permute-start.11) | collective-permute-done | bytes 368672 | tf_op jit(solution)/shard_map/ppermute | solution.py:84
  35.7 2.6 pad_maximum_fusion.1.refs_8_
  39.8 21.3 %collective-permute-done.17 = bf16[384,384]{1,0:T(8,128)(2,1)} collective-permute-done((bf16[384,384]{1,0:T(8,128)(2,1)}, bf16[384,384]{1,0:T(8,128)(2,1)}, u32[]{:S(2)}, u32[]{:S(2)}) %collective-permute-start.17) | collective-permute-done | bytes 294944 | tf_op jit(solution)/shard_map/ppermute | solution.py:84
  66.3 5.5 %collective-permute-start.3 = (bf16[96,640]{1,0:T(8,128)(2,1)S(1)}, bf16[96,640]{1,0:T(8,128)(2,1)S(1)}, u32[]{:S(2)}, u32[]{:S(2)}) collective-permute-start(bf16[96,640]{1,0:T(8,128)(2,1)S(1)} %concatenate.24), channel_id=1, source_target_pairs={{0,8},{4,12},{8,0},{12,4},{16,24},{20,28},{24,16},{28,20},{1,9},{5... | collective-permute-start | bytes 368648 | tf_op jit(solution)/shard_map/ppermute | solution.py:84
  72.9 3.0 collective-permute-done.3
  76.4 2.5 collective-permute-done.4
  81.3 4.3 %collective-permute-done.5 = bf16[96,640]{1,0:T(8,128)(2,1)S(1)} collective-permute-done((bf16[96,640]{1,0:T(8,128)(2,1)S(1)}, bf16[96,640]{1,0:T(8,128)(2,1)S(1)}, u32[]{:S(2)}, u32[]{:S(2)}) %collective-permute-start.5) | collective-permute-done | bytes 122912 | tf_op jit(solution)/shard_map/ppermute | solution.py:84
  87.0 17.4 %collective-permute-done.6.refs_5_ = bf16[4,96,640]{2,1,0:T(8,128)(2,1)S(1)} collective-permute-done((bf16[4,96,640]{2,1,0:T(8,128)(2,1)S(1)}, bf16[4,96,640]{2,1,0:T(8,128)(2,1)S(1)}, u32[]{:S(2)}, u32[]{:S(2)}) %collective-permute-start.6) | collective-permute-done | bytes 491552 | tf_op jit(solution)/shard_map/ppermute | solution.py:84
  106.2 10.6 %shard_map.256 = (bf16[3,2048,128]{2,1,0:T(8,128)(2,1)}, bf16[3,2048,128]{2,1,0:T(8,128)(2,1)}, bf16[3,2048,128]{2,1,0:T(8,128)(2,1)}, bf16[2048,768]{1,0:T(8,12...) custom-call(s32[1]{0:T(128)S(6)} %copy.82.length_ref, s32[1,4]{1,0:T(1,128)S(1)} %copy-done.4, ...), custom_call_target="tpu_custom_call" | custom-call | flops 2013265920 | bytes 31457280 | tf_op jit(solution)/shard_map/pallas_call | solution.py:176
  117.4 11.8 %shard_map.258 = (bf16[2,768,128]{2,1,0:T(8,128)(2,1)S(1)}, bf16[3,1024,128]{2,1,0:T(8,128)(2,1)S(1)}) custom-call(bf16[3,2048,128]{2,1,0:T(8,128)(2,1)} %get-tuple-element.39.q_ref, bf16[3,2048,128]{2,1,0:T(8,128)(2,1)} %get-tuple-element.40.k_ref.refs_1_, bf16[3,2048,128]{2,1,0:T(8,128)(2,1)} %get-tuple-element.41.v_ref.refs_2_), custom_call_target="tpu_custom_call" | custom-call | flops 6442450944 | bytes 6291456 | tf_op jit(solution)/shard_map/pallas_call | solution.py:226
  130.8 12.0 %shard_map.257 = (bf16[2,768,128]{2,1,0:T(8,128)(2,1)S(1)}, bf16[3,1024,128]{2,1,0:T(8,128)(2,1)S(1)}) custom-call(bf16[3,2048,128]{2,1,0:T(8,128)(2,1)} %get-tuple-element.39.q_ref, bf16[3,2048,128]{2,1,0:T(8,128)(2,1)} %get-tuple-element.40.k_ref.refs_1_, bf16[3,2048,128]{2,1,0:T(8,128)(2,1)} %get-tuple-element.41.v_ref.refs_2_), custom_call_target="tpu_custom_call" | custom-call | flops 6442450944 | bytes 6291456 | tf_op jit(solution)/shard_map/pallas_call | solution.py:226
  144.7 5.9 %collective-permute-done.9.refs_5_ = bf16[768,128]{1,0:T(8,128)(2,1)S(1)} collective-permute-done((bf16[768,128]{1,0:T(8,128)(2,1)S(1)}, bf16[768,128]{1,0:T(8,128)(2,1)S(1)}, u32[]{:S(2)}, u32[]{:S(2)}) %collective-permute-start.9) | collective-permute-done | bytes 196640 | tf_op jit(solution)/shard_map/ppermute | solution.py:84
  150.7 31.0 %shard_map.259 = (bf16[512,768]{1,0:T(8,128)(2,1)}, f32[512,768]{1,0:T(8,128)}, bf16[4,768,128]{2,1,0:T(8,128)(2,1)S(1)}, bf16[4,96,1920]{2,1,0:T(8,128)(2,1)}, ...) custom-call(s32[1]{0:T(128)S(6)} %copy.82.length_ref, ...), custom_call_target="tpu_custom_call" | custom-call | flops 16911433728 | bytes 23592960 | tf_op jit(solution)/shard_map/pallas_call | solution.py:444
  187.7 2.8 collective-permute-done.23.refs_7_
  190.5 3.3 collective-permute-done.24.refs_8_
  193.8 39.2 %shard_map.260 = (bf16[3,2048,128]{2,1,0:T(8,128)(2,1)}, bf16[3,2048,128]{2,1,0:T(8,128)(2,1)}) custom-call(bf16[3,2048,128]{2,1,0:T(8,128)(2,1)} %pad_maximum_fusion.refs_0_, bf16[3,2048,128]{2,1,0:T(8,128)(2,1)} %get-tuple-element.40.k_ref.refs_1_, bf16[3,2048,128]{2,1,0:T(8,128)(2,1)} %get-tuple-element.41.v_ref.refs_2_, ...), custom_call_target="tpu_custom_call" | custom-call | flops 32212254720 | bytes 9437184 | tf_op jit(solution)/shard_map/pallas_call | solution.py:566
  233.1 12.1 %shard_map.261 = (bf16[4,96,640]{2,1,0:T(8,128)(2,1)S(1)}, bf16[4,96,640]{2,1,0:T(8,128)(2,1)S(1)}, bf16[2,512,768]{2,1,0:T(8,128)(2,1)}, bf16[2,512,768]{2,1,0:T(8,128)(2,1)}) custom-call(bf16[3,2048,128]{2,1,0:T(8,128)(2,1)} %get-tuple-element.49.one_ref, bf16[3,2048,128]{2,1,0:T(8,128)(2,1)} %get-tuple-element.50.two_ref, ...), custom_call_target="tpu_custom_call" | custom-call | flops 4026531840 | bytes 12582912 | tf_op jit(solution)/shard_map/pallas_call | solution.py:644
  249.3 9.3 %collective-permute-done.28 = bf16[4,96,640]{2,1,0:T(8,128)(2,1)S(1)} collective-permute-done((bf16[4,96,640]{2,1,0:T(8,128)(2,1)S(1)}, bf16[4,96,640]{2,1,0:T(8,128)(2,1)S(1)}, u32[]{:S(2)}, u32[]{:S(2)}) %collective-permute-start.28) | collective-permute-done | bytes 491552 | tf_op jit(solution)/shard_map/ppermute | solution.py:84
  258.7 21.1 %collective-permute-start.29 = (bf16[96,640]{1,0:T(8,128)(2,1)S(1)}, bf16[96,640]{1,0:T(8,128)(2,1)S(1)}, u32[]{:S(2)}, u32[]{:S(2)}) collective-permute-start(bf16[96,640]{1,0:T(8,128)(2,1)S(1)} %get-tuple-element.119), channel_id=1, source_target_pairs={{0,8},{4,12},{8,0},{12,4},{16,24},{20,28},{24,16},{28,20},{1,9},{5... | collective-permute-start | bytes 368648 | tf_op jit(solution)/shard_map/ppermute | solution.py:84
  282.3 3.8 fusion.3
  287.6 3.8 fusion.1
  292.7 4.2 %collective-permute-done.33 = bf16[96,640]{1,0:T(8,128)(2,1)S(1)} collective-permute-done((bf16[96,640]{1,0:T(8,128)(2,1)S(1)}, bf16[96,640]{1,0:T(8,128)(2,1)S(1)}, u32[]{:S(2)}, u32[]{:S(2)}) %collective-permute-start.33) | collective-permute-done | bytes 122912 | tf_op jit(solution)/shard_map/ppermute | solution.py:84
  299.3 16.0 %collective-permute-done.43 = bf16[4,384,384]{2,1,0:T(8,128)(2,1)} collective-permute-done((bf16[4,384,384]{2,1,0:T(8,128)(2,1)}, bf16[4,384,384]{2,1,0:T(8,128)(2,1)}, u32[]{:S(2)}, u32[]{:S(2)}) %collective-permute-start.43) | collective-permute-done | bytes 1179680 | tf_op jit(solution)/shard_map/ppermute | solution.py:84
  321.8 22.9 %collective-permute-done.36 = bf16[4,96,1920]{2,1,0:T(8,128)(2,1)} collective-permute-done((bf16[4,96,1920]{2,1,0:T(8,128)(2,1)}, bf16[4,96,1920]{2,1,0:T(8,128)(2,1)}, u32[]{:S(2)}, u32[]{:S(2)}) %collective-permute-start.36) | collective-permute-done | bytes 1474592 | tf_op jit(solution)/shard_map/ppermute | solution.py:84
  357.9 4.5 %collective-permute-done.37 = bf16[96,1920]{1,0:T(8,128)(2,1)} collective-permute-done((bf16[96,1920]{1,0:T(8,128)(2,1)}, bf16[96,1920]{1,0:T(8,128)(2,1)}, u32[]{:S(2)}, u32[]{:S(2)}) %collective-permute-start.37) | collective-permute-done | bytes 368672 | tf_op jit(solution)/shard_map/ppermute | solution.py:84
  363.0 13.3 %collective-permute-done.38 = bf16[96,1920]{1,0:T(8,128)(2,1)} collective-permute-done((bf16[96,1920]{1,0:T(8,128)(2,1)}, bf16[96,1920]{1,0:T(8,128)(2,1)}, u32[]{:S(2)}, u32[]{:S(2)}) %collective-permute-start.38) | collective-permute-done | bytes 368672 | tf_op jit(solution)/shard_map/ppermute | solution.py:84
  382.4 4.0 %shard_map.262 = bf16[512,768]{1,0:T(8,128)(2,1)} custom-call(bf16[512,768]{1,0:T(8,128)(2,1)S(1)} %bitcast.154, bf16[512,768]{1,0:T(8,128)(2,1)S(1)} %slice_bitcast_fusion.6.one_ref, bf16[512,768]{1,0:T(8,128)(2,1)} %collective-permute-done.25.two_ref, bf16[512,768]{1,0:T(8,128)(2,1)} %collective-permute-done.27.three_ref, ...), custom_call_target="tpu_custom_call" | custom-call | tf_op jit(solution)/shard_map/pallas_call | solution.py:669
  (210 shorter events, 75.5 us)
Async XLA Ops:
  2.8 19.6 %collective-permute-start.10 = (bf16[96,1920]{1,0:T(8,128)(2,1)S(1)}, bf16[96,1920]{1,0:T(8,128)(2,1)S(1)}, u32[]{:S(2)}, u32[]{:S(2)}) collective-permute-start(bf16[96,1920]{1,0:T(8,128)(2,1)S(1)} %get-tuple-element.135), channel_id=1, source_target_pairs={{0,8},{4,12},{8,0},{12,4},{16,24},{20,28},{24,16},{28,20},{1,9},{5... | collective-permute-start | bytes 1105928 | tf_op jit(solution)/shard_map/ppermute | solution.py:84
  5.8 28.4 %collective-permute-start.11 = (bf16[96,1920]{1,0:T(8,128)(2,1)S(1)}, bf16[96,1920]{1,0:T(8,128)(2,1)}, u32[]{:S(2)}, u32[]{:S(2)}) collective-permute-start(bf16[96,1920]{1,0:T(8,128)(2,1)S(1)} %get-tuple-element.135), channel_id=1, source_target_pairs={{0,16},{4,20},{8,24},{12,28},{16,0},{20,4},{24,8},{28,12},{1,17},{... | collective-permute-start | bytes 1105928 | tf_op jit(solution)/shard_map/ppermute | solution.py:84
  8.4 27.3 %collective-permute-start.12 = (bf16[96,1920]{1,0:T(8,128)(2,1)S(1)}, bf16[96,1920]{1,0:T(8,128)(2,1)}, u32[]{:S(2)}, u32[]{:S(2)}) collective-permute-start(bf16[96,1920]{1,0:T(8,128)(2,1)S(1)} %get-tuple-element.135), channel_id=1, source_target_pairs={{0,24},{4,28},{8,16},{12,20},{16,8},{20,12},{24,0},{28,4},{1,25},{... | collective-permute-start | bytes 1105928 | tf_op jit(solution)/shard_map/ppermute | solution.py:84
  9.2 30.6 %collective-permute-start.16 = (bf16[384,384]{1,0:T(8,128)(2,1)}, bf16[384,384]{1,0:T(8,128)(2,1)}, u32[]{:S(2)}, u32[]{:S(2)}) collective-permute-start(bf16[384,384]{1,0:T(8,128)(2,1)} %constant_dynamic-slice_fusion), channel_id=1, source_target_pairs={{0,8},{4,12},{8,0},{12,4},{16,24},{20,28},{24,16},{28,20},{1,9},{5... | collective-permute-start | bytes 884744 | tf_op jit(solution)/shard_map/ppermute | solution.py:84
  10.1 51.0 %collective-permute-start.17 = (bf16[384,384]{1,0:T(8,128)(2,1)}, bf16[384,384]{1,0:T(8,128)(2,1)}, u32[]{:S(2)}, u32[]{:S(2)}) collective-permute-start(bf16[384,384]{1,0:T(8,128)(2,1)} %constant_dynamic-slice_fusion), channel_id=1, source_target_pairs={{0,16},{4,20},{8,24},{12,28},{16,0},{20,4},{24,8},{28,12},{1,17},{... | collective-permute-start | bytes 884744 | tf_op jit(solution)/shard_map/ppermute | solution.py:84
  23.1 37.9 %collective-permute-start.18 = (bf16[384,384]{1,0:T(8,128)(2,1)}, bf16[384,384]{1,0:T(8,128)(2,1)}, u32[]{:S(2)}, u32[]{:S(2)}) collective-permute-start(bf16[384,384]{1,0:T(8,128)(2,1)} %constant_dynamic-slice_fusion), channel_id=1, source_target_pairs={{0,24},{4,28},{8,16},{12,20},{16,8},{20,12},{24,0},{28,4},{1,25},{... | collective-permute-start | bytes 884744 | tf_op jit(solution)/shard_map/ppermute | solution.py:84
  34.2 41.7 %collective-permute-start.1 = (bf16[512,768]{1,0:T(8,128)(2,1)S(1)}, bf16[512,768]{1,0:T(8,128)(2,1)}, u32[]{:S(2)}, u32[]{:S(2)}) collective-permute-start(bf16[512,768]{1,0:T(8,128)(2,1)S(1)} %bitcast.151), channel_id=1, source_target_pairs={{0,2},{1,3},{2,0},{3,1},{4,6},{5,7},{6,4},{7,5},{8,10},{9,11},{10,... | collective-permute-start | bytes 2359304 | tf_op jit(solution)/shard_map/ppermute | solution.py:84
  38.3 78.5 %collective-permute-start.13 = (bf16[4,96,1920]{2,1,0:T(8,128)(2,1)}, bf16[4,96,1920]{2,1,0:T(8,128)(2,1)}, u32[]{:S(2)}, u32[]{:S(2)}) collective-permute-start(bf16[4,96,1920]{2,1,0:T(8,128)(2,1)} %pad_maximum_fusion.1.refs_8_), channel_id=1, source_target_pairs={{0,4},{4,0},{8,12},{12,8},{16,20},{20,16},{24,28},{28,24},{1,5},{5... | collective-permute-start | bytes 4423688 | tf_op jit(solution)/shard_map/ppermute | solution.py:84
  63.5 41.4 %collective-permute-start.19 = (bf16[4,384,384]{2,1,0:T(8,128)(2,1)}, bf16[4,384,384]{2,1,0:T(8,128)(2,1)}, u32[]{:S(2)}, u32[]{:S(2)}) collective-permute-start(bf16[4,384,384]{2,1,0:T(8,128)(2,1)} %pad_maximum_fusion.2.refs_12_), channel_id=1, source_target_pairs={{0,4},{4,0},{8,12},{12,8},{16,20},{20,16},{24,28},{28,24},{1,5},{5... | collective-permute-start | bytes 3538952 | tf_op jit(solution)/shard_map/ppermute | solution.py:84
  75.9 28.5 %collective-permute-start = (bf16[512,768]{1,0:T(8,128)(2,1)S(1)}, bf16[512,768]{1,0:T(8,128)(2,1)S(1)}, u32[]{:S(2)}, u32[]{:S(2)}) collective-permute-start(bf16[512,768]{1,0:T(8,128)(2,1)S(1)} %bitcast.152), channel_id=1, source_target_pairs={{0,1},{1,0},{2,3},{3,2},{4,5},{5,4},{6,7},{7,6},{8,9},{9,8},{10,11... | collective-permute-start | bytes 2359304 | tf_op jit(solution)/shard_map/ppermute | solution.py:84
  75.9 29.1 %collective-permute-start.2 = (bf16[512,768]{1,0:T(8,128)(2,1)}, bf16[512,768]{1,0:T(8,128)(2,1)S(1)}, u32[]{:S(2)}, u32[]{:S(2)}) collective-permute-start(bf16[512,768]{1,0:T(8,128)(2,1)} %collective-permute-done.1.refs_2_), channel_id=1, source_target_pairs={{0,1},{1,0},{2,3},{3,2},{4,5},{5,4},{6,7},{7,6},{8,9},{9,8},{10,11... | collective-permute-start | bytes 2359304 | tf_op jit(solution)/shard_map/ppermute | solution.py:84
  85.7 18.7 %collective-permute-start.6 = (bf16[4,96,640]{2,1,0:T(8,128)(2,1)S(1)}, bf16[4,96,640]{2,1,0:T(8,128)(2,1)S(1)}, u32[]{:S(2)}, u32[]{:S(2)}) collective-permute-start(bf16[4,96,640]{2,1,0:T(8,128)(2,1)S(1)} %pad_maximum_fusion.4.refs_4_), channel_id=1, source_target_pairs={{0,4},{4,0},{8,12},{12,8},{16,20},{20,16},{24,28},{28,24},{1,5},{5... | collective-permute-start | bytes 1474568 | tf_op jit(solution)/shard_map/ppermute | solution.py:84
  104.4 39.1 %collective-permute-start.20 = (bf16[4,384,384]{2,1,0:T(8,128)(2,1)}, bf16[4,384,384]{2,1,0:T(8,128)(2,1)S(1)}, u32[]{:S(2)}, u32[]{:S(2)}) collective-permute-start(bf16[4,384,384]{2,1,0:T(8,128)(2,1)} %pad_maximum_fusion.2.refs_12_), channel_id=1, source_target_pairs={{0,1},{1,0},{2,3},{3,2},{4,5},{5,4},{6,7},{7,6},{8,9},{9,8},{10,11... | collective-permute-start | bytes 3538952 | tf_op jit(solution)/shard_map/ppermute | solution.py:84
  104.4 46.3 %collective-permute-start.14 = (bf16[4,96,1920]{2,1,0:T(8,128)(2,1)}, bf16[4,96,1920]{2,1,0:T(8,128)(2,1)}, u32[]{:S(2)}, u32[]{:S(2)}) collective-permute-start(bf16[4,96,1920]{2,1,0:T(8,128)(2,1)} %pad_maximum_fusion.1.refs_8_), channel_id=1, source_target_pairs={{0,1},{1,0},{2,3},{3,2},{4,5},{5,4},{6,7},{7,6},{8,9},{9,8},{10,11... | collective-permute-start | bytes 4423688 | tf_op jit(solution)/shard_map/ppermute | solution.py:84
  104.9 45.8 %collective-permute-start.21 = (bf16[4,384,384]{2,1,0:T(8,128)(2,1)}, bf16[4,384,384]{2,1,0:T(8,128)(2,1)}, u32[]{:S(2)}, u32[]{:S(2)}) collective-permute-start(bf16[4,384,384]{2,1,0:T(8,128)(2,1)} %collective-permute-done.19.refs_13_), channel_id=1, source_target_pairs={{0,1},{1,0},{2,3},{3,2},{4,5},{5,4},{6,7},{7,6},{8,9},{9,8},{10,11... | collective-permute-start | bytes 3538952 | tf_op jit(solution)/shard_map/ppermute | solution.py:84
  116.8 33.9 %collective-permute-start.15 = (bf16[4,96,1920]{2,1,0:T(8,128)(2,1)}, bf16[4,96,1920]{2,1,0:T(8,128)(2,1)}, u32[]{:S(2)}, u32[]{:S(2)}) collective-permute-start(bf16[4,96,1920]{2,1,0:T(8,128)(2,1)} %collective-permute-done.13.refs_9_), channel_id=1, source_target_pairs={{0,1},{1,0},{2,3},{3,2},{4,5},{5,4},{6,7},{7,6},{8,9},{9,8},{10,11... | collective-permute-start | bytes 4423688 | tf_op jit(solution)/shard_map/ppermute | solution.py:84
  129.3 14.3 %collective-permute-start.8 = (bf16[768,128]{1,0:T(8,128)(2,1)S(1)}, bf16[768,128]{1,0:T(8,128)(2,1)S(1)}, u32[]{:S(2)}, u32[]{:S(2)}) collective-permute-start(bf16[768,128]{1,0:T(8,128)(2,1)S(1)} %get-tuple-element.131), channel_id=1, source_target_pairs={{0,2},{1,3},{2,0},{3,1},{4,6},{5,7},{6,4},{7,5},{8,10},{9,11},{10,... | collective-permute-start | bytes 589832 | tf_op jit(solution)/shard_map/ppermute | solution.py:84
  185.7 95.2 %collective-permute-start.42 = (bf16[2,4,384,384]{3,2,1,0:T(8,128)(2,1)}, bf16[2,4,384,384]{3,2,1,0:T(8,128)(2,1)}, u32[]{:S(2)}, u32[]{:S(2)}) collective-permute-start(bf16[2,4,384,384]{3,2,1,0:T(8,128)(2,1)} %get-tuple-element.64), channel_id=1, source_target_pairs={{0,1},{1,0},{2,3},{3,2},{4,5},{5,4},{6,7},{7,6},{8,9},{9,8},{10,11... | collective-permute-start | bytes 7077896 | tf_op jit(solution)/shard_map/ppermute | solution.py:84
  186.1 100.0 %collective-permute-start.35 = (bf16[2,4,96,1920]{3,2,1,0:T(8,128)(2,1)}, bf16[2,4,96,1920]{3,2,1,0:T(8,128)(2,1)}, u32[]{:S(2)}, u32[]{:S(2)}) collective-permute-start(bf16[2,4,96,1920]{3,2,1,0:T(8,128)(2,1)} %get-tuple-element.61), channel_id=1, source_target_pairs={{0,1},{1,0},{2,3},{3,2},{4,5},{5,4},{6,7},{7,6},{8,9},{9,8},{10,11... | collective-permute-start | bytes 8847368 | tf_op jit(solution)/shard_map/ppermute | solution.py:84
  249.3 47.6 %collective-permute-start.26 = (bf16[512,768]{1,0:T(8,128)(2,1)S(1)}, bf16[512,768]{1,0:T(8,128)(2,1)S(1)}, u32[]{:S(2)}, u32[]{:S(2)}) collective-permute-start(bf16[512,768]{1,0:T(8,128)(2,1)S(1)} %get-tuple-element.117), channel_id=1, source_target_pairs={{0,1},{1,0},{2,3},{3,2},{4,5},{5,4},{6,7},{7,6},{8,9},{9,8},{10,11... | collective-permute-start | bytes 2359304 | tf_op jit(solution)/shard_map/ppermute | solution.py:84
  258.7 32.7 %collective-permute-start.29 = (bf16[96,640]{1,0:T(8,128)(2,1)S(1)}, bf16[96,640]{1,0:T(8,128)(2,1)S(1)}, u32[]{:S(2)}, u32[]{:S(2)}) collective-permute-start(bf16[96,640]{1,0:T(8,128)(2,1)S(1)} %get-tuple-element.119), channel_id=1, source_target_pairs={{0,8},{4,12},{8,0},{12,4},{16,24},{20,28},{24,16},{28,20},{1,9},{5... | collective-permute-start | bytes 368648 | tf_op jit(solution)/shard_map/ppermute | solution.py:84
  286.0 29.2 %collective-permute-start.43 = (bf16[4,384,384]{2,1,0:T(8,128)(2,1)}, bf16[4,384,384]{2,1,0:T(8,128)(2,1)}, u32[]{:S(2)}, u32[]{:S(2)}) collective-permute-start(bf16[4,384,384]{2,1,0:T(8,128)(2,1)} %get-tuple-element.116), channel_id=1, source_target_pairs={{0,4},{4,0},{8,12},{12,8},{16,20},{20,16},{24,28},{28,24},{1,5},{5... | collective-permute-start | bytes 3538952 | tf_op jit(solution)/shard_map/ppermute | solution.py:84
  291.4 53.4 %collective-permute-start.36 = (bf16[4,96,1920]{2,1,0:T(8,128)(2,1)}, bf16[4,96,1920]{2,1,0:T(8,128)(2,1)}, u32[]{:S(2)}, u32[]{:S(2)}) collective-permute-start(bf16[4,96,1920]{2,1,0:T(8,128)(2,1)} %get-tuple-element.111), channel_id=1, source_target_pairs={{0,4},{4,0},{8,12},{12,8},{16,20},{20,16},{24,28},{28,24},{1,5},{5... | collective-permute-start | bytes 4423688 | tf_op jit(solution)/shard_map/ppermute | solution.py:84
  317.4 32.6 %collective-permute-start.44 = (bf16[384,384]{1,0:T(8,128)(2,1)S(1)}, bf16[384,384]{1,0:T(8,128)(2,1)S(1)}, u32[]{:S(2)}, u32[]{:S(2)}) collective-permute-start(bf16[384,384]{1,0:T(8,128)(2,1)S(1)} %get-tuple-element.112), channel_id=1, source_target_pairs={{0,8},{4,12},{8,0},{12,4},{16,24},{20,28},{24,16},{28,20},{1,9},{5... | collective-permute-start | bytes 884744 | tf_op jit(solution)/shard_map/ppermute | solution.py:84
  318.4 36.4 %collective-permute-start.45 = (bf16[384,384]{1,0:T(8,128)(2,1)}, bf16[384,384]{1,0:T(8,128)(2,1)}, u32[]{:S(2)}, u32[]{:S(2)}) collective-permute-start(bf16[384,384]{1,0:T(8,128)(2,1)} %get-tuple-element.114), channel_id=1, source_target_pairs={{0,16},{4,20},{8,24},{12,28},{16,0},{20,4},{24,8},{28,12},{1,17},{... | collective-permute-start | bytes 884744 | tf_op jit(solution)/shard_map/ppermute | solution.py:84
  320.4 34.5 %collective-permute-start.46 = (bf16[384,384]{1,0:T(8,128)(2,1)}, bf16[384,384]{1,0:T(8,128)(2,1)}, u32[]{:S(2)}, u32[]{:S(2)}) collective-permute-start(bf16[384,384]{1,0:T(8,128)(2,1)} %get-tuple-element.113), channel_id=1, source_target_pairs={{0,24},{4,28},{8,16},{12,20},{16,8},{20,12},{24,0},{28,4},{1,25},{... | collective-permute-start | bytes 884744 | tf_op jit(solution)/shard_map/ppermute | solution.py:84
  347.1 15.3 %collective-permute-start.37 = (bf16[96,1920]{1,0:T(8,128)(2,1)}, bf16[96,1920]{1,0:T(8,128)(2,1)}, u32[]{:S(2)}, u32[]{:S(2)}) collective-permute-start(bf16[96,1920]{1,0:T(8,128)(2,1)} %get-tuple-element.107), channel_id=1, source_target_pairs={{0,8},{4,12},{8,0},{12,4},{16,24},{20,28},{24,16},{28,20},{1,9},{5... | collective-permute-start | bytes 1105928 | tf_op jit(solution)/shard_map/ppermute | solution.py:84
  347.8 28.5 %collective-permute-start.38 = (bf16[96,1920]{1,0:T(8,128)(2,1)}, bf16[96,1920]{1,0:T(8,128)(2,1)}, u32[]{:S(2)}, u32[]{:S(2)}) collective-permute-start(bf16[96,1920]{1,0:T(8,128)(2,1)} %get-tuple-element.109), channel_id=1, source_target_pairs={{0,16},{4,20},{8,24},{12,28},{16,0},{20,4},{24,8},{28,12},{1,17},{... | collective-permute-start | bytes 1105928 | tf_op jit(solution)/shard_map/ppermute | solution.py:84
  350.1 26.3 %collective-permute-start.39 = (bf16[96,1920]{1,0:T(8,128)(2,1)}, bf16[96,1920]{1,0:T(8,128)(2,1)}, u32[]{:S(2)}, u32[]{:S(2)}) collective-permute-start(bf16[96,1920]{1,0:T(8,128)(2,1)} %get-tuple-element.108), channel_id=1, source_target_pairs={{0,24},{4,28},{8,16},{12,20},{16,8},{20,12},{24,0},{28,4},{1,25},{... | collective-permute-start | bytes 1105928 | tf_op jit(solution)/shard_map/ppermute | solution.py:84
  354.9 27.5 %collective-permute-start.25 = (bf16[512,768]{1,0:T(8,128)(2,1)}, bf16[512,768]{1,0:T(8,128)(2,1)}, u32[]{:S(2)}, u32[]{:S(2)}) collective-permute-start(bf16[512,768]{1,0:T(8,128)(2,1)} %get-tuple-element.118), channel_id=1, source_target_pairs={{0,1},{1,0},{2,3},{3,2},{4,5},{5,4},{6,7},{7,6},{8,9},{9,8},{10,11... | collective-permute-start | bytes 2359304 | tf_op jit(solution)/shard_map/ppermute | solution.py:84
  355.0 27.4 %collective-permute-start.27 = (bf16[512,768]{1,0:T(8,128)(2,1)}, bf16[512,768]{1,0:T(8,128)(2,1)}, u32[]{:S(2)}, u32[]{:S(2)}) collective-permute-start(bf16[512,768]{1,0:T(8,128)(2,1)} %fusion.4), channel_id=1, source_target_pairs={{0,2},{1,3},{2,0},{3,1},{4,6},{5,7},{6,4},{7,5},{8,10},{9,11},{10,... | collective-permute-start | bytes 2359304 | tf_op jit(solution)/shard_map/ppermute | solution.py:84
  362.4 24.0 %collective-permute-start.47 = (bf16[384,384]{1,0:T(8,128)(2,1)}, bf16[384,384]{1,0:T(8,128)(2,1)}, u32[]{:S(2)}, u32[]{:S(2)}) collective-permute-start(bf16[384,384]{1,0:T(8,128)(2,1)} %fusion.10), channel_id=1, source_target_pairs={{0,2},{1,3},{2,0},{3,1},{4,6},{5,7},{6,4},{7,5},{8,10},{9,11},{10,... | collective-permute-start | bytes 884744 | tf_op jit(solution)/shard_map/ppermute | solution.py:84
  (45 other events, 544.0 us)

commit v2 on v1

v2 whole, which is shorter than its diff:
```python
import functools
import math

import jax
import jax.numpy as jnp
from jax import lax
from jax.experimental import pallas as pl
from jax.experimental.pallas import tpu as pltpu
from jax.sharding import PartitionSpec as P

H = 12

epsilon = 1e-05
gelu_coeff = 0.7978845608
cubic_term = 0.044715
excluded = -1073741824.0
bf16 = jnp.bfloat16
f32 = jnp.float32
LANES = 128
GROUP = 4
VMEM_BYTES = 52 * 1024 * 1024

nt_dims = (((1,), (1,)), ((), ()))
tn_dims = (((0,), (0,)), ((), ()))


def mm(left, right):
    return jnp.dot(left, right, preferred_element_type=f32)


def mm_nt(left, right):
    return lax.dot_general(left, right, nt_dims, preferred_element_type=f32)


def mm_tn(left, right):
    return lax.dot_general(left, right, tn_dims, preferred_element_type=f32)


def whole(memory_space=pltpu.VMEM):
    return pl.BlockSpec(memory_space=memory_space)


def lanes_of(shape):
    return lax.broadcasted_iota(jnp.int32, shape, 1)


def norm_parts(values):
    center = values - jnp.mean(values, axis=-1, keepdims=True)
    spread = jnp.mean(center * center, axis=-1, keepdims=True)
    inverse = lax.rsqrt(spread + epsilon)
    return center * inverse, inverse


def norm_back(scaled, unit, inverse):
    return inverse * (
        scaled
        - jnp.mean(scaled, axis=-1, keepdims=True)
        - unit * jnp.mean(scaled * unit, axis=-1, keepdims=True)
    )


def three_parts(value):
    first = value.astype(bf16).astype(f32)
    rest = value - first
    second = rest.astype(bf16).astype(f32)
    return first, second, rest - second


def with_parts(base, value):
    lane = lanes_of(base.shape)
    one, two, three = three_parts(value)
    return jnp.where(
        lane == 64, one, jnp.where(lane == 65, two, jnp.where(lane == 66, three, base))
    )


def unpack_rows(packed, rows):
    tail = jnp.concatenate([packed[rows:, :64], packed[rows:, 64:]], axis=0)
    return packed[:rows], tail


def swap(value, axis, bit, name):
    size = lax.axis_size(axis)
    with jax.named_scope(name):
        return lax.ppermute(value, axis, [(i, i ^ bit) for i in range(size)])


def launch(kernel, gates, in_specs, cost=1.0, **options):
    count = len(gates)
    flops = int(cost * 1e9)

    def gated(*refs):
        kernel(*refs[count:])

    call = pl.pallas_call(
        gated,
        in_specs=[whole(pl.ANY)] * count + in_specs,
        compiler_params=pltpu.CompilerParams(vmem_limit_bytes=VMEM_BYTES),
        cost_estimate=pl.CostEstimate(flops=flops, bytes_accessed=1024, transcendentals=0),
        **options,
    )
    return lambda *operands: call(*gates, *operands)


def hold_kernel(value_ref, out_ref):
    pass


def after(value, *gates):
    return launch(
        hold_kernel,
        gates,
        [whole(pl.ANY)],
        out_shape=jax.ShapeDtypeStruct(value.shape, value.dtype),
        out_specs=whole(pl.ANY),
        input_output_aliases={len(gates): 0},
    )(value)


def far_pieces(piece, name):
    found = [piece]
    for k in range(1, lax.axis_size("dp") // 2):
        found.append(swap(piece, "dp", 2 * k, name + "_z"))
    return found


def add(left, right):
    return (left.astype(f32) + right.astype(f32)).astype(bf16)


def scatter_far(even, name):
    begun = None
    while even.shape[0] > 1:
        half = even.shape[0] // 2
        bit = lax.axis_size("dp") // (2 * half)
        pairs = even.reshape(half, 2, *even.shape[1:])
        even = add(pairs[:, 0], swap(pairs[:, 1], "dp", bit, name + "_z"))
        begun = even if begun is None else begun
    return begun, even[0]


def sum_groups(value):
    bit = GROUP
    while bit < lax.axis_size("ctx"):
        other = swap(value, "ctx", bit, "groups")
        value = (value.astype(f32) + other.astype(f32)).astype(bf16)
        bit *= 2
    return value


def gather_group(value, name):
    over = swap(value, "ctx", 2, name + "_x")
    side = swap(value, "ctx", 1, name + "_core")
    return [value, side, over, swap(over, "ctx", 1, name + "_pass")]


def exchange_group(values, name):
    names = ("", "_core", "_x", "_xcore")
    return [values[0]] + [swap(values[d], "ctx", d, name + names[d]) for d in range(1, GROUP)]


def position_of(order_ref, slot, rows):
    index = lax.axis_index("ctx")
    return order_ref[0, lax.bitwise_xor(index, slot)] * rows


def valid_rows(length_ref, order_ref, slot, row_count, offset, rows):
    stored = lax.broadcasted_iota(jnp.int32, (rows, LANES), 0)[:, :1]
    position = position_of(order_ref, slot, row_count) + offset + stored
    return jnp.where(position < length_ref[0], 1.0, 0.0)


def group_index():
    return lax.rem(lax.axis_index("ctx"), GROUP)


def load_pieces(sources, target, sems, first_sem=0):
    me = lax.axis_index("dp")
    copies = []
    for source, differences in sources:
        rows = source.shape[1]
        for k, difference in enumerate(differences):
            owner = lax.bitwise_xor(me, difference)
            copies.append(
                pltpu.make_async_copy(
                    source.at[k],
                    target.at[pl.ds(pl.multiple_of(owner * rows, 16), rows)],
                    sems.at[first_sem + len(copies)],
                )
            )
    for copy in copies:
        copy.start()
    return copies


def near_and_cross(near, cross):
    halves = near.shape[0]
    return [(near, [2 * k for k in range(halves)]), (cross, [2 * k + 1 for k in range(halves)])]


def store_pieces(source, even, odd, sems):
    halves, rows, _ = even.shape
    me = lax.axis_index("dp")
    copies = []
    for parity, target in ((0, even), (1, odd)):
        for k in range(halves):
            owner = lax.bitwise_xor(me, 2 * k + parity)
            copies.append(
                pltpu.make_async_copy(
                    source.at[pl.ds(pl.multiple_of(owner * rows, 16), rows)],
                    target.at[k],
                    sems.at[2 * k + parity],
                )
            )
    for copy in copies:
        copy.start()
    for copy in copies:
        copy.wait()


def pack_kernel(w_hbm, *refs):
    w_ref, sems = refs[-2:]
    count = (len(refs) - 3) // 2
    vectors, out_ref, held = refs[:count], refs[count], refs[count + 1 : -2]
    copies = [pltpu.make_async_copy(w_hbm, w_ref, sems.at[count])]
    for i in range(count):
        copies.append(pltpu.make_async_copy(vectors[i], held[i], sems.at[i]))
    for copy in copies:
        copy.start()
    for copy in copies:
        copy.wait()
    rows = w_ref.shape[0]
    width = w_ref.shape[1] // 3
    low = group_index()
    stacked = [v[...].astype(f32) for v in held]
    used = sum(v.shape[0] for v in stacked)
    stacked.append(jnp.zeros((LANES - used, rows), f32))
    small = jnp.concatenate(stacked, axis=0).T[:, :64].astype(bf16)
    for case in range(GROUP):

        @pl.when(low == case)
        def _():
            def head(kind, h):
                at = kind * width + 192 * case + 64 * h
                return w_ref[:, at : at + 64]

            out_ref[...] = jnp.concatenate(
                [
                    head(0, 0),
                    head(1, 0),
                    head(0, 1),
                    head(1, 1),
                    head(2, 0),
                    head(2, 1),
                    head(0, 2),
                    head(1, 2),
                    head(2, 2),
                    small,
                ],
                axis=1,
            )


def pack(w_qkv, vectors, gates=()):
    rows = w_qkv.shape[0]
    return launch(
        pack_kernel,
        gates,
        cost=1.0,
        out_shape=jax.ShapeDtypeStruct((rows, 640), bf16),
        in_specs=[whole(pl.ANY)] * (1 + len(vectors)),
        out_specs=whole(),
        scratch_shapes=[pltpu.VMEM(v.shape, bf16) for v in vectors]
        + [pltpu.VMEM(w_qkv.shape, bf16), pltpu.SemaphoreType.DMA((1 + len(vectors),))],
    )(w_qkv, *vectors)


def pack_ffn_kernel(out_ref, in_ref, down_ref, one_ref, two_ref):
    rows, ff = in_ref.shape
    width = out_ref.shape[1]
    half = width // 2
    low = group_index()
    per = 4 * rows
    for case in range(GROUP):

        @pl.when(low == case)
        def _():
            at = half * (case % 2)
            parts = [
                in_ref[:, per * i + rows * case : per * i + rows * (case + 1)]
                for i in range(ff // per)
            ]
            one_ref[:, :width] = jnp.concatenate(parts, axis=1)
            one_ref[:, width:] = out_ref[:, at : at + half]
            two_ref[...] = down_ref[rows * case : rows * (case + 1)]


def pack_ffn(w_out, w_in, w_down, gates=()):
    rows, width = w_out.shape
    return launch(
        pack_ffn_kernel,
        gates,
        cost=1.0,
        out_shape=(
            jax.ShapeDtypeStruct((rows, width + width // 2), bf16),
            jax.ShapeDtypeStruct((rows, width), bf16),
        ),
        in_specs=[whole()] * 3,
        out_specs=[whole()] * 2,
    )(w_out, w_in, w_down)


def qkv_kernel(length_ref, order_ref, *refs):
    tokens = refs[:GROUP]
    near, cross = refs[GROUP : GROUP + 2]
    q_ref, k_ref, v_ref, first_ref, small_ref, w_ref, sems = refs[GROUP + 2 :]
    row_count, width = tokens[0].shape
    for copy in load_pieces(near_and_cross(near, cross), w_ref, sems):
        copy.wait()
    small = w_ref[:, 512:640].astype(f32).T
    small_ref[...] = small[64:80]
    gain, shift = small[64:65], small[65:66]
    length = length_ref[0]
    lane = lanes_of((row_count, LANES))
    ones = jnp.where((lane >= 64) & (lane < 67), 1.0, 0.0)
    bias_lane = jnp.where(lane == 67, 1.0, 0.0)
    for d in range(GROUP):
        unit, _ = norm_parts(tokens[d][...].astype(f32))
        first = (unit * gain + shift).astype(bf16)
        part = pl.ds(d * row_count, row_count)
        first_ref[part] = first
        qkv = mm(first, w_ref[...]).astype(bf16).astype(f32)

        def head(place):
            block = qkv[:, place // 2 * LANES : (place // 2 + 1) * LANES]
            if place % 2:
                block = pltpu.roll(block, 64, 1)
            return jnp.where(lane < 64, block, 0.0)

        stored = lax.broadcasted_iota(jnp.int32, (row_count, LANES), 0)
        position = position_of(order_ref, d, row_count) + stored
        bias = jnp.where(position < length, 0.0, excluded) * bias_lane
        for h, (at_q, at_k, at_v) in enumerate(((0, 1, 4), (2, 3, 5), (6, 7, 8))):
            q_ref[h, part] = (head(at_q) * 0.125 + bias_lane).astype(bf16)
            k_ref[h, part] = (head(at_k) + ones + bias).astype(bf16)
            v_ref[h, part] = (head(at_v) + ones).astype(bf16)


def project(length, order, tokens, near, cross, gates=()):
    row_count, width = tokens[0].shape
    total = GROUP * row_count
    wide = near.shape[2]
    head_out = jax.ShapeDtypeStruct((3, total, LANES), bf16)
    return launch(
        qkv_kernel,
        gates,
        cost=10.0,
        out_shape=(
            head_out,
            head_out,
            head_out,
            jax.ShapeDtypeStruct((total, width), bf16),
            jax.ShapeDtypeStruct((16, width), f32),
            jax.ShapeDtypeStruct((width, wide), bf16),
        ),
        in_specs=[whole(pltpu.SMEM)] * 2 + [whole()] * GROUP + [whole(pl.ANY)] * 2,
        out_specs=[whole()] * 6,
        scratch_shapes=[pltpu.SemaphoreType.DMA((2 * near.shape[0],))],
    )(length, order, *tokens, near, cross)


def attend_kernel(block_rows, q_ref, k_ref, v_ref, packed_ref, q_out_ref):
    row_count = q_ref.shape[1]
    half = row_count // 2
    lane = lanes_of((block_rows, LANES))
    for i in range(row_count // block_rows):
        part = pl.ds(i * block_rows, block_rows)
        heads = []
        for h in range(3):
            query = q_ref[h, part]
            scores = mm_nt(query, k_ref[h])
            top = jnp.max(scores, axis=1, keepdims=True)
            weights = jnp.exp(scores - top).astype(bf16)
            result = mm(weights, v_ref[h])
            denom = result[:, 64:65]
            heads.append(jnp.where(lane < 64, result / denom, 0.0))
            log_total = top + jnp.log(denom)
            q_out_ref[h, part] = with_parts(query.astype(f32), -log_total).astype(bf16)
        packed_ref[0, part] = (heads[0] + pltpu.roll(heads[1], 64, 1)).astype(bf16)
        for r in range(0, block_rows, half):
            size = min(half, block_rows)
            row = i * block_rows + r
            side, place = row // half, row % half
            packed_ref[
                0, pl.ds(row_count + place, size), 64 * side : 64 * side + 64
            ] = heads[2][r : r + size, :64].astype(bf16)


def attend(query, keys, values, first_slot, slots, row_count, gates=()):
    total = keys.shape[1]
    block_rows = min(row_count // 2, 256)
    return launch(
        functools.partial(attend_kernel, block_rows),
        gates,
        cost=7.0 * slots,
        grid=(slots,),
        out_shape=(
            jax.ShapeDtypeStruct((slots, row_count * 3 // 2, LANES), bf16),
            jax.ShapeDtypeStruct((3, slots * row_count, LANES), bf16),
        ),
        in_specs=[
            pl.BlockSpec((3, row_count, LANES), lambda s: (0, s + first_slot, 0)),
            whole(),
            whole(),
        ],
        out_specs=(
            pl.BlockSpec((1, row_count * 3 // 2, LANES), lambda s: (s, 0, 0)),
            pl.BlockSpec((3, row_count, LANES), lambda s: (0, s, 0)),
        ),
    )(query, keys, values)


def out_kernel(token_ref, *refs):
    attn_refs, pieces = refs[:GROUP], refs[GROUP : GROUP + 2]
    small_ref, mixed_ref, second_ref, w_o, sems = refs[GROUP + 2 :]
    row_count, width = token_ref.shape
    half = width // 2
    number = pieces[0].shape[0]
    low = group_index()
    core = lax.rem(low, 2)
    differences = [2 * k for k in range(number // 2)] + [2 * k + 1 for k in range(number // 2)]
    copies = []
    for side in range(2):
        column = pl.multiple_of((core if side == 0 else 1 - core) * half, LANES)
        target = w_o.at[:, pl.ds(column, half)]
        copies += load_pieces([(pieces[side], differences)], target, sems, side * number)
    mixed = token_ref[...].astype(f32)
    for copy in copies:
        copy.wait()
    for d in range(GROUP):
        attn = jnp.concatenate(unpack_rows(attn_refs[d][...], row_count), axis=1)
        at = pl.ds(pl.multiple_of(lax.bitwise_xor(low, d) * 192, 16), 192)
        mixed = mixed + mm(attn, w_o[at, :])
    mixed_ref[...] = mixed
    unit, _ = norm_parts(mixed)
    second_ref[...] = (unit * small_ref[2:3] + small_ref[3:4]).astype(bf16)


def project_out(tokens, attn, pieces, small, gates=()):
    row_count, width = tokens.shape
    number = pieces[0].shape[0]
    return launch(
        out_kernel,
        gates,
        cost=4.5,
        out_shape=(
            jax.ShapeDtypeStruct((row_count, width), f32),
            jax.ShapeDtypeStruct((row_count, width), bf16),
            jax.ShapeDtypeStruct((width, width), bf16),
        ),
        in_specs=[whole()] * (1 + GROUP)
        + [whole(pl.ANY)] * 2
        + [whole()],
        out_specs=[whole()] * 3,
        scratch_shapes=[pltpu.SemaphoreType.DMA((2 * number,))],
    )(tokens, *attn, *pieces, small)


def ffn_kernel(slots, offset, gathers, length_ref, order_ref, small_ref, *refs):
    number = len(slots)
    seconds, cots = refs[:number], refs[number : 2 * number]
    refs = refs[2 * number :]
    count = 2 + gathers if gathers else 2
    sources, refs = refs[:count], refs[count:]
    outs = [refs[4 * i : 4 + 4 * i] for i in range(number)]
    refs = refs[4 * number :]
    rows, width = seconds[0].shape
    if gathers:
        w_i, w_d, sems = refs
        near, cross, *downs = sources
        parts = near_and_cross(*(v.at[:, :, pl.ds(0, width)] for v in (near, cross)))
        copies = load_pieces(parts, w_i, sems)
        pairs = [(pair, (2 * k, 2 * k + 1)) for k, pair in enumerate(downs)]
        copies += load_pieces(pairs, w_d, sems, 2 * gathers)
        for copy in copies:
            copy.wait()
    else:
        w_i, w_d = sources
    bias = small_ref[pl.ds(5 + group_index(), 1)]
    for i, slot in enumerate(slots):
        ds_ref, out_ref, active_ref, dhid_ref = outs[i]
        row_count = cots[i].shape[0]
        valid = valid_rows(length_ref, order_ref, slot, row_count, offset, rows)
        dlow = (cots[i][offset : offset + rows].astype(f32) * valid).astype(bf16)
        hidden = mm(seconds[i][...], w_i[...]) + bias
        squared = hidden * hidden
        bent = jnp.tanh(hidden * (gelu_coeff + gelu_coeff * cubic_term * squared))
        plus = 0.5 + 0.5 * bent
        active = (hidden * plus).astype(bf16)
        slope = plus + hidden * (plus * (1.0 - bent)) * (
            gelu_coeff + gelu_coeff * 3.0 * cubic_term * squared
        )
        active_ref[...] = active
        dhid = (mm_nt(dlow, w_d[...]) * slope).astype(bf16)
        dhid_ref[...] = dhid
        ds_ref[...] = mm_nt(dhid, w_i[...]).astype(bf16)
        out_ref[...] = mm(active, w_d[...]).astype(bf16)


def feed_forward(length, order, small, seconds, cots, weights, slots, offset, gates=()):
    rows, width = seconds[0].shape
    gathers = len(weights) - 2
    number = len(slots)
    block = jax.ShapeDtypeStruct((rows, width), bf16)
    square = jax.ShapeDtypeStruct((width, width), bf16)
    results = launch(
        functools.partial(ffn_kernel, slots, offset, gathers),
        gates,
        cost=10.0 * rows / 512,
        out_shape=[block] * (4 * number) + [square] * (2 if gathers else 0),
        in_specs=[whole(pltpu.SMEM)] * 2
        + [whole()] * (1 + 2 * number)
        + [whole(pl.ANY) if gathers else whole()] * len(weights),
        out_specs=[whole()] * (4 * number + (2 if gathers else 0)),
        scratch_shapes=[pltpu.SemaphoreType.DMA((4 * gathers,))] if gathers else [],
    )(length, order, small, *seconds, *cots, *weights)
    grouped = [results[4 * i : 4 * i + 4] for i in range(number)]
    return grouped, results[4 * number :]


def ffn_grad_kernel(blocks, length_ref, order_ref, *refs):
    number = len(blocks)
    cots = refs[:GROUP]
    refs = refs[GROUP:]
    seconds, actives, dhids = refs[:number], refs[number : 2 * number], refs[2 * number : 3 * number]
    even, odd, bias_ref, g_ref, sems = refs[3 * number :]
    row_count, width = cots[0].shape
    total = GROUP * row_count
    bias = jnp.zeros((1, width), f32)
    grad_in = jnp.zeros((width, width), f32)
    for i in range(number):
        dhid = dhids[i][...]
        bias = bias + jnp.sum(dhid.astype(f32), axis=0, keepdims=True)
        grad_in = grad_in + mm_tn(seconds[i][...], dhid)
    g_ref[:, :width] = grad_in.astype(bf16)
    bias_ref[...] = bias
    grad_down = jnp.zeros((width, width), f32)
    for i, (slot, offset) in enumerate(blocks):
        rows = actives[i].shape[0]
        valid = valid_rows(length_ref, order_ref, slot, row_count, offset, rows)
        dlow = (cots[slot][offset : offset + rows].astype(f32) * valid).astype(bf16)
        grad_down = grad_down + mm_tn(actives[i][...], dlow)
    g_ref[:, width:] = grad_down.astype(bf16)
    store_pieces(g_ref, even, odd, sems)


def ffn_grads(length, order, cots, seconds, actives, dhids, blocks, dp_size, gates=()):
    row_count, width = cots[0].shape
    halves = dp_size // 2
    piece = jax.ShapeDtypeStruct((halves, width // dp_size, 2 * width), bf16)
    number = len(blocks)
    return launch(
        functools.partial(ffn_grad_kernel, blocks),
        gates,
        cost=11.0,
        out_shape=(piece, piece, jax.ShapeDtypeStruct((1, width), f32)),
        in_specs=[whole(pltpu.SMEM)] * 2 + [whole()] * (GROUP + 3 * number),
        out_specs=[whole(pl.ANY)] * 2 + [whole()],
        scratch_shapes=[
            pltpu.VMEM((width, 2 * width), bf16),
            pltpu.SemaphoreType.DMA((dp_size,)),
        ],
    )(length, order, *cots, *seconds, *actives, *dhids)


def mixed_back_kernel(length_ref, order_ref, *refs):
    mixed_ref, cot_ref, small_ref, w_o = refs[:4]
    attn_refs = refs[4 : 4 + GROUP]
    ds_own, ds_side, ds_over_one, ds_over_two = refs[8:12]
    dmixed_ref, small_grad_ref = refs[12:14]
    dattn_refs = refs[14 : 14 + GROUP]
    block_refs = refs[18 : 18 + GROUP]
    g_o = refs[22]
    row_count, width = mixed_ref.shape
    half = row_count // 2
    low = group_index()
    unit, inverse = norm_parts(mixed_ref[...])
    over = jnp.concatenate([ds_over_one[...], ds_over_two[...]], axis=0).astype(f32)
    ds = ds_own[...].astype(f32) + ds_side[...].astype(f32) + over
    valid = valid_rows(length_ref, order_ref, 0, row_count, 0, row_count)
    dout = cot_ref[...].astype(f32) * valid
    dmixed = dout + norm_back(ds * small_ref[2:3], unit, inverse)
    dmixed_ref[...] = dmixed
    dbranch = dmixed.astype(bf16)

    def out_rows(d):
        return pl.ds(pl.multiple_of(lax.bitwise_xor(low, d) * 192, 16), 192)

    for d in range(GROUP):
        dattn = mm_nt(dbranch, w_o[out_rows(d), :])
        dattn_refs[d][:row_count] = dattn[:, :LANES].astype(bf16)
        dattn_refs[d][row_count:, :64] = dattn[:half, LANES:].astype(bf16)
        dattn_refs[d][row_count:, 64:] = dattn[half:, LANES:].astype(bf16)
    g_o[:, width:] = jnp.zeros((width, 1024 - width), bf16)
    for d in range(GROUP):
        attn = jnp.concatenate(unpack_rows(attn_refs[d][...], row_count), axis=1)
        g_o[out_rows(d), :width] = mm_tn(attn, dbranch).astype(bf16)
    for d in range(GROUP):
        column = pl.multiple_of(lax.bitwise_xor(low, d) * 256, LANES)
        block_refs[d][...] = g_o[:, pl.ds(column, 256)]
    small_grad_ref[...] = jnp.zeros_like(small_grad_ref)
    small_grad_ref[2:3] = jnp.sum(ds * unit, axis=0, keepdims=True)
    small_grad_ref[3:4] = jnp.sum(ds, axis=0, keepdims=True)
    small_grad_ref[4:5] = jnp.sum(dout, axis=0, keepdims=True)


def mixed_back(length, order, mixed, cot, small, w_o, attn, ds, gates=()):
    row_count, width = mixed.shape
    results = launch(
        mixed_back_kernel,
        gates,
        cost=7.0,
        out_shape=[
            jax.ShapeDtypeStruct((row_count, width), f32),
            jax.ShapeDtypeStruct((16, width), f32),
        ]
        + [jax.ShapeDtypeStruct((row_count * 3 // 2, LANES), bf16)] * GROUP
        + [jax.ShapeDtypeStruct((width, 256), bf16)] * GROUP,
        in_specs=[whole(pltpu.SMEM)] * 2 + [whole()] * 12,
        out_specs=[whole()] * 10,
        scratch_shapes=[pltpu.VMEM((width, 1024), bf16)],
    )(length, order, mixed, cot, small, w_o, *attn, *ds)
    return results[0], results[1], results[2:6], results[6:10]


def layer_out_kernel(length_ref, order_ref, mixed_ref, small_ref, *refs):
    own, side, over, out_ref = refs
    row_count = mixed_ref.shape[0]
    valid = valid_rows(length_ref, order_ref, 0, row_count, 0, row_count)
    total = mixed_ref[...] + own[...].astype(f32) + side[...].astype(f32) + over[...].astype(f32)
    out_ref[...] = ((total + small_ref[4:5]) * valid).astype(bf16)


def finish_out(length, order, mixed, small, parts, gates=()):
    return launch(
        layer_out_kernel,
        gates,
        cost=3.0,
        out_shape=jax.ShapeDtypeStruct(mixed.shape, bf16),
        in_specs=[whole(pltpu.SMEM)] * 2 + [whole()] * 5,
        out_specs=whole(),
    )(length, order, mixed, small, *parts)


def attend_back_kernel(mode, heads, slots, row_count, starts, *refs):
    q_ref, k_ref, v_ref = refs[:3]
    number = len(slots)
    attn_refs, dattn_refs = refs[3 : 3 + number], refs[3 + number : 3 + 2 * number]
    refs = refs[3 + 2 * number :]
    if starts:
        dk_in, dv_in, dq_in = refs[:3]
        refs = refs[3:]
    outs = refs[:-5]
    grad_ref, k_turned, dq_ref, dk_ref, dv_ref = refs[-5:]
    head, step = pl.program_id(0), pl.program_id(1)
    total = k_ref.shape[1]
    chunk = row_count
    first_slot = slots[0] if mode == "final" else 0

    @pl.when((head == 0) & (step == 0))
    def _():
        lane = lanes_of((row_count, LANES))
        for d in range(number):
            top, tail = unpack_rows(dattn_refs[d][...].astype(f32), row_count)
            top_a, tail_a = unpack_rows(attn_refs[d][...].astype(f32), row_count)
            product = top * top_a
            for i, h in enumerate(heads):
                if h == 0:
                    block = top
                    delta = jnp.sum(jnp.where(lane < 64, product, 0.0), axis=1, keepdims=True)
                elif h == 1:
                    block = pltpu.roll(top, 64, 1)
                    delta = jnp.sum(jnp.where(lane >= 64, product, 0.0), axis=1, keepdims=True)
                else:
                    block = jnp.concatenate([tail, tail], axis=1)
                    delta = jnp.sum(tail * tail_a, axis=1, keepdims=True)
                base = jnp.where(lane < 64, block, 0.0)
                grad_ref[i, pl.ds(d * row_count, row_count)] = with_parts(base, -delta).astype(bf16)

    @pl.when(step == 0)
    def _():
        k_turned[...] = k_ref[0].astype(f32).T.astype(bf16)
        if starts:
            dk_ref[...] = dk_in[0]
            dv_ref[...] = dv_in[0]
            dq_ref[: first_slot * row_count] = dq_in[0]
        else:
            dk_ref[...] = jnp.zeros_like(dk_ref)
            dv_ref[...] = jnp.zeros_like(dv_ref)

    query = q_ref[0]
    grad = grad_ref[head, pl.ds(pl.multiple_of(step * row_count, row_count), row_count)]
    turned = jnp.zeros((LANES, row_count), f32)
    for c in range(total // chunk):
        at = pl.ds(c * chunk, chunk)
        probs = jnp.exp(mm_nt(k_ref[0, at], query))
        dscores = (probs * mm_nt(v_ref[0, at], grad)).astype(bf16)
        dv_ref[at] += mm(probs.astype(bf16), grad)
        dk_ref[at] += mm(dscores, query)
        turned = turned + mm(k_turned[:, at], dscores)
    place = pl.multiple_of((first_slot + step) * row_count, row_count)
    dq_ref[pl.ds(place, row_count)] = turned.T * 0.125

    @pl.when(step == number - 1)
    def _():
        if mode != "final":
            outs[0][0] = dk_ref[...]
            outs[1][0] = dv_ref[...]
            outs[2][0] = dq_ref[...]
            return
        lane = lanes_of((row_count, LANES))
        last_at = LANES * len(heads)
        for i in range(len(heads)):

            @pl.when(head == i)
            def _():
                for d in range(GROUP):
                    at = pl.ds(d * row_count, row_count)
                    pair = jnp.where(lane < 64, dq_ref[at], pltpu.roll(dk_ref[at], 64, 1))
                    outs[d][:, i * LANES : (i + 1) * LANES] = pair.astype(bf16)
                    value = dv_ref[at]
                    if i == 0:
                        value = jnp.where(lane < 64, value, 0.0)
                        outs[d][:, last_at : last_at + LANES] = value.astype(bf16)
                    else:
                        outs[d][:, last_at + 64 : last_at + LANES] = value[:, :64].astype(bf16)


def attend_back(query, keys, values, attn, dattn, heads, slots, mode, begun, gates=()):
    row_count = attn[0].shape[0] * 2 // 3
    total = keys.shape[1]
    number = len(slots)
    kept = GROUP if mode == "final" else number
    first_head = heads[0]
    query_head = first_head if query.shape[0] == 3 else 0

    def per_head(size):
        return (
            jax.ShapeDtypeStruct((len(heads), size, LANES), f32),
            pl.BlockSpec((1, size, LANES), lambda h, s: (h, 0, 0)),
        )

    if mode == "final":
        wide = LANES * (len(heads) + 1)
        outs = [
            (
                jax.ShapeDtypeStruct((row_count, wide), bf16),
                pl.BlockSpec((row_count, wide), lambda h, s: (0, 0)),
            )
        ] * GROUP
    else:
        outs = [per_head(total), per_head(total), per_head(number * row_count)]
    begun_specs = []
    if begun:
        begun_specs = [
            pl.BlockSpec((1, v.shape[1], LANES), lambda h, s: (h, 0, 0)) for v in begun
        ]
    return launch(
        functools.partial(attend_back_kernel, mode, heads, slots, row_count, bool(begun)),
        gates,
        cost=3.8 * number * len(heads),
        grid=(len(heads), number),
        out_shape=[shape for shape, _ in outs],
        out_specs=[spec for _, spec in outs],
        in_specs=[
            pl.BlockSpec((1, row_count, LANES), lambda h, s: (h + query_head, s, 0)),
            pl.BlockSpec((1, total, LANES), lambda h, s: (h + first_head, 0, 0)),
            pl.BlockSpec((1, total, LANES), lambda h, s: (h + first_head, 0, 0)),
        ]
        + [whole()] * (2 * number)
        + begun_specs,
        scratch_shapes=[
            pltpu.VMEM((len(heads), number * row_count, LANES), bf16),
            pltpu.VMEM((LANES, total), bf16),
            pltpu.VMEM((kept * row_count, LANES), f32),
            pltpu.VMEM((total, LANES), f32),
            pltpu.VMEM((total, LANES), f32),
        ],
    )(query, keys, values, *attn, *dattn, *begun)


def first_grad_kernel(*refs):
    parts, first_ref, w_ref, block_ref = refs[:4], refs[4], refs[5], refs[6]
    even, odd, side_ref, d_ref, g_ref, sems = refs[7:]
    row_count, wide = parts[0].shape
    for d in range(GROUP):
        d_ref[d * row_count : (d + 1) * row_count] = parts[d][...]
    weights = w_ref[...].astype(f32)
    grad = mm_tn(first_ref[...], d_ref[...])
    g_ref[:, :wide] = grad.astype(bf16)
    columns = jnp.sum(d_ref[...].astype(f32), axis=0, keepdims=True)
    shift = weights[:, 577:578]
    used = weights[:, :wide]
    gain_part = jnp.sum(used * (grad - shift * columns), axis=1, keepdims=True)
    shift_part = jnp.sum(used * columns, axis=1, keepdims=True)
    lane = lanes_of(side_ref.shape)
    side_ref[...] = jnp.where(lane == 64, gain_part, jnp.where(lane == 65, shift_part, 0.0))
    g_ref[:, wide:] = block_ref[...]
    store_pieces(g_ref, even, odd, sems)


def first_grad(parts, first, weights, block, dp_size, gates=()):
    total, width = first.shape
    wide = parts[0].shape[1]
    piece = jax.ShapeDtypeStruct((dp_size // 2, width // dp_size, wide + 256), bf16)
    return launch(
        first_grad_kernel,
        gates,
        cost=5.0,
        out_shape=(piece, piece, jax.ShapeDtypeStruct((width, LANES), f32)),
        in_specs=[whole()] * 7,
        out_specs=[whole(pl.ANY)] * 2 + [whole()],
        scratch_shapes=[
            pltpu.VMEM((total, wide), bf16),
            pltpu.VMEM((width, wide + 256), bf16),
            pltpu.SemaphoreType.DMA((dp_size,)),
        ],
    )(*parts, first, weights, block)


def second_grad_kernel(*refs):
    parts = refs[:4]
    first_ref, w_ref, side_ref, small_grad_ref, bias_grad_ref = refs[4:9]
    even, odd, d_ref, g_ref, turn_ref, sems = refs[9:]
    row_count, wide = parts[0].shape
    width = first_ref.shape[1]
    for d in range(GROUP):
        d_ref[d * row_count : (d + 1) * row_count] = parts[d][...]
    weights = w_ref[...].astype(f32)
    grad = mm_tn(first_ref[...], d_ref[...])
    columns = jnp.sum(d_ref[...].astype(f32), axis=0, keepdims=True)
    gain, shift = weights[:, 576:577], weights[:, 577:578]
    used = weights[:, 640 - wide :]
    gain_part = jnp.sum(used * (grad - shift * columns), axis=1, keepdims=True)
    shift_part = jnp.sum(used * columns, axis=1, keepdims=True)
    gain_part = (gain_part + side_ref[:, 64:65]) / gain
    shift_part = shift_part + side_ref[:, 65:66]
    turn_ref[...] = jnp.zeros_like(turn_ref)
    turn_ref[64:80] = small_grad_ref[...]
    turn_ref[pl.ds(69 + group_index(), 1)] = bias_grad_ref[...]
    lane = lanes_of((width, LANES))
    last = jnp.where(lane < 64, grad[:, wide - LANES :], turn_ref[...].T)
    last = jnp.where(lane == 64, gain_part, jnp.where(lane == 65, shift_part, last))
    g_ref[:, : wide - LANES] = grad[:, : wide - LANES].astype(bf16)
    g_ref[:, wide - LANES :] = last.astype(bf16)
    store_pieces(g_ref, even, odd, sems)


def second_grad(parts, first, weights, side, small_grad, bias_grad, dp_size, gates=()):
    total, width = first.shape
    wide = parts[0].shape[1]
    piece = jax.ShapeDtypeStruct((dp_size // 2, width // dp_size, wide), bf16)
    return launch(
        second_grad_kernel,
        gates,
        cost=5.0,
        out_shape=(piece, piece),
        in_specs=[whole()] * 9,
        out_specs=[whole(pl.ANY)] * 2,
        scratch_shapes=[
            pltpu.VMEM((total, wide), bf16),
            pltpu.VMEM((width, wide), bf16),
            pltpu.VMEM((LANES, width), f32),
            pltpu.SemaphoreType.DMA((dp_size,)),
        ],
    )(*parts, first, weights, side, small_grad, bias_grad)


def part_kernel(*refs):
    ones, twos, weights = refs[:4], refs[4:8], refs[8][...]
    cut = ones[0].shape[1]
    for d in range(GROUP):
        part = mm_nt(ones[d][...], weights[:, :cut]) + mm_nt(twos[d][...], weights[:, cut:])
        refs[9 + d][...] = part.astype(bf16)


def input_parts(ones, twos, weights, gates=()):
    row_count, width = ones[0].shape[0], weights.shape[0]
    return launch(
        part_kernel,
        gates,
        cost=5.0,
        out_shape=[jax.ShapeDtypeStruct((row_count, width), bf16)] * GROUP,
        in_specs=[whole()] * 9,
        out_specs=[whole()] * GROUP,
    )(*ones, *twos, weights)


def last_kernel(token_ref, one_ref, two_ref, three_ref, dmixed_ref, small_ref, out_ref):
    unit, inverse = norm_parts(token_ref[...].astype(f32))
    df = one_ref[...].astype(f32) + two_ref[...].astype(f32) + three_ref[...].astype(f32)
    back = norm_back(df * small_ref[0:1], unit, inverse)
    out_ref[...] = (dmixed_ref[...] + back).astype(bf16)


def finish_input(tokens, parts, dmixed, small, gates=()):
    return launch(
        last_kernel,
        gates,
        cost=4.0,
        out_shape=jax.ShapeDtypeStruct(tokens.shape, bf16),
        in_specs=[whole()] * 6,
        out_specs=whole(),
    )(tokens, *parts, dmixed, small)


def place_ffn_kernel(*refs):
    shares, in_ref, down_ref = refs[:4], refs[4], refs[5]
    rows, ff = in_ref.shape
    width = down_ref.shape[1]
    low = group_index()
    for case in range(GROUP):

        @pl.when(low == case)
        def _():
            for d in range(GROUP):
                whose = case ^ d
                down_ref[rows * whose : rows * (whose + 1)] = shares[d][:, width:].astype(f32)
                part = shares[d][:, :width].astype(f32)
                for i in range(width // rows):
                    at = 4 * rows * i + rows * whose
                    in_ref[:, at : at + rows] = part[:, rows * i : rows * (i + 1)]


def place_ffn(shares, gates=()):
    rows, wide = shares[0].shape
    width = wide // 2
    return launch(
        place_ffn_kernel,
        gates,
        cost=3.0,
        out_shape=(
            jax.ShapeDtypeStruct((rows, 4 * width), f32),
            jax.ShapeDtypeStruct((4 * rows, width), f32),
        ),
        in_specs=[whole()] * 4,
        out_specs=[whole()] * 2,
    )(*shares)


def place_qkv_kernel(*refs):
    ones, twos, qkv_ref, out_ref, small_ref = refs[:4], refs[4:8], refs[8], refs[9], refs[10]
    width = out_ref.shape[1]
    low = group_index()
    vectors = twos[0][:, 128:].astype(f32)
    for d in range(1, GROUP):
        vectors = vectors + twos[d][:, 128:].astype(f32)
    small_ref[...] = vectors.T[64:80]
    for case in range(GROUP):

        @pl.when(low == case)
        def _():
            for d in range(GROUP):
                whose = case ^ d
                one, two = ones[d][...].astype(f32), twos[d][...].astype(f32)

                def put(kind, h, part):
                    at = kind * width + 192 * whose + 64 * h
                    qkv_ref[:, at : at + 64] = part

                for h in range(2):
                    put(0, h, one[:, LANES * h : LANES * h + 64])
                    put(1, h, one[:, LANES * h + 64 : LANES * h + LANES])
                    put(2, h, one[:, 2 * LANES + 64 * h : 2 * LANES + 64 * h + 64])
                for kind in range(3):
                    put(kind, 2, two[:, 64 * kind : 64 * kind + 64])
                if 256 * whose < width:
                    out_ref[:, 256 * whose : 256 * whose + 256] = one[:, 3 * LANES :]


def place_qkv(ones, twos, width, gates=()):
    rows = ones[0].shape[0]
    return launch(
        place_qkv_kernel,
        gates,
        cost=2.0,
        out_shape=(
            jax.ShapeDtypeStruct((rows, 3 * width), f32),
            jax.ShapeDtypeStruct((rows, width), f32),
            jax.ShapeDtypeStruct((16, rows), f32),
        ),
        in_specs=[whole()] * 8,
        out_specs=[whole()] * 3,
    )(*ones, *twos)


def on_device(
    tokens,
    attn_gain,
    attn_shift,
    w_qkv,
    w_out,
    ffn_gain,
    ffn_shift,
    w_in,
    b_in,
    w_down,
    b_down,
    cotangent,
    lengths,
    block_order,
):
    mine = tokens[0]
    row_count, width = mine.shape
    ctx_size = lax.axis_size("ctx")
    dp_size = lax.axis_size("dp")
    far = ctx_size // GROUP
    rows = w_qkv.shape[0]
    half = row_count // 2
    assert math.gcd(H, ctx_size) == GROUP and w_down.shape[0] == GROUP * rows
    where = (lengths, block_order)

    vectors = [attn_gain, attn_shift, ffn_gain, ffn_shift, b_down, b_in]
    vectors = [v.reshape(-1, rows) for v in vectors]
    piece = pack(w_qkv, vectors)
    far_qkv = far_pieces(piece, "qkv")
    tok_over = swap(mine, "ctx", 2, "tokens_x")
    tok_side = swap(mine, "ctx", 1, "tokens_core")
    piece_in, piece_down = pack_ffn(w_out, w_in, w_down, gates=(piece, tok_side))
    down_near = swap(piece_down, "dp", 1, "down_y")
    near_qkv = jnp.stack([after(far_qkv[0], down_near)] + far_qkv[1:])
    cross_qkv = swap(near_qkv, "dp", 1, "qkv_y")
    blocks = [mine, tok_side, tok_over, swap(tok_over, "ctx", 1, "tokens_pass")]
    far_in = far_pieces(after(piece_in, near_qkv), "in")
    cot = cotangent[0]
    cot_over = swap(after(cot, tok_over), "ctx", 2, "cot_x")

    query, keys, values, first, small, qkv_weight = project(
        *where, blocks, near_qkv, cross_qkv
    )
    near_in = jnp.stack([far_in[0]] + [after(v, query) for v in far_in[1:]])
    downs = far_pieces(after(jnp.stack([piece_down, down_near]), query), "down")
    cross_in = swap(near_in, "dp", 1, "in_y")
    cot_side = swap(after(cot, query), "ctx", 1, "cot_core")
    cot_pass = swap(after(cot_over, query), "ctx", 1, "cot_pass")
    if far > 1:
        groups = [[g * GROUP + i for g in range(far)] for i in range(GROUP)]
        keys = lax.all_gather(keys, "ctx", axis=1, tiled=True, axis_index_groups=groups)
        values = lax.all_gather(values, "ctx", axis=1, tiled=True, axis_index_groups=groups)

    def attend_slot(slot, *gates):
        return attend(query, keys, values, slot, 1, row_count, gates=gates)

    attn_two, query_two = attend_slot(2, near_in, cot_side, cot_pass)
    over_attn = swap(attn_two[0], "ctx", 2, "attn_x")
    attn_three, query_three = attend_slot(3, attn_two)
    far_attn = swap(attn_three[0], "ctx", 3, "attn_xcore")
    attn_one, query_one = attend_slot(1, attn_three)
    side_attn = swap(attn_one[0], "ctx", 1, "attn_core")
    attn_zero, query_zero = attend_slot(0, attn_one, over_attn, *downs)
    own_attn = [attn_zero[0], attn_one[0], attn_two[0], attn_three[0]]
    attn = [attn_zero[0], side_attn, over_attn, far_attn]
    near_query = jnp.concatenate([query_zero, query_one], axis=1)
    far_query = jnp.concatenate([query_two, query_three], axis=1)
    cots = [cot, cot_side, cot_over, cot_pass]
    held_in = after(cross_in, attn_one)
    out_piece = jnp.concatenate([near_in[:, :, width:], held_in[:, :, width:]])
    out_pieces = [out_piece, swap(out_piece, "ctx", 1, "out_core")]

    mixed, second, w_o = project_out(mine, attn, out_pieces, small)
    side = swap(second, "ctx", 1, "second_core")
    over = [swap(second[i * half : (i + 1) * half], "ctx", 2, "second_x") for i in range(2)]
    near_parts, weights = feed_forward(
        *where, small, [second, side], cots[:2], [near_in, held_in, *downs], (0, 1), 0
    )
    cross = [swap(after(v, near_parts[0][0]), "ctx", 1, "second_pass") for v in over]
    ds_side = swap(near_parts[1][0], "ctx", 1, "ds_core")
    far_parts, ds_overs = [], []
    previous = near_parts[0][0]
    for i in range(2):
        part = feed_forward(
            *where,
            small,
            [over[i], cross[i]],
            cots[2:],
            weights,
            (2, 3),
            i * half,
            gates=(previous,),
        )[0]
        previous = add(part[0][0], swap(part[1][0], "ctx", 1, "ds_side"))
        ds_overs.append(swap(previous, "ctx", 2, "ds_x"))
        far_parts.append(part)

    spans = ((0, 0), (1, 0), (2, 0), (3, 0), (2, half), (3, half))
    every = near_parts + far_parts[0] + far_parts[1]
    even_ff, odd_ff, bias_grad = ffn_grads(
        *where,
        cots,
        [second, side, over[0], cross[0], over[1], cross[1]],
        [part[2] for part in every],
        [part[3] for part in every],
        spans,
        dp_size,
        gates=(ds_side, previous),
    )
    dmixed, small_grad, dattn, out_blocks = mixed_back(
        *where,
        mixed,
        cot,
        small,
        w_o,
        attn,
        [near_parts[0][0], ds_side] + ds_overs,
        gates=(even_ff,),
    )
    dattn = exchange_group(dattn, "dattn")
    ffn_even = add(even_ff, swap(odd_ff, "dp", 1, "ffn_y"))
    outs_near = near_parts[0][1], near_parts[1][1]
    outs_far = [jnp.concatenate([far_parts[i][s][1] for i in range(2)]) for s in range(2)]

    def blocks_sum(*gates):
        one, three = after(out_blocks[1], *gates), after(out_blocks[3], *gates)
        own = add(out_blocks[0], swap(one, "ctx", 1, "dw_out_core"))
        across = add(out_blocks[2], swap(three, "ctx", 1, "dw_out_side"))
        return own, swap(across, "ctx", 2, "dw_out_x")

    if far > 1:
        all_query = jnp.concatenate([near_query, far_query], axis=1)
        dk, dv, dq = attend_back(
            all_query, keys, values, own_attn, dattn, (0, 1, 2), (0, 1, 2, 3), "raw", ()
        )
        dk, dv = (
            lax.psum_scatter(v, "ctx", scatter_dimension=1, tiled=True, axis_index_groups=groups)
            for v in (dk, dv)
        )
        dq, dk, dv = (v[..., :64].astype(bf16) for v in (dq, dk, dv))
        one = jnp.concatenate([dq[0], dk[0], dq[1], dk[1], dv[0], dv[1]], axis=1)
        two = jnp.concatenate([dq[2], dk[2], dv[2], jnp.zeros_like(dv[2])], axis=1)
        ones = [one[d * row_count : (d + 1) * row_count] for d in range(GROUP)]
        twos = [two[d * row_count : (d + 1) * row_count] for d in range(GROUP)]
        begun = (dq, dk, dv)
        out_block = add(*blocks_sum())
    else:
        begun = attend_back(
            near_query, keys, values, own_attn[:2], dattn[:2], (0, 1), (0, 1), "begin", ()
        )
        out_block = blocks_sum(dattn[2], begun[0])
        ones = attend_back(
            far_query,
            keys,
            values,
            own_attn[2:],
            dattn[2:],
            (0, 1),
            (2, 3),
            "final",
            begun,
            gates=(ffn_even,),
        )
        out_block = add(*out_block)
    outs_side = swap(after(outs_near[1], ones[0]), "ctx", 1, "outs_core")
    outs_back = swap(after(outs_far[1], ones[0]), "ctx", 1, "outs_side")
    outs_sum = add(outs_far[0], outs_back)
    ffn_share = scatter_far(ffn_even, "ffn")

    even, odd, part_sums = first_grad(
        ones, first, qkv_weight, out_block, dp_size, gates=(ffn_share[0], outs_sum, outs_side)
    )
    outs_over = swap(after(outs_sum, even), "ctx", 2, "outs_x")
    one_even = add(even, swap(odd, "dp", 1, "one_y"))
    if far == 1:
        all_query = jnp.concatenate([near_query[2:], far_query[2:]], axis=1)
        twos = attend_back(
            all_query,
            keys,
            values,
            own_attn,
            dattn,
            (2,),
            (0, 1, 2, 3),
            "final",
            (),
            gates=(even,),
        )
    even, odd = second_grad(
        twos,
        first,
        qkv_weight,
        part_sums,
        small_grad,
        bias_grad,
        dp_size,
        gates=(one_even, ffn_share[1], outs_over),
    )
    two_even = add(even, swap(odd, "dp", 1, "two_y"))
    one_share = scatter_far(one_even, "one")
    ffn_shares = gather_group(sum_groups(ffn_share[1]), "ffn")
    parts = input_parts(ones, twos, qkv_weight, gates=(even,))
    layer_out = finish_out(
        *where, mixed, small, [outs_near[0], outs_side, outs_over], gates=(parts[0],)
    )
    part_over = swap(add(parts[2], swap(parts[3], "ctx", 1, "df_side")), "ctx", 2, "df_x")
    part_side = swap(parts[1], "ctx", 1, "df_core")
    grad_w_in, grad_w_down = place_ffn(ffn_shares, gates=(layer_out, two_even))
    two_share = scatter_far(two_even, "two")
    one_shares = gather_group(sum_groups(one_share[1]), "one")
    two_shares = gather_group(sum_groups(two_share[1]), "two")
    input_grad = finish_input(mine, [parts[0], part_side, part_over], dmixed, small)
    grad_w_qkv, grad_w_out, vector_grads = place_qkv(one_shares, two_shares, width)
    return (
        layer_out[None],
        input_grad[None],
        vector_grads[0],
        vector_grads[1],
        grad_w_qkv,
        grad_w_out,
        vector_grads[2],
        vector_grads[3],
        grad_w_in,
        vector_grads[5:9].reshape(-1),
        grad_w_down,
        vector_grads[4],
    )


def solution(mesh):
    placed = (
        P("dp", "ctx", None),
        P("dp"),
        P("dp"),
        P("dp", None),
        P("dp", None),
        P("dp"),
        P("dp"),
        P("dp", None),
        P("dp"),
        P("dp", None),
        P("dp"),
        P("dp", "ctx", None),
        P("dp"),
        P("dp", None),
    )
    return jax.shard_map(
        on_device,
        mesh=mesh,
        in_specs=placed,
        out_specs=(
            P("dp", "ctx", None),
            P("dp", "ctx", None),
            P("dp"),
            P("dp"),
            P("dp", None),
            P("dp", None),
            P("dp"),
            P("dp"),
            P("dp", None),
            P("dp"),
            P("dp", None),
            P("dp"),
        ),
        check_vma=False,
    )
```

time: 399 us -> 352 us (0.88)
  waiting for transfers between devices: 149 us -> 83.2 us
  Pallas kernels: 121 us -> 167 us
  other arithmetic: 30.9 us -> 6.36 us
  starting transfers between devices: 73.7 us -> 58.2 us
  local copies, waits for them, and re-layouts: 18.7 us -> 29.3 us
    ppermute x49 -> x62, waiting for transfers between devices: 149 us -> 83.2 us  [swap(): return lax.ppermute(value, axis, [(i, i ^ bit) for i in range(size)])]
    pallas_call x7 -> x40, Pallas kernels: 121 us -> 167 us  [launch(): return lambda *operands: call(*gates, *operands)]
    unnamed x58 -> x149, local copies, waits for them, and re-layouts: 3.94 us -> 25.9 us
    convert_element_type x13 -> x10, other arithmetic: 20.5 us -> 4.97 us  [add(): return (left.astype(f32) + right.astype(f32)).astype(bf16)]
    ppermute x49 -> x62, starting transfers between devices: 73.7 us -> 58.2 us  [swap(): return lax.ppermute(value, axis, [(i, i ^ bit) for i in range(size)])]
    another operation x5 -> x3, other arithmetic: 5.17 us -> 0.24 us  [the longest x1 0.13 us: on_device(): near_in = jnp.stack([far_in[0]] + [after(v, query) for v in far_in[1:]])]
  transfers between devices with their start and end apart: 49 -> 62, of which waited for: 19 -> 16; matrix products, arithmetic and copies ran while one was open for 11% -> 3% of each run, Pallas kernels for 23% -> 41%
where the time goes in v2:
time: 352 us; the launch traced here: 346 us
  Pallas kernels  167 us (47%)
  waiting for transfers between devices  83.2 us (24%)
  starting transfers between devices  58.2 us (17%)
  local copies, waits for them, and re-layouts  29.3 us (8%)
  other arithmetic  6.36 us (2%)
    pallas_call x40, Pallas kernels, launch(): return lambda *operands: call(*gates, *operands)  167 us
    ppermute x62, waiting for transfers between devices, swap(): return lax.ppermute(value, axis, [(i, i ^ bit) for i in range(size)])  83.2 us
    ppermute x62, starting transfers between devices, swap(): return lax.ppermute(value, axis, [(i, i ^ bit) for i in range(size)])  58.2 us
    unnamed x149, local copies, waits for them, and re-layouts  25.9 us
  transfers between devices with their start and end apart: 62, of which 16 were waited for; matrix products, arithmetic and copies ran while one was open for 3% of the time, Pallas kernels for 41%

profile of v2, /device:TPU:0, one launch (start us, length us, event | category | flops | bytes accessed | tf_op | source)
XLA Modules:
  0.0 346.1 jit_solution(18366628835167070988)
XLA Ops:
  11.9 3.6 %collective-permute-start.6 = (bf16[96,640]{1,0:T(8,128)(2,1)S(1)}, bf16[96,640]{1,0:T(8,128)(2,1)S(1)}, u32[]{:S(2)}, u32[]{:S(2)}) collective-permute-start(bf16[96,640]{1,0:T(8,128)(2,1)S(1)} %shard_map.229.refs_0_.refs_1_), channel_id=1, source_target_pairs={{0,24},{4,28},{8,16},{12,20},{16,8},{20,12},{24,0},{28,4},{1,25},{... | collective-permute-start | bytes 368648 | tf_op jit(solution)/shard_map/qkv_z/ppermute | solution.py:85
  16.3 5.8 %collective-permute-done.1.refs_4_.refs_0_ = bf16[512,768]{1,0:T(8,128)(2,1)S(1)} collective-permute-done((bf16[512,768]{1,0:T(8,128)(2,1)}, bf16[512,768]{1,0:T(8,128)(2,1)S(1)}, u32[]{:S(2)}, u32[]{:S(2)}) %collective-permute-start.1) | collective-permute-done | bytes 786464 | tf_op jit(solution)/shard_map/tokens_x/ppermute | solution.py:85
  22.1 3.9 %collective-permute-done.5 = bf16[96,640]{1,0:T(8,128)(2,1)S(1)} collective-permute-done((bf16[96,640]{1,0:T(8,128)(2,1)S(1)}, bf16[96,640]{1,0:T(8,128)(2,1)S(1)}, u32[]{:S(2)}, u32[]{:S(2)}) %collective-permute-start.5) | collective-permute-done | bytes 122912 | tf_op jit(solution)/shard_map/qkv_z/ppermute | solution.py:85
  28.1 10.4 %collective-permute-done.7.refs_7_ = bf16[4,96,640]{2,1,0:T(8,128)(2,1)S(1)} collective-permute-done((bf16[4,96,640]{2,1,0:T(8,128)(2,1)S(1)}, bf16[4,96,640]{2,1,0:T(8,128)(2,1)S(1)}, u32[]{:S(2)}, u32[]{:S(2)}) %collective-permute-start.7) | collective-permute-done | bytes 491552 | tf_op jit(solution)/shard_map/qkv_y/ppermute | solution.py:85
  39.4 10.2 %shard_map.232 = (bf16[3,2048,128]{2,1,0:T(8,128)(2,1)}, bf16[3,2048,128]{2,1,0:T(8,128)(2,1)}, bf16[3,2048,128]{2,1,0:T(8,128)(2,1)}, bf16[2048,768]{1,0:T(8,12...) custom-call(s32[1]{0:T(128)S(6)} %copy.76.refs_0_.refs_1_.refs_2_, s32[1,4]{1,0:T(1,128)S(1)} %copy-done.27, ...), custom_call_target="tpu_custom_call" | custom-call | flops 10000000000 | bytes 1024 | tf_op jit(solution)/shard_map/pallas_call | solution.py:102
  55.6 5.8 %collective-permute-done.10.refs_1_ = bf16[96,1152]{1,0:T(8,128)(2,1)S(1)} collective-permute-done((bf16[96,1152]{1,0:T(8,128)(2,1)S(1)}, bf16[96,1152]{1,0:T(8,128)(2,1)S(1)}, u32[]{:S(2)}, u32[]{:S(2)}) %collective-permute-start.10) | collective-permute-done | bytes 221216 | tf_op jit(solution)/shard_map/in_z/ppermute | solution.py:85
  61.4 7.5 %collective-permute-start.15 = (bf16[2,96,768]{2,1,0:T(8,128)(2,1)S(1)}, bf16[2,96,768]{2,1,0:T(8,128)(2,1)S(1)}, u32[]{:S(2)}, u32[]{:S(2)}) collective-permute-start(bf16[2,96,768]{2,1,0:T(8,128)(2,1)S(1)} %shard_map.243.refs_2_.refs_9_), channel_id=1, source_target_pairs={{0,8},{4,12},{8,0},{12,4},{16,24},{20,28},{24,16},{28,20},{1,9},{5... | collective-permute-start | bytes 884744 | tf_op jit(solution)/shard_map/down_z/ppermute | solution.py:85
  76.7 6.9 %shard_map.240 = (bf16[1,768,128]{2,1,0:T(8,128)(2,1)S(1)}, bf16[3,512,128]{2,1,0:T(8,128)(2,1)S(1)}) custom-call(bf16[4,96,1152]{2,1,0:T(8,128)(2,1)} %copy-done.49, bf16[512,768]{1,0:T(8,128)(2,1)S(1)} %collective-permute-done.11.refs_1_.refs_6_.refs_5_, bf16[512,768]{1,0:T(8,128)(2,1)} %copy-done.60, ...), custom_call_target="tpu_custom_call" | custom-call | flops 7000000000 | bytes 1024 | tf_op jit(solution)/shard_map/pallas_call | solution.py:102
  83.6 7.1 %shard_map.241 = (bf16[1,768,128]{2,1,0:T(8,128)(2,1)S(1)}, bf16[3,512,128]{2,1,0:T(8,128)(2,1)S(1)}) custom-call(bf16[1,768,128]{2,1,0:T(8,128)(2,1)S(1)} %get-tuple-element.101.refs_0_, bf16[3,2048,128]{2,1,0:T(8,128)(2,1)} %get-tuple-element.98.refs_0_.refs_3_.refs_1_.refs_6_, bf16[3,2048,128]{2,1,0:T(8,128)(2,1)} %get-tuple-element.99.refs_4_.refs_2_.refs_7_.refs_1_, ...), custom_call_target="tpu_custom_call" | custom-call | flops 7000000000 | bytes 1024 | tf_op jit(solution)/shard_map/pallas_call | solution.py:102
  90.8 6.9 %shard_map.242 = (bf16[1,768,128]{2,1,0:T(8,128)(2,1)S(1)}, bf16[3,512,128]{2,1,0:T(8,128)(2,1)S(1)}) custom-call(bf16[1,768,128]{2,1,0:T(8,128)(2,1)S(1)} %get-tuple-element.102.refs_0_, bf16[3,2048,128]{2,1,0:T(8,128)(2,1)} %get-tuple-element.98.refs_0_.refs_3_.refs_1_.refs_6_, bf16[3,2048,128]{2,1,0:T(8,128)(2,1)} %get-tuple-element.99.refs_4_.refs_2_.refs_7_.refs_1_, ...), custom_call_target="tpu_custom_call" | custom-call | flops 7000000000 | bytes 1024 | tf_op jit(solution)/shard_map/pallas_call | solution.py:102
  100.1 4.3 %collective-permute-done.14.refs_1_.refs_3_.refs_9_ = bf16[768,128]{1,0:T(8,128)(2,1)S(1)} collective-permute-done((bf16[768,128]{1,0:T(8,128)(2,1)S(1)}, bf16[768,128]{1,0:T(8,128)(2,1)S(1)}, u32[]{:S(2)}, u32[]{:S(2)}) %collective-permute-start.14) | collective-permute-done | bytes 196640 | tf_op jit(solution)/shard_map/attn_x/ppermute | solution.py:85
  104.4 18.3 %shard_map.244 = (bf16[1,768,128]{2,1,0:T(8,128)(2,1)S(1)}, bf16[3,512,128]{2,1,0:T(8,128)(2,1)}) custom-call(bf16[1,768,128]{2,1,0:T(8,128)(2,1)S(1)} %get-tuple-element.103.refs_0_, bf16[768,128]{1,0:T(8,128)(2,1)S(1)} %collective-permute-done.14.refs_1_.refs_3_.refs_9_, bf16[2,96,768]{2,1,0:T(8,128)(2,1)S(1)} %shard_map.243.refs_2_.refs_9_, ...), custom_call_target="tpu_custom_call" | custom-call | flops 7000000000 | bytes 1024 | tf_op jit(solution)/shard_map/pallas_call | solution.py:102
  122.7 4.4 %shard_map.246 = (f32[512,768]{1,0:T(8,128)}, bf16[512,768]{1,0:T(8,128)(2,1)}, bf16[768,768]{1,0:T(8,128)(2,1)}) custom-call(bf16[512,768]{1,0:T(8,128)(2,1)} %bitcast.112, bf16[768,128]{1,0:T(8,128)(2,1)S(1)} %bitcast.129, bf16[768,128]{1,0:T(8,128)(2,1)S(1)} %collective-permute-done.18.refs_2_.refs_8_, ...), custom_call_target="tpu_custom_call" | custom-call | flops 4499999744 | bytes 1024 | tf_op jit(solution)/shard_map/pallas_call | solution.py:102
  130.9 9.8 %collective-permute-done.24.refs_4_.refs_10_ = bf16[256,768]{1,0:T(8,128)(2,1)S(1)} collective-permute-done((bf16[256,768]{1,0:T(8,128)(2,1)S(1)}, bf16[256,768]{1,0:T(8,128)(2,1)S(1)}, u32[]{:S(2)}, u32[]{:S(2)}) %collective-permute-start.24) | collective-permute-done | bytes 393248 | tf_op jit(solution)/shard_map/second_x/ppermute | solution.py:85
  141.7 10.1 %shard_map.247 = (bf16[512,768]{1,0:T(8,128)(2,1)S(1)}, bf16[512,768]{1,0:T(8,128)(2,1)}, bf16[512,768]{1,0:T(8,128)(2,1)}, bf16[512,768]{1,0:T(8,128)(2,1)}, bf...) custom-call(s32[1]{0:T(128)S(6)} %copy.76.refs_0_.refs_1_.refs_2_, ...), custom_call_target="tpu_custom_call" | custom-call | flops 10000000000 | bytes 1024 | tf_op jit(solution)/shard_map/pallas_call | solution.py:102
  155.2 6.1 %shard_map.249 = (bf16[256,768]{1,0:T(8,128)(2,1)S(1)}, bf16[256,768]{1,0:T(8,128)(2,1)S(1)}, bf16[256,768]{1,0:T(8,128)(2,1)S(1)}, bf16[256,768]{1,0:T(8,128)(2...) custom-call(bf16[512,768]{1,0:T(8,128)(2,1)} %copy-done.29, ...), custom_call_target="tpu_custom_call" | custom-call | flops 5000000000 | bytes 1024 | tf_op jit(solution)/shard_map/pallas_call | solution.py:102
  167.5 6.1 %shard_map.251 = (bf16[256,768]{1,0:T(8,128)(2,1)S(1)}, bf16[256,768]{1,0:T(8,128)(2,1)S(1)}, bf16[256,768]{1,0:T(8,128)(2,1)S(1)}, bf16[256,768]{1,0:T(8,128)(2...) custom-call(bf16[256,768]{1,0:T(8,128)(2,1)} %add_convert_fusion.8.r, ...), custom_call_target="tpu_custom_call" | custom-call | flops 5000000000 | bytes 1024 | tf_op jit(solution)/shard_map/pallas_call | solution.py:102
  178.2 11.0 %shard_map.252 = (bf16[4,96,1536]{2,1,0:T(8,128)(2,1)}, bf16[4,96,1536]{2,1,0:T(8,128)(2,1)}, f32[1,768]{1,0:T(1,128)S(1)}) custom-call(bf16[512,768]{1,0:T(8,128)(2,1)} %copy-done.66, bf16[256,768]{1,0:T(8,128)(2,1)S(1)} %add_convert_fusion.7.refs_1_, s32[1]{0:T(128)S(6)} %copy.76.refs_0_.refs_1_.refs_2_, s32[1,4]{1,0:T(1,128)S(1)} %copy-done.27, ...), custom_call_target="tpu_custom_call" | custom-call | flops 11000000512 | bytes 1024 | tf_op jit(solution)/shard_map/pallas_call | solution.py:102
  189.3 5.2 %collective-permute-done.33.refs_14_ = bf16[256,768]{1,0:T(8,128)(2,1)S(1)} collective-permute-done((bf16[256,768]{1,0:T(8,128)(2,1)S(1)}, bf16[256,768]{1,0:T(8,128)(2,1)S(1)}, u32[]{:S(2)}, u32[]{:S(2)}) %collective-permute-start.33) | collective-permute-done | bytes 393248 | tf_op jit(solution)/shard_map/ds_x/ppermute | solution.py:85
  195.2 6.9 %shard_map.253 = (f32[512,768]{1,0:T(8,128)}, f32[16,768]{1,0:T(8,128)S(1)}, bf16[768,128]{1,0:T(8,128)(2,1)S(1)}, bf16[768,128]{1,0:T(8,128)(2,1)S(1)}, bf16[76...) custom-call(bf16[4,96,1536]{2,1,0:T(8,128)(2,1)} %get-tuple-element., ...), custom_call_target="tpu_custom_call" | custom-call | flops 7000000000 | bytes 1024 | tf_op jit(solution)/shard_map/pallas_call | solution.py:102
  205.7 15.8 %shard_map.254 = (f32[2,2048,128]{2,1,0:T(8,128)}, f32[2,2048,128]{2,1,0:T(8,128)}, f32[2,1024,128]{2,1,0:T(8,128)}) custom-call(bf16[3,1024,128]{2,1,0:T(8,128)(2,1)S(1)} %constant_dynamic-update-slice_fusion.2.refs_0_, bf16[3,2048,128]{2,1,0:T(8,128)(2,1)} %get-tuple-element.99.refs_4_.refs_2_.refs_7_.refs_1_, ...), custom_call_target="tpu_custom_call" | custom-call | flops 15200000000 | bytes 1024 | tf_op jit(solution)/shard_map/pallas_call | solution.py:102
  225.8 4.9 %collective-permute-done.30 = bf16[4,96,1536]{2,1,0:T(8,128)(2,1)S(1)} collective-permute-done((bf16[4,96,1536]{2,1,0:T(8,128)(2,1)S(1)}, bf16[4,96,1536]{2,1,0:T(8,128)(2,1)S(1)}, u32[]{:S(2)}, u32[]{:S(2)}) %collective-permute-start.30) | collective-permute-done | bytes 1179680 | tf_op jit(solution)/shard_map/ffn_y/ppermute | solution.py:85
  232.1 15.9 %shard_map.255 = (bf16[512,384]{1,0:T(8,128)(2,1)S(1)}, bf16[512,384]{1,0:T(8,128)(2,1)S(1)}, bf16[512,384]{1,0:T(8,128)(2,1)S(1)}, bf16[512,384]{1,0:T(8,128)(2,1)}) custom-call(bf16[4,96,1536]{2,1,0:T(8,128)(2,1)} %copy-done.43, bf16[3,1024,128]{2,1,0:T(8,128)(2,1)} %copy-done.52, bf16[3,2048,128]{2,1,0:T(8,128)(2,1)} %get-tuple-element.99.refs_4_.refs_2_.refs_7_.refs_1_, ...), custom_call_target="tpu_custom_call" | custom-call | flops 15200000000 | bytes 1024 | tf_op jit(solution)/shard_map/pallas_call | solution.py:102
  255.3 5.3 %shard_map.260 = (bf16[4,96,640]{2,1,0:T(8,128)(2,1)}, bf16[4,96,640]{2,1,0:T(8,128)(2,1)}, f32[768,128]{1,0:T(8,128)S(1)}) custom-call(bf16[2,96,1536]{2,1,0:T(8,128)(2,1)} %copy-done.46, bf16[512,768]{1,0:T(8,128)(2,1)} %add_convert_fusion.2.refs_1_, bf16[512,768]{1,0:T(8,128)(2,1)} %copy-done.61, ...), custom_call_target="tpu_custom_call" | custom-call | flops 5000000000 | bytes 1024 | tf_op jit(solution)/shard_map/pallas_call | solution.py:102
  269.0 4.3 %collective-permute-done.42 = bf16[4,96,640]{2,1,0:T(8,128)(2,1)S(1)} collective-permute-done((bf16[4,96,640]{2,1,0:T(8,128)(2,1)}, bf16[4,96,640]{2,1,0:T(8,128)(2,1)S(1)}, u32[]{:S(2)}, u32[]{:S(2)}) %collective-permute-start.42) | collective-permute-done | bytes 491552 | tf_op jit(solution)/shard_map/one_y/ppermute | solution.py:85
  274.7 14.8 %shard_map.262 = (bf16[512,256]{1,0:T(8,128)(2,1)S(1)}, bf16[512,256]{1,0:T(8,128)(2,1)}, bf16[512,256]{1,0:T(8,128)(2,1)}, bf16[512,256]{1,0:T(8,128)(2,1)}) custom-call(bf16[4,96,640]{2,1,0:T(8,128)(2,1)} %get-tuple-element.156.refs_0_, bf16[1,2048,128]{2,1,0:T(8,128)(2,1)} %pad_maximum_fusion.3.refs_1_, ...), custom_call_target="tpu_custom_call" | custom-call | flops 15200000000 | bytes 1024 | tf_op jit(solution)/shard_map/pallas_call | solution.py:102
  293.8 4.6 %shard_map.263 = (bf16[4,96,256]{2,1,0:T(8,128)(2,1)S(1)}, bf16[4,96,256]{2,1,0:T(8,128)(2,1)S(1)}) custom-call(bf16[4,96,640]{2,1,0:T(8,128)(2,1)} %copy-done.48, bf16[96,1536]{1,0:T(8,128)(2,1)S(1)} %fusion.3.refs_1_.refs_2_, bf16[512,768]{1,0:T(8,128)(2,1)} %copy-done.62, bf16[512,256]{1,0:T(8,128)(2,1)S(1)} %get-tuple-element.158.refs_3_.refs_5_, ...), custom_call_target="tpu_custom_call" | custom-call | flops 5000000000 | bytes 1024 | tf_op jit(solution)/shard_map/pallas_call | solution.py:102
  300.6 4.7 %collective-permute-done.53 = bf16[4,96,256]{2,1,0:T(8,128)(2,1)S(1)} collective-permute-done((bf16[4,96,256]{2,1,0:T(8,128)(2,1)S(1)}, bf16[4,96,256]{2,1,0:T(8,128)(2,1)S(1)}, u32[]{:S(2)}, u32[]{:S(2)}) %collective-permute-start.53) | collective-permute-done | bytes 196640 | tf_op jit(solution)/shard_map/two_y/ppermute | solution.py:85
  306.4 5.1 %shard_map.264 = (bf16[512,768]{1,0:T(8,128)(2,1)}, bf16[512,768]{1,0:T(8,128)(2,1)}, bf16[512,768]{1,0:T(8,128)(2,1)}, bf16[512,768]{1,0:T(8,128)(2,1)}) custom-call(bf16[4,96,256]{2,1,0:T(8,128)(2,1)S(1)} %get-tuple-element.165.refs_0_, bf16[512,384]{1,0:T(8,128)(2,1)S(1)} %get-tuple-element.143.refs_0_.refs_3_.refs_1_, ...), custom_call_target="tpu_custom_call" | custom-call | flops 5000000000 | bytes 1024 | tf_op jit(solution)/shard_map/pallas_call | solution.py:102
  313.2 4.7 %collective-permute-done.55 = bf16[1,96,256]{2,1,0:T(8,128)(2,1)S(1)} collective-permute-done((bf16[1,96,256]{2,1,0:T(8,128)(2,1)S(1)}, bf16[1,96,256]{2,1,0:T(8,128)(2,1)S(1)}, u32[]{:S(2)}, u32[]{:S(2)}) %collective-permute-start.55) | collective-permute-done | bytes 49184 | tf_op jit(solution)/shard_map/two_z/ppermute | solution.py:85
  331.2 10.7 %collective-permute-done.47.refs_3_ = bf16[512,768]{1,0:T(8,128)(2,1)} collective-permute-done((bf16[512,768]{1,0:T(8,128)(2,1)S(1)}, bf16[512,768]{1,0:T(8,128)(2,1)}, u32[]{:S(2)}, u32[]{:S(2)}) %collective-permute-start.47) | collective-permute-done | bytes 786464 | tf_op jit(solution)/shard_map/df_x/ppermute | solution.py:85
  341.9 4.0 %shard_map.266 = bf16[512,768]{1,0:T(8,128)(2,1)} custom-call(bf16[512,768]{1,0:T(8,128)(2,1)S(1)} %bitcast.114, bf16[512,768]{1,0:T(8,128)(2,1)S(1)} %copy-done.32, bf16[512,768]{1,0:T(8,128)(2,1)} %copy-done.63, bf16[512,768]{1,0:T(8,128)(2,1)} %collective-permute-done.47.refs_3_, f32[512,768]{1,0:T(8,128)} %get-tuple-element.171.refs_4_, ...), custom_call_target="tpu_custom_call" | custom-call | flops 4000000000 | bytes 1024 | tf_op jit(solution)/shard_map/pallas_call | solution.py:102
  (319 shorter events, 98.5 us)
Async XLA Ops:
  1.2 20.9 %collective-permute-start.1 = (bf16[512,768]{1,0:T(8,128)(2,1)}, bf16[512,768]{1,0:T(8,128)(2,1)S(1)}, u32[]{:S(2)}, u32[]{:S(2)}) collective-permute-start(bf16[512,768]{1,0:T(8,128)(2,1)} %bitcast.111), channel_id=1, source_target_pairs={{0,2},{1,3},{2,0},{3,1},{4,6},{5,7},{6,4},{7,5},{8,10},{9,11},{10,... | collective-permute-start | bytes 2359304 | tf_op jit(solution)/shard_map/tokens_x/ppermute | solution.py:85
  10.3 15.7 %collective-permute-start.3 = (bf16[96,768]{1,0:T(8,128)(2,1)S(1)}, bf16[96,768]{1,0:T(8,128)(2,1)S(1)}, u32[]{:S(2)}, u32[]{:S(2)}) collective-permute-start(bf16[96,768]{1,0:T(8,128)(2,1)S(1)} %get-tuple-element.95), channel_id=1, source_target_pairs={{0,4},{4,0},{8,12},{12,8},{16,20},{20,16},{24,28},{28,24},{1,5},{5... | collective-permute-start | bytes 442376 | tf_op jit(solution)/shard_map/down_y/ppermute | solution.py:85
  22.1 16.4 %collective-permute-start.2 = (bf16[512,768]{1,0:T(8,128)(2,1)S(1)}, bf16[512,768]{1,0:T(8,128)(2,1)S(1)}, u32[]{:S(2)}, u32[]{:S(2)}) collective-permute-start(bf16[512,768]{1,0:T(8,128)(2,1)S(1)} %collective-permute-done.1.refs_4_.refs_0_), channel_id=1, source_target_pairs={{0,1},{1,0},{2,3},{3,2},{4,5},{5,4},{6,7},{7,6},{8,9},{9,8},{10,11... | collective-permute-start | bytes 2359304 | tf_op jit(solution)/shard_map/tokens_pass/ppermute | solution.py:85
  27.5 22.2 %collective-permute-start.12 = (bf16[512,768]{1,0:T(8,128)(2,1)S(1)}, bf16[512,768]{1,0:T(8,128)(2,1)S(1)}, u32[]{:S(2)}, u32[]{:S(2)}) collective-permute-start(bf16[512,768]{1,0:T(8,128)(2,1)S(1)} %shard_map.238), channel_id=1, source_target_pairs={{0,2},{1,3},{2,0},{3,1},{4,6},{5,7},{6,4},{7,5},{8,10},{9,11},{10,... | collective-permute-start | bytes 2359304 | tf_op jit(solution)/shard_map/cot_x/ppermute | solution.py:85
  49.6 24.6 %collective-permute-start.11 = (bf16[512,768]{1,0:T(8,128)(2,1)S(1)}, bf16[512,768]{1,0:T(8,128)(2,1)S(1)}, u32[]{:S(2)}, u32[]{:S(2)}) collective-permute-start(bf16[512,768]{1,0:T(8,128)(2,1)S(1)} %shard_map.237), channel_id=1, source_target_pairs={{0,1},{1,0},{2,3},{3,2},{4,5},{5,4},{6,7},{7,6},{8,9},{9,8},{10,11... | collective-permute-start | bytes 2359304 | tf_op jit(solution)/shard_map/cot_core/ppermute | solution.py:85
  50.6 25.2 %collective-permute-start.13 = (bf16[512,768]{1,0:T(8,128)(2,1)S(1)}, bf16[512,768]{1,0:T(8,128)(2,1)S(1)}, u32[]{:S(2)}, u32[]{:S(2)}) collective-permute-start(bf16[512,768]{1,0:T(8,128)(2,1)S(1)} %shard_map.239), channel_id=1, source_target_pairs={{0,1},{1,0},{2,3},{3,2},{4,5},{5,4},{6,7},{7,6},{8,9},{9,8},{10,11... | collective-permute-start | bytes 2359304 | tf_op jit(solution)/shard_map/cot_pass/ppermute | solution.py:85
  53.5 18.7 %collective-permute-start.9 = (bf16[96,1152]{1,0:T(8,128)(2,1)S(1)}, bf16[96,1152]{1,0:T(8,128)(2,1)S(1)}, u32[]{:S(2)}, u32[]{:S(2)}) collective-permute-start(bf16[96,1152]{1,0:T(8,128)(2,1)S(1)} %shard_map.233), channel_id=1, source_target_pairs={{0,16},{4,20},{8,24},{12,28},{16,0},{20,4},{24,8},{28,12},{1,17},{... | collective-permute-start | bytes 663560 | tf_op jit(solution)/shard_map/in_z/ppermute | solution.py:85
  53.5 18.7 %collective-permute-start.8 = (bf16[96,1152]{1,0:T(8,128)(2,1)S(1)}, bf16[96,1152]{1,0:T(8,128)(2,1)S(1)}, u32[]{:S(2)}, u32[]{:S(2)}) collective-permute-start(bf16[96,1152]{1,0:T(8,128)(2,1)S(1)} %shard_map.233), channel_id=1, source_target_pairs={{0,8},{4,12},{8,0},{12,4},{16,24},{20,28},{24,16},{28,20},{1,9},{5... | collective-permute-start | bytes 663560 | tf_op jit(solution)/shard_map/in_z/ppermute | solution.py:85
  61.4 38.0 %collective-permute-start.15 = (bf16[2,96,768]{2,1,0:T(8,128)(2,1)S(1)}, bf16[2,96,768]{2,1,0:T(8,128)(2,1)S(1)}, u32[]{:S(2)}, u32[]{:S(2)}) collective-permute-start(bf16[2,96,768]{2,1,0:T(8,128)(2,1)S(1)} %shard_map.243.refs_2_.refs_9_), channel_id=1, source_target_pairs={{0,8},{4,12},{8,0},{12,4},{16,24},{20,28},{24,16},{28,20},{1,9},{5... | collective-permute-start | bytes 884744 | tf_op jit(solution)/shard_map/down_z/ppermute | solution.py:85
  72.2 27.9 %collective-permute-start.16 = (bf16[2,96,768]{2,1,0:T(8,128)(2,1)S(1)}, bf16[2,96,768]{2,1,0:T(8,128)(2,1)S(1)}, u32[]{:S(2)}, u32[]{:S(2)}) collective-permute-start(bf16[2,96,768]{2,1,0:T(8,128)(2,1)S(1)} %shard_map.243.refs_2_.refs_9_), channel_id=1, source_target_pairs={{0,16},{4,20},{8,24},{12,28},{16,0},{20,4},{24,8},{28,12},{1,17},{... | collective-permute-start | bytes 884744 | tf_op jit(solution)/shard_map/down_z/ppermute | solution.py:85
  72.2 27.9 %collective-permute-start.17 = (bf16[2,96,768]{2,1,0:T(8,128)(2,1)S(1)}, bf16[2,96,768]{2,1,0:T(8,128)(2,1)S(1)}, u32[]{:S(2)}, u32[]{:S(2)}) collective-permute-start(bf16[2,96,768]{2,1,0:T(8,128)(2,1)S(1)} %shard_map.243.refs_2_.refs_9_), channel_id=1, source_target_pairs={{0,24},{4,28},{8,16},{12,20},{16,8},{20,12},{24,0},{28,4},{1,25},{... | collective-permute-start | bytes 884744 | tf_op jit(solution)/shard_map/down_z/ppermute | solution.py:85
  74.2 25.0 %collective-permute-start.20 = (bf16[4,96,1152]{2,1,0:T(8,128)(2,1)S(1)}, bf16[4,96,1152]{2,1,0:T(8,128)(2,1)S(1)}, u32[]{:S(2)}, u32[]{:S(2)}) collective-permute-start(bf16[4,96,1152]{2,1,0:T(8,128)(2,1)S(1)} %pad_maximum_fusion.refs_0_.refs_7_), channel_id=1, source_target_pairs={{0,4},{4,0},{8,12},{12,8},{16,20},{20,16},{24,28},{28,24},{1,5},{5... | collective-permute-start | bytes 2654216 | tf_op jit(solution)/shard_map/in_y/ppermute | solution.py:85
  99.2 23.4 %collective-permute-start.18 = (bf16[768,128]{1,0:T(8,128)(2,1)S(1)}, bf16[768,128]{1,0:T(8,128)(2,1)S(1)}, u32[]{:S(2)}, u32[]{:S(2)}) collective-permute-start(bf16[768,128]{1,0:T(8,128)(2,1)S(1)} %bitcast.121), channel_id=1, source_target_pairs={{0,1},{1,0},{2,3},{3,2},{4,5},{5,4},{6,7},{7,6},{8,9},{9,8},{10,11... | collective-permute-start | bytes 589832 | tf_op jit(solution)/shard_map/attn_core/ppermute | solution.py:85
  99.4 23.3 %collective-permute-start.19 = (bf16[768,128]{1,0:T(8,128)(2,1)S(1)}, bf16[768,128]{1,0:T(8,128)(2,1)S(1)}, u32[]{:S(2)}, u32[]{:S(2)}) collective-permute-start(bf16[768,128]{1,0:T(8,128)(2,1)S(1)} %bitcast.118), channel_id=1, source_target_pairs={{0,3},{1,2},{2,1},{3,0},{4,7},{5,6},{6,5},{7,4},{8,11},{9,10},{10,... | collective-permute-start | bytes 589832 | tf_op jit(solution)/shard_map/attn_xcore/ppermute | solution.py:85
  100.1 22.6 %collective-permute-start.21 = (bf16[8,96,384]{2,1,0:T(8,128)(2,1)S(1)}, bf16[8,96,384]{2,1,0:T(8,128)(2,1)S(1)}, u32[]{:S(2)}, u32[]{:S(2)}) collective-permute-start(bf16[8,96,384]{2,1,0:T(8,128)(2,1)S(1)} %pad_maximum_fusion.2.refs_5_), channel_id=1, source_target_pairs={{0,1},{1,0},{2,3},{3,2},{4,5},{5,4},{6,7},{7,6},{8,9},{9,8},{10,11... | collective-permute-start | bytes 1769480 | tf_op jit(solution)/shard_map/out_core/ppermute | solution.py:85
  127.1 13.6 %collective-permute-start.22 = (bf16[512,768]{1,0:T(8,128)(2,1)}, bf16[512,768]{1,0:T(8,128)(2,1)S(1)}, u32[]{:S(2)}, u32[]{:S(2)}) collective-permute-start(bf16[512,768]{1,0:T(8,128)(2,1)} %get-tuple-element.105.refs_3_.refs_8_), channel_id=1, source_target_pairs={{0,1},{1,0},{2,3},{3,2},{4,5},{5,4},{6,7},{7,6},{8,9},{9,8},{10,11... | collective-permute-start | bytes 2359304 | tf_op jit(solution)/shard_map/second_core/ppermute | solution.py:85
  174.9 14.4 %collective-permute-start.32 = (bf16[256,768]{1,0:T(8,128)(2,1)S(1)}, bf16[256,768]{1,0:T(8,128)(2,1)S(1)}, u32[]{:S(2)}, u32[]{:S(2)}) collective-permute-start(bf16[256,768]{1,0:T(8,128)(2,1)S(1)} %copy-done.58), channel_id=1, source_target_pairs={{0,2},{1,3},{2,0},{3,1},{4,6},{5,7},{6,4},{7,5},{8,10},{9,11},{10,... | collective-permute-start | bytes 1179656 | tf_op jit(solution)/shard_map/ds_x/ppermute | solution.py:85
  176.8 17.7 %collective-permute-start.33 = (bf16[256,768]{1,0:T(8,128)(2,1)S(1)}, bf16[256,768]{1,0:T(8,128)(2,1)S(1)}, u32[]{:S(2)}, u32[]{:S(2)}) collective-permute-start(bf16[256,768]{1,0:T(8,128)(2,1)S(1)} %add_convert_fusion.7.refs_1_), channel_id=1, source_target_pairs={{0,2},{1,3},{2,0},{3,1},{4,6},{5,7},{6,4},{7,5},{8,10},{9,11},{10,... | collective-permute-start | bytes 1179656 | tf_op jit(solution)/shard_map/ds_x/ppermute | solution.py:85
  203.4 27.3 %collective-permute-start.30 = (bf16[4,96,1536]{2,1,0:T(8,128)(2,1)S(1)}, bf16[4,96,1536]{2,1,0:T(8,128)(2,1)S(1)}, u32[]{:S(2)}, u32[]{:S(2)}) collective-permute-start(bf16[4,96,1536]{2,1,0:T(8,128)(2,1)S(1)} %copy-done.59), channel_id=1, source_target_pairs={{0,4},{4,0},{8,12},{12,8},{16,20},{20,16},{24,28},{28,24},{1,5},{5... | collective-permute-start | bytes 3538952 | tf_op jit(solution)/shard_map/ffn_y/ppermute | solution.py:85
  203.9 17.5 %collective-permute-start.34 = (bf16[768,128]{1,0:T(8,128)(2,1)S(1)}, bf16[768,128]{1,0:T(8,128)(2,1)S(1)}, u32[]{:S(2)}, u32[]{:S(2)}) collective-permute-start(bf16[768,128]{1,0:T(8,128)(2,1)S(1)} %get-tuple-element.134), channel_id=1, source_target_pairs={{0,2},{1,3},{2,0},{3,1},{4,6},{5,7},{6,4},{7,5},{8,10},{9,11},{10,... | collective-permute-start | bytes 589832 | tf_op jit(solution)/shard_map/dattn_x/ppermute | solution.py:85
  223.0 26.4 %collective-permute-start.39 = (bf16[768,256]{1,0:T(8,128)(2,1)S(1)}, bf16[768,256]{1,0:T(8,128)(2,1)S(1)}, u32[]{:S(2)}, u32[]{:S(2)}) collective-permute-start(bf16[768,256]{1,0:T(8,128)(2,1)S(1)} %shard_map.258), channel_id=1, source_target_pairs={{0,1},{1,0},{2,3},{3,2},{4,5},{5,4},{6,7},{7,6},{8,9},{9,8},{10,11... | collective-permute-start | bytes 1179656 | tf_op jit(solution)/shard_map/dw_out_core/ppermute | solution.py:85
  224.1 25.3 %collective-permute-start.41 = (bf16[768,256]{1,0:T(8,128)(2,1)S(1)}, bf16[768,256]{1,0:T(8,128)(2,1)S(1)}, u32[]{:S(2)}, u32[]{:S(2)}) collective-permute-start(bf16[768,256]{1,0:T(8,128)(2,1)S(1)} %add_convert_fusion.5), channel_id=1, source_target_pairs={{0,2},{1,3},{2,0},{3,1},{4,6},{5,7},{6,4},{7,5},{8,10},{9,11},{10,... | collective-permute-start | bytes 1179656 | tf_op jit(solution)/shard_map/dw_out_x/ppermute | solution.py:85
  231.1 20.1 %collective-permute-start.31 = (bf16[2,96,1536]{2,1,0:T(8,128)(2,1)S(1)}, bf16[2,96,1536]{2,1,0:T(8,128)(2,1)S(1)}, u32[]{:S(2)}, u32[]{:S(2)}) collective-permute-start(bf16[2,96,1536]{2,1,0:T(8,128)(2,1)S(1)} %slice_bitcast_fusion), channel_id=1, source_target_pairs={{0,8},{4,12},{8,0},{12,4},{16,24},{20,28},{24,16},{28,20},{1,9},{5... | collective-permute-start | bytes 1769480 | tf_op jit(solution)/shard_map/ffn_z/ppermute | solution.py:85
  251.4 15.7 %collective-permute-start.43 = (bf16[1,96,1536]{2,1,0:T(8,128)(2,1)S(1)}, bf16[1,96,1536]{2,1,0:T(8,128)(2,1)S(1)}, u32[]{:S(2)}, u32[]{:S(2)}) collective-permute-start(bf16[1,96,1536]{2,1,0:T(8,128)(2,1)S(1)} %slice_bitcast_fusion.2), channel_id=1, source_target_pairs={{0,16},{4,20},{8,24},{12,28},{16,0},{20,4},{24,8},{28,12},{1,17},{... | collective-permute-start | bytes 884744 | tf_op jit(solution)/shard_map/ffn_z/ppermute | solution.py:85
  262.3 27.8 %collective-permute-start.44 = (bf16[512,768]{1,0:T(8,128)(2,1)S(1)}, bf16[512,768]{1,0:T(8,128)(2,1)S(1)}, u32[]{:S(2)}, u32[]{:S(2)}) collective-permute-start(bf16[512,768]{1,0:T(8,128)(2,1)S(1)} %shard_map.261), channel_id=1, source_target_pairs={{0,2},{1,3},{2,0},{3,1},{4,6},{5,7},{6,4},{7,5},{8,10},{9,11},{10,... | collective-permute-start | bytes 2359304 | tf_op jit(solution)/shard_map/outs_x/ppermute | solution.py:85
  267.2 22.2 %collective-permute-start.60 = (bf16[96,1536]{1,0:T(8,128)(2,1)S(1)}, bf16[96,1536]{1,0:T(8,128)(2,1)S(1)}, u32[]{:S(2)}, u32[]{:S(2)}) collective-permute-start(bf16[96,1536]{1,0:T(8,128)(2,1)S(1)} %fusion.3.refs_1_.refs_2_), channel_id=1, source_target_pairs={{0,2},{1,3},{2,0},{3,1},{4,6},{5,7},{6,4},{7,5},{8,10},{9,11},{10,... | collective-permute-start | bytes 884744 | tf_op jit(solution)/shard_map/ffn_x/ppermute | solution.py:85
  273.5 16.5 %collective-permute-start.48 = (bf16[2,96,640]{2,1,0:T(8,128)(2,1)S(1)}, bf16[2,96,640]{2,1,0:T(8,128)(2,1)S(1)}, u32[]{:S(2)}, u32[]{:S(2)}) collective-permute-start(bf16[2,96,640]{2,1,0:T(8,128)(2,1)S(1)} %slice_bitcast_fusion.4), channel_id=1, source_target_pairs={{0,8},{4,12},{8,0},{12,4},{16,24},{20,28},{24,16},{28,20},{1,9},{5... | collective-permute-start | bytes 737288 | tf_op jit(solution)/shard_map/one_z/ppermute | solution.py:85
  289.5 31.6 %collective-permute-start.59 = (bf16[96,1536]{1,0:T(8,128)(2,1)S(1)}, bf16[96,1536]{1,0:T(8,128)(2,1)S(1)}, u32[]{:S(2)}, u32[]{:S(2)}) collective-permute-start(bf16[96,1536]{1,0:T(8,128)(2,1)S(1)} %fusion.3.refs_1_.refs_2_), channel_id=1, source_target_pairs={{0,1},{1,0},{2,3},{3,2},{4,5},{5,4},{6,7},{7,6},{8,9},{9,8},{10,11... | collective-permute-start | bytes 884744 | tf_op jit(solution)/shard_map/ffn_core/ppermute | solution.py:85
  289.5 31.9 %collective-permute-start.61 = (bf16[96,1536]{1,0:T(8,128)(2,1)S(1)}, bf16[96,1536]{1,0:T(8,128)(2,1)S(1)}, u32[]{:S(2)}, u32[]{:S(2)}) collective-permute-start(bf16[96,1536]{1,0:T(8,128)(2,1)S(1)} %collective-permute-done.60.refs_4_), channel_id=1, source_target_pairs={{0,1},{1,0},{2,3},{3,2},{4,5},{5,4},{6,7},{7,6},{8,9},{9,8},{10,11... | collective-permute-start | bytes 884744 | tf_op jit(solution)/shard_map/ffn_pass/ppermute | solution.py:85
  299.1 13.0 %collective-permute-start.49 = (bf16[1,96,640]{2,1,0:T(8,128)(2,1)S(1)}, bf16[1,96,640]{2,1,0:T(8,128)(2,1)S(1)}, u32[]{:S(2)}, u32[]{:S(2)}) collective-permute-start(bf16[1,96,640]{2,1,0:T(8,128)(2,1)S(1)} %slice_bitcast_fusion.6), channel_id=1, source_target_pairs={{0,16},{4,20},{8,24},{12,28},{16,0},{20,4},{24,8},{28,12},{1,17},{... | collective-permute-start | bytes 368648 | tf_op jit(solution)/shard_map/one_z/ppermute | solution.py:85
  311.5 19.8 %collective-permute-start.45 = (bf16[512,768]{1,0:T(8,128)(2,1)}, bf16[512,768]{1,0:T(8,128)(2,1)S(1)}, u32[]{:S(2)}, u32[]{:S(2)}) collective-permute-start(bf16[512,768]{1,0:T(8,128)(2,1)} %get-tuple-element.168), channel_id=1, source_target_pairs={{0,1},{1,0},{2,3},{3,2},{4,5},{5,4},{6,7},{7,6},{8,9},{9,8},{10,11... | collective-permute-start | bytes 2359304 | tf_op jit(solution)/shard_map/df_core/ppermute | solution.py:85
  321.4 20.5 %collective-permute-start.47 = (bf16[512,768]{1,0:T(8,128)(2,1)S(1)}, bf16[512,768]{1,0:T(8,128)(2,1)}, u32[]{:S(2)}, u32[]{:S(2)}) collective-permute-start(bf16[512,768]{1,0:T(8,128)(2,1)S(1)} %add_convert_fusion.1), channel_id=1, source_target_pairs={{0,2},{1,3},{2,0},{3,1},{4,6},{5,7},{6,4},{7,5},{8,10},{9,11},{10,... | collective-permute-start | bytes 2359304 | tf_op jit(solution)/shard_map/df_x/ppermute | solution.py:85
  (101 other events, 516.5 us)
